TPU v7x, 32 devices: a whole 2x2x4 slice. The times are simulated.
32 devices in a mesh: req: 4 (over y, x), tp: 8 (over z, core).
Axes of the slice: x: 2, y: 2, z: 4, core: 2. Of those that a mesh axis runs over, the one named last changes fastest.
Arguments:
- hidden_states: bfloat16 [16, 4, 1024], P('req'), may hold values from -48 to 48
- lengths: int32 [16], P('req'), may hold values from 16 to 1024, as said below
- qkv_weight: bfloat16 [2048, 1024], P('tp'), may hold values from -1 to 1
- rotated_key_cache: bfloat16 [16, 1024, 512], P('req', 'tp'), may hold values from -1000 to 1000
- earlier_value_cache: bfloat16 [16, 1024, 512], P('req', 'tp'), may hold values from -16 to 16
- out_weight: bfloat16 [1024, 1024], P('tp'), may hold values from -0.1875 to 0.1875
- expert_ids: int32 [16, 4, 8], P('req'), may hold values from 0 to 31, all different within a row
- combine_weights: int32 [16, 4, 8], P('req'), may hold values from 4096 to 65535
- gate_up_weight: bfloat16 [32, 1024, 1024], P('tp'), may hold values from -0.1875 to 0.1875
- down_weight: bfloat16 [32, 512, 1024], P('tp'), may hold values from -0.25 to 0.25
Outputs:
- layer_output: bfloat16 [16, 4, 1024], P('req')
Inputs may be any that keep to these rules, and one draw needn't show every extreme that they name: `lengths`: cache length of each request; some request has exactly 1024. `expert_ids`: each token's 8 experts are distinct.
All inputs are finite; a program needn't handle non-finite values.
Results may differ from a plain program's by a relative error of at most 0.008.
Values may be sent and summed in bfloat16 or wider, within the bound.
No kernel may reach another device: no remote copies, remote signals or barrier semaphores. Data moves between devices by JAX's collectives and lax.ppermute only.
A program may use at most 64 MiB of HBM per device.

v0:
```python
import jax
import jax.numpy as jnp
from jax import lax
from jax.sharding import PartitionSpec as P

QUERY_HEADS = 16
KEY_VALUE_HEADS = 8
HEAD_DIMENSION = 64


EPSILON = 1e-05
ROPE_BASE = 10000.0
NEGATIVE = -1e30


def merged(part, axis, combine):
    gathered = jax.tree.map(lambda a: lax.all_gather(a, axis), part)

    def take(source):
        return jax.tree.map(lambda a: lax.dynamic_index_in_dim(a, source, 0, False), gathered)

    return lax.fori_loop(
        1, lax.axis_size(axis), lambda source, state: combine(state, take(source)), take(0)
    )


def rms_rows(value_rows):
    return value_rows * lax.rsqrt(
        jnp.mean(value_rows * value_rows, axis=-1, keepdims=True) + EPSILON
    )


def apply_rotation(value_rows, position_index):
    half_width = value_rows.shape[-1] // 2
    rates = ROPE_BASE ** (-2.0 * jnp.arange(half_width, dtype=jnp.float32) / value_rows.shape[-1])
    angles = position_index[:, None, None] * rates
    cosine = jnp.cos(angles)
    sines = jnp.sin(angles)
    front_half = value_rows[..., :half_width]
    back_half = value_rows[..., half_width:]
    return jnp.concatenate(
        [front_half * cosine - back_half * sines, back_half * cosine + front_half * sines], axis=-1
    )


def join_parts(earlier, later):
    highest = jnp.maximum(earlier[0], later[0])
    scale_earlier = jnp.exp(earlier[0] - highest)
    scale_later = jnp.exp(later[0] - highest)
    weight_sum = earlier[1] * scale_earlier + later[1] * scale_later
    value_sum = earlier[2] * scale_earlier[..., None] + later[2] * scale_later[..., None]
    return (highest, weight_sum, value_sum)


def to_columns(value_rows, step_number, group_count):
    request_list, kv_heads, _, head_size = value_rows.shape
    return (
        value_rows.reshape(request_list, kv_heads, step_number, group_count, head_size)
        .transpose(0, 2, 1, 3, 4)
        .reshape(request_list * step_number, kv_heads * group_count * head_size)
    )


def expert_terms(normed, chosen, shares, gate_up_weight, down_weight, first_expert):
    ff_width = down_weight.shape[1]
    united_out = jnp.einsum(
        "nd,edf->enf", normed, gate_up_weight, preferred_element_type=jnp.float32
    )
    activation = (jax.nn.silu(united_out[..., :ff_width]) * united_out[..., ff_width:]).astype(
        jnp.bfloat16
    )
    outcome = jnp.einsum(
        "enf,efd->end", activation, down_weight, preferred_element_type=jnp.float32
    )
    owners = first_expert + jnp.arange(gate_up_weight.shape[0], dtype=jnp.int32)
    factors = jnp.sum(
        jnp.where(chosen[None, :, :] == owners[:, None, None], shares[None, :, :], 0.0), axis=-1
    )
    return jnp.sum(factors[:, :, None] * outcome, axis=0)


def per_device(
    hidden_states,
    lengths,
    qkv_weight,
    rotated_key_cache,
    earlier_value_cache,
    out_weight,
    expert_ids,
    combine_weights,
    gate_up_weight,
    down_weight,
):
    request_list, step_number, model_width = hidden_states.shape
    token_rows = request_list * step_number
    group_count = QUERY_HEADS // KEY_VALUE_HEADS
    query_total_width = QUERY_HEADS * HEAD_DIMENSION
    key_value_width = KEY_VALUE_HEADS * HEAD_DIMENSION
    score_scale = HEAD_DIMENSION ** (-0.5)
    inputs_flat = hidden_states.reshape(token_rows, model_width)
    normed = rms_rows(inputs_flat.astype(jnp.float32)).astype(jnp.bfloat16)
    projected_part = lax.dot_general(
        qkv_weight, normed, (((1,), (1,)), ((), ())), preferred_element_type=jnp.float32
    ).astype(jnp.bfloat16)
    projected_all = lax.all_gather(projected_part, "tp", axis=0, tiled=True)
    query_key_value_rows = projected_all.T
    position_index = (
        (lengths[:, None] + jnp.arange(step_number, dtype=jnp.int32)[None, :])
        .reshape(token_rows)
        .astype(jnp.float32)
    )
    query_rows = apply_rotation(
        query_key_value_rows[:, :query_total_width]
        .reshape(token_rows, QUERY_HEADS, HEAD_DIMENSION)
        .astype(jnp.float32),
        position_index,
    ).astype(jnp.bfloat16)
    fresh_keys = apply_rotation(
        query_key_value_rows[:, query_total_width : query_total_width + key_value_width]
        .reshape(token_rows, KEY_VALUE_HEADS, HEAD_DIMENSION)
        .astype(jnp.float32),
        position_index,
    ).astype(jnp.bfloat16)
    fresh_values = query_key_value_rows[:, query_total_width + key_value_width :].reshape(
        request_list, step_number, KEY_VALUE_HEADS, HEAD_DIMENSION
    )
    grouped_rows = (
        query_rows.reshape(request_list, step_number, KEY_VALUE_HEADS, group_count, HEAD_DIMENSION)
        .transpose(0, 2, 1, 3, 4)
        .reshape(request_list, KEY_VALUE_HEADS, step_number * group_count, HEAD_DIMENSION)
    )
    cache_extent = rotated_key_cache.shape[1]
    stored_keys = rotated_key_cache.reshape(
        request_list, cache_extent, KEY_VALUE_HEADS, HEAD_DIMENSION
    )
    stored_values = earlier_value_cache.reshape(
        request_list, cache_extent, KEY_VALUE_HEADS, HEAD_DIMENSION
    )
    scores = (
        jnp.einsum("bgqd,bcgd->bgqc", grouped_rows, stored_keys, preferred_element_type=jnp.float32)
        * score_scale
    )
    start_pos = lax.axis_index("tp") * cache_extent
    live_rows = (start_pos + jnp.arange(cache_extent, dtype=jnp.int32))[None, :] < lengths[:, None]
    live_mask = live_rows[:, None, None, :]
    masked = jnp.where(live_mask, scores, NEGATIVE)
    highest = jnp.max(masked, axis=-1)
    weights = jnp.where(live_mask, jnp.exp(masked - highest[..., None]), 0.0)
    weight_sum = jnp.sum(weights, axis=-1)
    value_sum = jnp.einsum(
        "bgqc,bcgd->bgqd",
        weights.astype(jnp.bfloat16),
        stored_values,
        preferred_element_type=jnp.float32,
    )
    feature_rows = out_weight.shape[0]
    column_begin = lax.axis_index("tp") * feature_rows
    top_score, total_all, sum_all = merged((highest, weight_sum, value_sum), "tp", join_parts)
    grouped_keys = fresh_keys.reshape(request_list, step_number, KEY_VALUE_HEADS, HEAD_DIMENSION)
    new_scores = (
        jnp.einsum(
            "bgqd,bsgd->bgqs", grouped_rows, grouped_keys, preferred_element_type=jnp.float32
        )
        * score_scale
    )
    query_step = jnp.arange(step_number * group_count, dtype=jnp.int32) // group_count
    causal = jnp.arange(step_number, dtype=jnp.int32)[None, :] <= query_step[:, None]
    new_masked = jnp.where(causal, new_scores, NEGATIVE)
    final_peak = jnp.maximum(top_score, jnp.max(new_masked, axis=-1))
    new_weights = jnp.where(causal, jnp.exp(new_masked - final_peak[..., None]), 0.0)
    carried = jnp.exp(top_score - final_peak)
    denominator = total_all * carried + jnp.sum(new_weights, axis=-1)
    new_part = jnp.einsum(
        "bgqs,bsgd->bgqd",
        new_weights.astype(jnp.bfloat16),
        fresh_values,
        preferred_element_type=jnp.float32,
    )
    numerator = sum_all * carried[..., None] + new_part
    attended = to_columns(numerator / denominator[..., None], step_number, group_count).astype(
        jnp.bfloat16
    )
    attended_part = lax.dynamic_slice_in_dim(attended, column_begin, feature_rows, 1)
    first_expert = lax.axis_index("tp") * gate_up_weight.shape[0]
    chosen = expert_ids.reshape(token_rows, -1)
    shares = combine_weights.reshape(token_rows, -1).astype(jnp.float32) / 65536.0
    head_terms = jnp.dot(attended_part, out_weight, preferred_element_type=jnp.float32)
    projected_rows = lax.psum(head_terms, "tp")
    residual = inputs_flat.astype(jnp.float32) + projected_rows
    normed_second = rms_rows(residual).astype(jnp.bfloat16)
    mixture = lax.psum(
        expert_terms(
            normed_second, chosen, shares, gate_up_weight, down_weight, first_expert
        ).astype(jnp.bfloat16),
        "tp",
    ).astype(jnp.float32)
    final_result = (residual + mixture).astype(jnp.bfloat16)
    return final_result.reshape(request_list, step_number, model_width)


def solution(mesh):
    in_specs = (
        P("req", None, None),
        P("req"),
        P("tp", None),
        P("req", "tp", None),
        P("req", "tp", None),
        P("tp", None),
        P("req", None, None),
        P("req", None, None),
        P("tp", None, None),
        P("tp", None, None),
    )
    out_specs = P("req", None, None)
    return jax.shard_map(
        per_device, mesh=mesh, in_specs=in_specs, out_specs=out_specs, check_vma=False
    )
```

profile of v0, /device:TPU:0, one launch (start us, length us, event | category | flops | bytes accessed | tf_op | source)
XLA Modules:
  0.0 173.6 jit_solution(5050978438124329771)
XLA Ops:
  6.5 0.0 copy-start
  6.5 0.0 copy-start.2
  6.5 0.0 copy-start.3
  6.5 0.0 copy-start.4
  6.5 0.0 all-reduce.2.cloned.1.call-start
  6.6 0.9 multiply_reduce_fusion.1
  7.5 0.8 reshape.208
  8.3 0.1 rsqrt.20
  8.4 0.0 copy-done
  8.4 0.2 fusion.8
  8.6 15.6 %all_gather.21 = bf16[2048,16]{0,1:T(8,128)(2,1)S(1)} all-gather(bf16[256,16]{0,1:T(8,128)(2,1)S(1)} %fusion.8), channel_id=1, replica_groups=mesh['req'=4,'tp'=8] {'tp'}, dimensions={0}, use_global_device_ids=true | all-gather | bytes 73728 | tf_op jit(solution)/shard_map/all_gather | solution.py:105
  24.3 0.7 add_convert_fusion.3
  25.0 0.7 broadcast_compare_fusion
  25.7 0.1 convert_element_type.95
  25.8 0.1 reshape.206
  25.9 0.1 reshape.210
  26.0 0.1 multiply_cosine_fusion
  26.1 0.1 subtract_convert_fusion.1
  26.3 0.1 reshape.209
  26.4 0.1 subtract_convert_fusion
  26.5 0.2 pad_maximum_fusion
  26.7 1.3 copy.34
  28.0 0.3 fusion.42
  28.4 14.0 %all-gather = f32[32,8,8]{2,1,0:T(8,128)S(1)} all-gather(f32[4,8,8]{2,1,0:T(8,128)S(1)} %get-tuple-element.216), channel_id=2, replica_groups=mesh['req'=4,'tp'=8] {'tp'}, dimensions={0}, use_global_device_ids=true | all-gather | bytes 9216 | tf_op jit(solution)/shard_map/all_gather | solution.py:17
  42.3 0.2 fusion.11
  42.5 14.0 %all-gather.1 = f32[32,8,8]{2,1,0:T(8,128)S(1)} all-gather(f32[4,8,8]{2,1,0:T(8,128)S(1)} %fusion.11), channel_id=3, replica_groups=mesh['req'=4,'tp'=8] {'tp'}, dimensions={0}, use_global_device_ids=true | all-gather | bytes 9216 | tf_op jit(solution)/shard_map/all_gather | solution.py:17
  56.5 1.3 copy.35
  57.8 0.4 fusion.12
  58.3 17.0 %all-gather.2 = f32[32,8,8,64]{3,2,1,0:T(8,128)S(1)} all-gather(f32[4,8,8,64]{3,2,1,0:T(8,128)S(1)} %fusion.12), channel_id=4, replica_groups=mesh['req'=4,'tp'=8] {'tp'}, dimensions={0}, use_global_device_ids=true | all-gather | bytes 589824 | tf_op jit(solution)/shard_map/all_gather | solution.py:17
  75.3 1.5 while.19
  75.4 0.2 fusion.55
  75.6 0.2 fusion.55
  75.8 0.2 fusion.55
  76.0 0.2 fusion.55
  76.2 0.2 fusion.55
  76.5 0.2 fusion.55
  76.7 0.2 fusion.55
  76.9 0.3 fusion.43
  77.1 0.1 fusion.19
  77.2 0.2 fusion.6
  77.5 0.1 convert_element_type.103
  77.7 0.0 copy-done.2
  77.7 0.8 fusion.33
  78.4 0.0 all-reduce.2.cloned.1.call-update
  78.5 0.0 copy-done.3
  78.5 0.1 copy.40
  78.6 0.0 copy-done.4
  78.6 0.1 copy.41
  78.6 0.1 select_reduce_fusion
  78.7 54.8 %all-reduce.2.cloned.1.call-done = f32[16,1024]{1,0:T(8,128)} async-done(((f32[16,1024]{1,0:T(8,128)}), f32[16,1024]{1,0:T(8,128)}) %all-reduce.2.cloned.1.call-update) | async-done | bytes 65552 | tf_op jit(solution)/shard_map/psum | solution.py:188
  133.5 0.0 copy-start.1
  133.5 1.1 multiply_reduce_fusion
  134.6 4.8 %convolution_bitcast_fusion = f32[4,16,1024]{2,1,0:T(8,128)S(1)} fusion(bf16[4,1024,1024]{2,1,0:T(8,128)(2,1)} %param.20, f32[16,1024]{1,0:T(8,128)S(1)} %get-tuple-element.205, f32[16]{0:T(128)S(1)} %add_rsqrt_fusion.1), kind=kOutput, calls=%fused_computation.8 | convolution fusion | flops 134250496 | bytes 8716352 | tf_op jit(solution)/shard_map/nd,edf->enf/dot_general | solution.py:66
  139.4 0.0 copy-done.1
  139.4 0.7 fusion.3
  140.1 26.0 %psum.15 = bf16[16,1024]{1,0:T(8,128)(2,1)S(1)} all-reduce(bf16[16,1024]{1,0:T(8,128)(2,1)S(1)} %fusion.3), channel_id=1, replica_groups=mesh['req'=4,'tp'=8] {'tp'}, use_global_device_ids=true, to_apply=%region_11.12 | all-reduce | flops 16384 | bytes 65536 | tf_op jit(solution)/shard_map/psum | solution.py:191
  166.1 0.6 reshape.207
  (27 shorter events, 0.4 us)
Async XLA Ops:
  6.5 1.9 %copy-start = (bf16[256,1024]{1,0:T(8,128)(2,1)S(1)}, bf16[256,1024]{1,0:T(8,128)(2,1)}, u32[]{:S(2)}) copy-start(bf16[256,1024]{1,0:T(8,128)(2,1)} %param.14) | copy-start | bytes 1572868
  6.5 71.1 %copy-start.2 = (bf16[128,1024]{1,0:T(8,128)(2,1)S(1)}, bf16[128,1024]{1,0:T(8,128)(2,1)}, u32[]{:S(2)}) copy-start(bf16[128,1024]{1,0:T(8,128)(2,1)} %param.17) | copy-start | bytes 786436
  6.5 71.9 %copy-start.3 = (s32[4,4,8]{2,1,0:T(4,128)S(1)}, s32[4,4,8]{2,1,0:T(4,128)}, u32[]{:S(2)}) copy-start(s32[4,4,8]{2,1,0:T(4,128)} %param.18) | copy-start | bytes 1540
  6.5 72.0 %copy-start.4 = (s32[4,4,8]{2,1,0:T(4,128)S(1)}, s32[4,4,8]{2,1,0:T(4,128)}, u32[]{:S(2)}) copy-start(s32[4,4,8]{2,1,0:T(4,128)} %param.19) | copy-start | bytes 1540
  6.5 127.0 %all-reduce.2.cloned.1.call-start = ((), (), s32[]{:S(2)}) async-start(), calls=%async_computation | async-start | bytes 131072 | tf_op jit(solution)/shard_map/psum | solution.py:188
  133.5 5.9 %copy-start.1 = (bf16[4,512,1024]{2,1,0:T(8,128)(2,1)S(1)}, bf16[4,512,1024]{2,1,0:T(8,128)(2,1)}, u32[]{:S(2)}) copy-start(bf16[4,512,1024]{2,1,0:T(8,128)(2,1)} %param.21) | copy-start | bytes 12582916
Sparse Core Ops, SparseCore 0:
  78.6 54.8 all-reduce.1
where the time goes:
time: 174 us
  blocking collectives  86.6 us (50%)
  waiting for transfers between devices  54.8 us (31%)
  between operations  13.6 us (8%)
  matrix products  7.72 us (4%)
  other arithmetic  5.75 us (3%)
  local copies, waits for them, and re-layouts  4.85 us (3%)
    psum x1, waiting for transfers between devices, per_device(): projected_rows = lax.psum(head_terms, 'tp')  54.8 us
    all_gather x3, blocking collectives, merged(): gathered = jax.tree.map(lambda a: lax.all_gather(a, axis), part)  45 us
    psum x1, blocking collectives, per_device(): lax.psum(expert_terms(normed_second, chosen, shares, gate_up_weight, down...  26 us
    all_gather x1, blocking collectives, per_device(): projected_all = lax.all_gather(projected_part, 'tp', axis=0, tiled=True)  15.6 us
    dot_general x1, matrix products, expert_terms(): jnp.einsum('nd,edf->enf', normed, gate_up_weight, preferred_element_type=...  4.79 us
  transfers between devices with their start and end apart: 1, of which 1 were waited for; matrix products, arithmetic and copies ran while one was open for 0% of the time, Pallas kernels for 0%

commit v1 on v0

--- a/solution.py
+++ b/solution.py
@@ -1,16 +1,307 @@
+import functools
+
 import jax
 import jax.numpy as jnp
 from jax import lax
+from jax.experimental import pallas as pl
+from jax.experimental.pallas import tpu as pltpu
 from jax.sharding import PartitionSpec as P
 
 QUERY_HEADS = 16
 KEY_VALUE_HEADS = 8
 HEAD_DIMENSION = 64
-
-
+GROUP = QUERY_HEADS // KEY_VALUE_HEADS
 EPSILON = 1e-05
 ROPE_BASE = 10000.0
 NEGATIVE = -1e30
+F32 = jnp.float32
+BF16 = jnp.bfloat16
+VMEM_LIMIT = 8 * 1024 * 1024
+
+
+def iota(shape, dim):
+    return lax.broadcasted_iota(jnp.int32, shape, dim)
+
+
+def merge_rows(blocks):
+    return jnp.concatenate(blocks, axis=0)
+
+
+def in_vmem(x):
+    return pltpu.with_memory_space_constraint(x, pltpu.VMEM)
+
+
+def whole(memory_space=pltpu.VMEM):
+    return pl.BlockSpec(memory_space=memory_space)
+
+
+def call(kernel, outs, operands, name, scratch=(), smem=(), hbm_out=False):
+    args = [x if i in smem else in_vmem(x) for i, x in enumerate(operands)]
+    return pl.pallas_call(
+        kernel,
+        out_shape=[
+            jax.ShapeDtypeStruct(s, d) if hbm_out else pltpu.VMEM(s, d) for s, d in outs
+        ],
+        in_specs=[whole(pltpu.SMEM if i in smem else pltpu.VMEM) for i in range(len(args))],
+        out_specs=[whole() for _ in outs],
+        scratch_shapes=list(scratch),
+        compiler_params=pltpu.CompilerParams(vmem_limit_bytes=VMEM_LIMIT),
+        name=name,
+    )(*args)
+
+
+def project_kernel(requests, steps, lengths, hidden, weight, out):
+    device = lax.axis_index("tp")
+    devices = lax.axis_size("tp")
+    x = merge_rows([hidden[b].astype(F32) for b in range(requests)])
+    normed = (x * lax.rsqrt(jnp.mean(x * x, axis=-1, keepdims=True) + EPSILON)).astype(BF16)
+    y = lax.dot_general(normed, weight[...], (((1,), (1,)), ((), ())), preferred_element_type=F32)
+    y = y.astype(BF16).astype(F32)
+    tokens, width = y.shape
+    row = iota((tokens, 128), 0)
+    lane = iota((tokens, 128), 1)
+    position = jnp.zeros((tokens, 128), jnp.int32)
+    for b in range(requests):
+        position = jnp.where(row // steps == b, lengths[b] + row - b * steps, position)
+    half = HEAD_DIMENSION // 2
+    rates = jnp.exp((lane % half).astype(F32) * (-2.0 / HEAD_DIMENSION * 9.210340371976184))
+    angles = position.astype(F32) * rates
+    turned = device < devices * 3 // 4
+    cosine = jnp.where(turned, jnp.cos(angles), 1.0)
+    sine = jnp.where(turned, jnp.sin(angles), 0.0)
+    first = lane % HEAD_DIMENSION < half
+    sine = jnp.where(first, -sine, sine)
+    parts = []
+    for k in range(width // 128):
+        v = y[:, k * 128 : (k + 1) * 128]
+        other = jnp.where(first, pltpu.roll(v, 128 - half, 1), pltpu.roll(v, half, 1))
+        parts.append(v * cosine + other * sine)
+    a, b = parts
+    low = lane < HEAD_DIMENSION
+    even = jnp.where(low, a, pltpu.roll(b, HEAD_DIMENSION, 1))
+    odd = jnp.where(low, pltpu.roll(a, HEAD_DIMENSION, 1), b)
+    rows = []
+    for r in range(requests):
+        rows += [even[r * steps : (r + 1) * steps], odd[r * steps : (r + 1) * steps]]
+    query = merge_rows(rows)
+    plain = merge_rows([a, b])
+    out[...] = jnp.where(device < devices // 2, query, plain).astype(BF16)
+
+
+def fold(x, rows, lanes):
+    groups = lanes // HEAD_DIMENSION
+    lane = iota((rows, lanes), 1) // HEAD_DIMENSION
+    total = jnp.broadcast_to(x[0:rows], (rows, lanes))
+    for g in range(1, groups):
+        total = jnp.where(lane == g, jnp.broadcast_to(x[g * rows : (g + 1) * rows], (rows, lanes)), total)
+    return total
+
+
+def spread(x, groups):
+    rows, lanes = x.shape
+    lane = iota((rows, lanes), 1) // HEAD_DIMENSION
+    return merge_rows([jnp.where(lane == g, x, 0.0) for g in range(groups)]).astype(BF16)
+
+
+def pack_stats(peak, total):
+    lane = iota(peak.shape, 1)
+    return jnp.where(lane % HEAD_DIMENSION < HEAD_DIMENSION // 2, peak, total)
+
+
+def unpack_stats(stats):
+    half = HEAD_DIMENSION // 2
+    low = iota(stats.shape, 1) % HEAD_DIMENSION < half
+    return (
+        jnp.where(low, stats, pltpu.roll(stats, half, 1)),
+        jnp.where(low, pltpu.roll(stats, stats.shape[1] - half, 1), stats),
+    )
+
+
+def soft(scores, live, values):
+    masked = jnp.where(live, scores, NEGATIVE)
+    peak = jnp.max(masked, axis=-1, keepdims=True)
+    weights = jnp.where(live, jnp.exp(masked - peak), 0.0)
+    total = jnp.sum(weights, axis=-1, keepdims=True)
+    return peak, total, jnp.dot(weights.astype(BF16), values, preferred_element_type=F32)
+
+
+def attend_kernel(
+    requests, steps, lengths, own, sibling, keys, values, out0, out1, out2, out3, fresh, heads, blocks
+):
+    device = lax.axis_index("tp")
+    chip, core = device // 2, device % 2
+    chips = own.shape[0]
+    for k in range(chips):
+        heads[2 * (chip ^ k) + core] = own[k]
+        heads[2 * (chip ^ k) + 1 - core] = sibling[k]
+    rows = steps * GROUP
+    count = keys.shape[1]
+    scale = HEAD_DIMENSION**-0.5
+    query = jnp.concatenate([heads[t].astype(F32) for t in range(chips)], axis=1) * scale
+    lanes = query.shape[1]
+    groups = lanes // HEAD_DIMENSION
+    position = device * count + iota((groups * rows, count), 1)
+    for r in range(requests):
+        q = spread(query[r * rows : (r + 1) * rows], groups)
+        scores = lax.dot_general(q, keys[r], (((1,), (1,)), ((), ())), preferred_element_type=F32)
+        peak, total, summed = soft(scores, position < lengths[r], values[r])
+        summed = fold(summed, rows, lanes)
+        stats = pack_stats(fold(peak, rows, lanes), fold(total, rows, lanes))
+        for k in range(chips):
+            blocks[k, r * rows : (r + 1) * rows, :] = summed[:, k * 128 : (k + 1) * 128]
+            blocks[k, (requests + r) * rows : (requests + r + 1) * rows, :] = stats[:, k * 128 : (k + 1) * 128]
+    for k, out in enumerate((out0, out1, out2, out3)):
+        out[...] = blocks[chip ^ k]
+    tokens = requests * steps
+    place = chips + chip // 2
+    second = chip % 2 == 1
+    pick = lambda x: jnp.where(second, x[tokens:].astype(F32), x[:tokens].astype(F32)).astype(BF16)
+    new_keys = pick(heads[place])
+    new_values = pick(heads[place + chips // 2])
+    q = spread(heads[chip].astype(F32) * scale, 2)
+    scores = lax.dot_general(q, new_keys, (((1,), (1,)), ((), ())), preferred_element_type=F32)
+    shape = scores.shape
+    row, column = iota(shape, 0) % (requests * rows), iota(shape, 1)
+    live = (row // rows == column // steps) & (column % steps <= row % steps)
+    peak, total, summed = soft(scores, live, new_values)
+    n = requests * rows
+    fresh[0:n] = fold(summed, n, 128)
+    fresh[n : 2 * n] = pack_stats(fold(peak, n, 128), fold(total, n, 128))
+
+
+def join(a, b):
+    peak = jnp.maximum(a[0], b[0])
+    left, right = jnp.exp(a[0] - peak), jnp.exp(b[0] - peak)
+    return peak, a[1] * left + b[1] * right, a[2] * left + b[2] * right
+
+
+def read_part(ref):
+    n = ref.shape[0] // 2
+    return (*unpack_stats(ref[n:]), ref[0:n])
+
+
+def join_kernel(a, b, c, d, out):
+    peak, total, summed = join(join(read_part(a), read_part(b)), join(read_part(c), read_part(d)))
+    n = summed.shape[0]
+    out[0:n] = summed
+    out[n:] = pack_stats(peak, total)
+
+
+def output_kernel(requests, steps, own, sibling, fresh, weight, sibling_weight, out):
+    core = lax.axis_index("tp") % 2
+    _, total, summed = join(join(read_part(own), read_part(sibling)), read_part(fresh))
+    attended = summed / total
+    rows = steps * GROUP
+    heads = []
+    for j in range(GROUP):
+        heads.append(merge_rows([attended[r * rows + j * steps : r * rows + (j + 1) * steps] for r in range(requests)]))
+    low = iota(heads[0].shape, 1) < HEAD_DIMENSION
+    zero = jnp.where(low, heads[0], pltpu.roll(heads[1], HEAD_DIMENSION, 1))
+    one = jnp.where(low, pltpu.roll(heads[0], HEAD_DIMENSION, 1), heads[1])
+    mine = jnp.where(core == 0, zero, one).astype(BF16)
+    theirs = jnp.where(core == 0, one, zero).astype(BF16)
+    out[...] = jnp.dot(mine, weight[...], preferred_element_type=F32) + jnp.dot(
+        theirs, sibling_weight[...], preferred_element_type=F32
+    )
+
+
+def expert_kernel(requests, hidden, a, b, c, d, ids, shares, gate_up, down, out, residual_out):
+    device = lax.axis_index("tp")
+    x = merge_rows([hidden[r].astype(F32) for r in range(requests)])
+    residual = x + ((a[...] + b[...]) + (c[...] + d[...]))
+    residual_out[...] = residual
+    normed = (
+        residual * lax.rsqrt(jnp.mean(residual * residual, axis=-1, keepdims=True) + EPSILON)
+    ).astype(BF16)
+    chosen = merge_rows([ids[r] for r in range(requests)])
+    share = merge_rows([shares[r].astype(F32) for r in range(requests)]) * (1.0 / 65536.0)
+    experts, _, width = gate_up.shape
+    total = None
+    for e in range(experts):
+        united = jnp.dot(normed, gate_up[e], preferred_element_type=F32)
+        gate, up = united[:, : width // 2], united[:, width // 2 :]
+        active = (gate / (1.0 + jnp.exp(-gate)) * up).astype(BF16)
+        outcome = jnp.dot(active, down[e], preferred_element_type=F32)
+        factor = jnp.sum(jnp.where(chosen == device * experts + e, share, 0.0), axis=-1, keepdims=True)
+        total = factor * outcome if total is None else total + factor * outcome
+    out[...] = total.astype(BF16)
+
+
+def final_kernel(requests, steps, residual, a, b, c, d, out):
+    mixture = (a[...].astype(F32) + b[...].astype(F32)) + (c[...].astype(F32) + d[...].astype(F32))
+    result = residual[...] + mixture
+    for r in range(requests):
+        out[r] = result[r * steps : (r + 1) * steps].astype(BF16)
+
+
+def other_chip(x, k, devices):
+    return lax.ppermute(x, "tp", [(i, i ^ (2 * k)) for i in range(devices)])
+
+
+def other_core(x, devices):
+    return lax.ppermute(x, "tp", [(i, i ^ 1) for i in range(devices)])
+
+
+def fast_device(
+    hidden_states,
+    lengths,
+    qkv_weight,
+    rotated_key_cache,
+    earlier_value_cache,
+    out_weight,
+    expert_ids,
+    combine_weights,
+    gate_up_weight,
+    down_weight,
+):
+    requests, steps, model_width = hidden_states.shape
+    tokens = requests * steps
+    devices = lax.axis_size("tp")
+    chips = devices // 2
+    rows = tokens * GROUP
+    sibling_weight = other_core(out_weight, devices)
+    (heads,) = call(
+        functools.partial(project_kernel, requests, steps),
+        [((rows, 128), BF16)],
+        [lengths, hidden_states, qkv_weight],
+        "project",
+        smem=(0,),
+    )
+    gathered = jnp.stack([heads] + [other_chip(heads, k, devices) for k in range(1, chips)])
+    parts = call(
+        functools.partial(attend_kernel, requests, steps),
+        [((2 * rows, 128), F32)] * (chips + 1),
+        [lengths, gathered, other_core(gathered, devices), rotated_key_cache, earlier_value_cache],
+        "attend",
+        scratch=[pltpu.VMEM((devices, rows, 128), BF16), pltpu.VMEM((chips, 2 * rows, 128), F32)],
+        smem=(0,),
+    )
+    fresh = parts[chips]
+    arrived = [parts[0]] + [other_chip(parts[k], k, devices) for k in range(1, chips)]
+    (joined,) = call(join_kernel, [((2 * rows, 128), F32)], arrived, "join")
+    (projected,) = call(
+        functools.partial(output_kernel, requests, steps),
+        [((tokens, model_width), F32)],
+        [joined, other_core(joined, devices), fresh, out_weight, sibling_weight],
+        "output",
+    )
+    projections = [projected] + [other_chip(projected, k, devices) for k in range(1, chips)]
+    mixture, residual = call(
+        functools.partial(expert_kernel, requests),
+        [((tokens, model_width), BF16), ((tokens, model_width), F32)],
+        [hidden_states, *projections, expert_ids, combine_weights, gate_up_weight, down_weight],
+        "experts",
+    )
+    mixture = (mixture.astype(F32) + other_core(mixture, devices).astype(F32)).astype(BF16)
+    mixtures = [mixture] + [other_chip(mixture, k, devices) for k in range(1, chips)]
+    (result,) = call(
+        functools.partial(final_kernel, requests, steps),
+        [(hidden_states.shape, BF16)],
+        [residual, *mixtures],
+        "final",
+        hbm_out=True,
+    )
+    return result
 
 
 def merged(part, axis, combine):
@@ -79,7 +370,7 @@
     return jnp.sum(factors[:, :, None] * outcome, axis=0)
 
 
-def per_device(
+def general_device(
     hidden_states,
     lengths,
     qkv_weight,
@@ -212,6 +503,7 @@
         P("tp", None, None),
     )
     out_specs = P("req", None, None)
+    per_device = fast_device if mesh.shape["tp"] == 8 else general_device
     return jax.shard_map(
         per_device, mesh=mesh, in_specs=in_specs, out_specs=out_specs, check_vma=False
     )

time: 174 us -> 57.9 us (0.33)
  blocking collectives: 86.6 us -> 0 us
  waiting for transfers between devices: 54.8 us -> 18 us
  starting transfers between devices: 0.03 us -> 19.2 us
  between operations: 13.6 us -> 0.07 us
  local copies, waits for them, and re-layouts: 4.85 us -> 13.9 us
  matrix products: 7.72 us -> 0 us
  Pallas kernels: 0 us -> 6.22 us
  other arithmetic: 5.75 us -> 0.02 us
    all_gather x4 -> x0, blocking collectives: 60.6 us -> none  [the longest x3 45 us: merged(): gathered = jax.tree.map(lambda a: lax.all_gather(a, axis), part)]
    psum x1 -> x0, waiting for transfers between devices: 54.8 us -> none  [per_device(): projected_rows = lax.psum(head_terms, 'tp')]
    psum x1 -> x0, blocking collectives: 26 us -> none  [per_device(): lax.psum(expert_terms(normed_second, chosen, shares, gate_up_weight, down...]
    ppermute x0 -> x16, starting transfers between devices: none -> 19.2 us  [the longest x12 18.5 us: other_chip(): return lax.ppermute(x, 'tp', [(i, i ^ 2 * k) for i in range(devices)])]
    ppermute x0 -> x16, waiting for transfers between devices: none -> 18 us  [the longest x12 14.4 us: other_chip(): return lax.ppermute(x, 'tp', [(i, i ^ 2 * k) for i in range(devices)])]
    unnamed x12 -> x24, local copies, waits for them, and re-layouts: 2.64 us -> 13.9 us
    dot_general x8 -> x0, matrix products: 7.72 us -> none  [the longest x1 4.79 us: expert_terms(): jnp.einsum('nd,edf->enf', normed, gate_up_weight, preferred_element_type=...]
    pallas_call x0 -> x6, Pallas kernels: none -> 6.22 us  [call(): pl.pallas_call(kernel, out_shape=[jax.ShapeDtypeStruct(s, d) if hbm_out e...]
  transfers between devices with their start and end apart: 1 -> 16, of which waited for: 1 -> 11; matrix products, arithmetic and copies ran while one was open for 0% -> 0% of each run, Pallas kernels for 0% -> 5%
where the time goes in v1:
time: 57.9 us; the launch traced here: 57.3 us
  starting transfers between devices  19.2 us (33%)
  waiting for transfers between devices  18 us (31%)
  local copies, waits for them, and re-layouts  13.9 us (24%)
  Pallas kernels  6.22 us (11%)
    ppermute x12, starting transfers between devices, other_chip(): return lax.ppermute(x, 'tp', [(i, i ^ 2 * k) for i in range(devices)])  18.5 us
    ppermute x12, waiting for transfers between devices, other_chip(): return lax.ppermute(x, 'tp', [(i, i ^ 2 * k) for i in range(devices)])  14.4 us
    unnamed x24, local copies, waits for them, and re-layouts  13.9 us
    pallas_call x6, Pallas kernels, call(): pl.pallas_call(kernel, out_shape=[jax.ShapeDtypeStruct(s, d) if hbm_out e...  6.22 us
    ppermute x4, waiting for transfers between devices, other_core(): return lax.ppermute(x, 'tp', [(i, i ^ 1) for i in range(devices)])  3.58 us
  transfers between devices with their start and end apart: 16, of which 11 were waited for; matrix products, arithmetic and copies ran while one was open for 0% of the time, Pallas kernels for 5%

profile of v1, /device:TPU:0, one launch (start us, length us, event | category | flops | bytes accessed | tf_op | source)
XLA Modules:
  0.0 57.3 jit_solution(6074118080455606734)
XLA Ops:
  0.0 0.5 collective-permute-start.8
  0.5 0.0 copy-start.2
  0.5 1.0 %copy-done.2 = bf16[256,1024]{1,0:T(8,128)(2,1)S(1)} copy-done((bf16[256,1024]{1,0:T(8,128)(2,1)S(1)}, bf16[256,1024]{1,0:T(8,128)(2,1)}, u32[]{:S(2)}) %copy-start.2) | copy-done | bytes 524312
  1.5 0.0 copy-start.6
  1.5 0.8 %copy-done.6 = bf16[4,4,1024]{2,1,0:T(4,128)(2,1)S(1)} copy-done((bf16[4,4,1024]{2,1,0:T(4,128)(2,1)S(1)}, bf16[4,4,1024]{2,1,0:T(4,128)(2,1)}, u32[]{:S(2)}) %copy-start.6) | copy-done | bytes 32792
  2.3 0.0 copy-start.10
  2.3 0.7 %copy-done.10 = s32[4]{0:T(128)S(1)} copy-done((s32[4]{0:T(128)S(1)}, s32[4]{0:T(128)}, u32[]{:S(2)}) %copy-start.10) | copy-done | bytes 40
  2.9 1.0 %project.1 = bf16[32,128]{1,0:T(8,128)(2,1)S(1)} custom-call(s32[4]{0:T(128)S(1)} %copy-done.10, bf16[4,4,1024]{2,1,0:T(4,128)(2,1)S(1)} %copy-done.6, bf16[256,1024]{1,0:T(8,128)(2,1)S(1)} %copy-done.2), custom_call_target="tpu_custom_call" | custom-call | tf_op jit(solution)/shard_map/project/pallas_call | solution.py:40
  3.9 4.6 %collective-permute-start.2 = (bf16[32,128]{1,0:T(8,128)(2,1)S(1)}, bf16[32,128]{1,0:T(8,128)(2,1)S(1)}, u32[]{:S(2)}, u32[]{:S(2)}) collective-permute-start(bf16[32,128]{1,0:T(8,128)(2,1)S(1)} %project.1), channel_id=1, source_target_pairs={{0,6},{1,7},{2,4},{3,5},{4,2},{5,3},{6,0},{7,1},{8,14},{9,15},{10,... | collective-permute-start | bytes 24584 | tf_op jit(solution)/shard_map/ppermute | solution.py:238
  8.5 0.0 collective-permute-start.1
  8.5 0.6 %collective-permute-start = (bf16[32,128]{1,0:T(8,128)(2,1)S(1)}, bf16[32,128]{1,0:T(8,128)(2,1)S(1)}, u32[]{:S(2)}, u32[]{:S(2)}) collective-permute-start(bf16[32,128]{1,0:T(8,128)(2,1)S(1)} %project.1), channel_id=1, source_target_pairs={{0,2},{1,3},{2,0},{3,1},{4,6},{5,7},{6,4},{7,5},{8,10},{9,11},{10,... | collective-permute-start | bytes 24584 | tf_op jit(solution)/shard_map/ppermute | solution.py:238
  9.1 1.0 %collective-permute-done.2 = bf16[32,128]{1,0:T(8,128)(2,1)S(1)} collective-permute-done((bf16[32,128]{1,0:T(8,128)(2,1)S(1)}, bf16[32,128]{1,0:T(8,128)(2,1)S(1)}, u32[]{:S(2)}, u32[]{:S(2)}) %collective-permute-start.2) | collective-permute-done | bytes 8224 | tf_op jit(solution)/shard_map/ppermute | solution.py:238
  10.1 2.9 %collective-permute-done.1 = bf16[32,128]{1,0:T(8,128)(2,1)S(1)} collective-permute-done((bf16[32,128]{1,0:T(8,128)(2,1)S(1)}, bf16[32,128]{1,0:T(8,128)(2,1)S(1)}, u32[]{:S(2)}, u32[]{:S(2)}) %collective-permute-start.1) | collective-permute-done | bytes 8224 | tf_op jit(solution)/shard_map/ppermute | solution.py:238
  13.0 0.0 collective-permute-done
  13.1 0.1 collective-permute-start.3
  13.1 1.2 %collective-permute-done.3.sibling = bf16[4,32,128]{2,1,0:T(8,128)(2,1)S(1)} collective-permute-done((bf16[4,32,128]{2,1,0:T(8,128)(2,1)S(1)}, bf16[4,32,128]{2,1,0:T(8,128)(2,1)S(1)}, u32[]{:S(2)}, u32[]{:S(2)}) %collective-permute-start.3) | collective-permute-done | bytes 32800 | tf_op jit(solution)/shard_map/ppermute | solution.py:242
  14.3 0.0 copy-start.3
  14.3 1.0 %copy-done.3 = bf16[4,128,512]{2,1,0:T(8,128)(2,1)S(1)} copy-done((bf16[4,128,512]{2,1,0:T(8,128)(2,1)S(1)}, bf16[4,128,512]{2,1,0:T(8,128)(2,1)}, u32[]{:S(2)}) %copy-start.3) | copy-done | bytes 524312
  15.4 0.0 copy-start.4
  15.4 1.0 %copy-done.4 = bf16[4,128,512]{2,1,0:T(8,128)(2,1)S(1)} copy-done((bf16[4,128,512]{2,1,0:T(8,128)(2,1)S(1)}, bf16[4,128,512]{2,1,0:T(8,128)(2,1)}, u32[]{:S(2)}) %copy-start.4) | copy-done | bytes 524312
  16.4 0.0 copy-start.11
  16.4 0.7 %copy-done.11 = s32[4]{0:T(128)S(1)} copy-done((s32[4]{0:T(128)S(1)}, s32[4]{0:T(128)}, u32[]{:S(2)}) %copy-start.11) | copy-done | bytes 40
  17.1 2.0 %attend.1 = (f32[64,128]{1,0:T(8,128)S(1)}, f32[64,128]{1,0:T(8,128)S(1)}, f32[64,128]{1,0:T(8,128)S(1)}, f32[64,128]{1,0:T(8,128)S(1)}, f32[64,128]{1,0:T(8,128)S(1)}) custom-call(s32[4]{0:T(128)S(1)} %copy-done.11, bf16[4,32,128]{2,1,0:T(8,128)(2,1)S(1)} %pad_maximum_fusion.own, bf16[4,32,128]{2,1,0:T(8,128)(2,1)S(1)} %collective-permute-done.3.sibling, ...), custom_call_target="tpu_custom_call" | custom-call | tf_op jit(solution)/shard_map/attend/pallas_call | solution.py:40
  19.1 0.1 collective-permute-start.4
  19.2 2.1 %collective-permute-start.5 = (f32[64,128]{1,0:T(8,128)S(1)}, f32[64,128]{1,0:T(8,128)S(1)}, u32[]{:S(2)}, u32[]{:S(2)}) collective-permute-start(f32[64,128]{1,0:T(8,128)S(1)} %get-tuple-element.14), channel_id=1, source_target_pairs={{0,4},{1,5},{2,6},{3,7},{4,0},{5,1},{6,2},{7,3},{8,12},{9,13},{10,... | collective-permute-start | bytes 98312 | tf_op jit(solution)/shard_map/ppermute | solution.py:238
  21.2 2.3 %collective-permute-start.6 = (f32[64,128]{1,0:T(8,128)S(1)}, f32[64,128]{1,0:T(8,128)S(1)}, u32[]{:S(2)}, u32[]{:S(2)}) collective-permute-start(f32[64,128]{1,0:T(8,128)S(1)} %get-tuple-element.15), channel_id=1, source_target_pairs={{0,6},{1,7},{2,4},{3,5},{4,2},{5,3},{6,0},{7,1},{8,14},{9,15},{10,... | collective-permute-start | bytes 98312 | tf_op jit(solution)/shard_map/ppermute | solution.py:238
  23.5 0.0 collective-permute-done.4.b
  23.5 0.5 collective-permute-done.5.c
  24.0 2.9 %collective-permute-done.6.d = f32[64,128]{1,0:T(8,128)S(1)} collective-permute-done((f32[64,128]{1,0:T(8,128)S(1)}, f32[64,128]{1,0:T(8,128)S(1)}, u32[]{:S(2)}, u32[]{:S(2)}) %collective-permute-start.6) | collective-permute-done | bytes 32800 | tf_op jit(solution)/shard_map/ppermute | solution.py:238
  26.9 0.1 join.1.own
  27.1 0.1 collective-permute-start.7
  27.1 1.2 %collective-permute-done.7.sibling = f32[64,128]{1,0:T(8,128)S(1)} collective-permute-done((f32[64,128]{1,0:T(8,128)S(1)}, f32[64,128]{1,0:T(8,128)S(1)}, u32[]{:S(2)}, u32[]{:S(2)}) %collective-permute-start.7) | collective-permute-done | bytes 32800 | tf_op jit(solution)/shard_map/ppermute | solution.py:242
  28.3 0.0 collective-permute-done.8.sibling_weight
  28.3 0.0 copy-start.5
  28.3 0.9 %copy-done.5 = bf16[128,1024]{1,0:T(8,128)(2,1)S(1)} copy-done((bf16[128,1024]{1,0:T(8,128)(2,1)S(1)}, bf16[128,1024]{1,0:T(8,128)(2,1)}, u32[]{:S(2)}) %copy-start.5) | copy-done | bytes 262168
  29.3 0.3 output.1.a
  29.6 2.3 %collective-permute-start.11 = (f32[16,1024]{1,0:T(8,128)S(1)}, f32[16,1024]{1,0:T(8,128)S(1)}, u32[]{:S(2)}, u32[]{:S(2)}) collective-permute-start(f32[16,1024]{1,0:T(8,128)S(1)} %output.1.a), channel_id=1, source_target_pairs={{0,6},{1,7},{2,4},{3,5},{4,2},{5,3},{6,0},{7,1},{8,14},{9,15},{10,... | collective-permute-start | bytes 196616 | tf_op jit(solution)/shard_map/ppermute | solution.py:238
  31.9 0.0 collective-permute-start.10
  31.9 2.1 %collective-permute-start.9 = (f32[16,1024]{1,0:T(8,128)S(1)}, f32[16,1024]{1,0:T(8,128)S(1)}, u32[]{:S(2)}, u32[]{:S(2)}) collective-permute-start(f32[16,1024]{1,0:T(8,128)S(1)} %output.1.a), channel_id=1, source_target_pairs={{0,2},{1,3},{2,0},{3,1},{4,6},{5,7},{6,4},{7,5},{8,10},{9,11},{10,... | collective-permute-start | bytes 196616 | tf_op jit(solution)/shard_map/ppermute | solution.py:238
  34.0 2.4 %collective-permute-done.11.d = f32[16,1024]{1,0:T(8,128)S(1)} collective-permute-done((f32[16,1024]{1,0:T(8,128)S(1)}, f32[16,1024]{1,0:T(8,128)S(1)}, u32[]{:S(2)}, u32[]{:S(2)}) %collective-permute-start.11) | collective-permute-done | bytes 65568 | tf_op jit(solution)/shard_map/ppermute | solution.py:238
  36.4 2.0 %collective-permute-done.10.c = f32[16,1024]{1,0:T(8,128)S(1)} collective-permute-done((f32[16,1024]{1,0:T(8,128)S(1)}, f32[16,1024]{1,0:T(8,128)S(1)}, u32[]{:S(2)}, u32[]{:S(2)}) %collective-permute-start.10) | collective-permute-done | bytes 65568 | tf_op jit(solution)/shard_map/ppermute | solution.py:238
  38.4 0.0 collective-permute-done.9.b
  38.4 0.0 copy-start
  38.4 3.4 %copy-done = bf16[4,1024,1024]{2,1,0:T(8,128)(2,1)S(1)} copy-done((bf16[4,1024,1024]{2,1,0:T(8,128)(2,1)S(1)}, bf16[4,1024,1024]{2,1,0:T(8,128)(2,1)}, u32[]{:S(2)}) %copy-start) | copy-done | bytes 8388632
  41.8 0.0 copy-start.1
  41.8 2.2 %copy-done.1 = bf16[4,512,1024]{2,1,0:T(8,128)(2,1)S(1)} copy-done((bf16[4,512,1024]{2,1,0:T(8,128)(2,1)S(1)}, bf16[4,512,1024]{2,1,0:T(8,128)(2,1)}, u32[]{:S(2)}) %copy-start.1) | copy-done | bytes 4194328
  44.0 0.0 copy-start.7
  44.0 0.8 %copy-done.7 = bf16[4,4,1024]{2,1,0:T(4,128)(2,1)S(1)} copy-done((bf16[4,4,1024]{2,1,0:T(4,128)(2,1)S(1)}, bf16[4,4,1024]{2,1,0:T(4,128)(2,1)}, u32[]{:S(2)}) %copy-start.7) | copy-done | bytes 32792
  44.7 0.0 copy-start.8
  44.7 0.7 %copy-done.8 = s32[4,4,8]{2,1,0:T(4,128)S(1)} copy-done((s32[4,4,8]{2,1,0:T(4,128)S(1)}, s32[4,4,8]{2,1,0:T(4,128)}, u32[]{:S(2)}) %copy-start.8) | copy-done | bytes 536
  45.4 0.0 copy-start.9
  45.4 0.7 %copy-done.9 = s32[4,4,8]{2,1,0:T(4,128)S(1)} copy-done((s32[4,4,8]{2,1,0:T(4,128)S(1)}, s32[4,4,8]{2,1,0:T(4,128)}, u32[]{:S(2)}) %copy-start.9) | copy-done | bytes 536
  46.1 2.2 %experts.1 = (bf16[16,1024]{1,0:T(8,128)(2,1)S(1)}, f32[16,1024]{1,0:T(8,128)S(1)}) custom-call(bf16[4,4,1024]{2,1,0:T(4,128)(2,1)S(1)} %copy-done.7, f32[16,1024]{1,0:T(8,128)S(1)} %output.1.a, f32[16,1024]{1,0:T(8,128)S(1)} %collective-permute-done.9.b, f32[16,1024]{1,0:T(8,128)S(1)} %collective-permute-done.10.c, ...), custom_call_target="tpu_custom_call" | custom-call | tf_op jit(solution)/shard_map/experts/pallas_call | solution.py:40
  48.3 0.0 collective-permute-start.12
  48.3 1.2 %collective-permute-done.12 = bf16[16,1024]{1,0:T(8,128)(2,1)S(1)} collective-permute-done((bf16[16,1024]{1,0:T(8,128)(2,1)S(1)}, bf16[16,1024]{1,0:T(8,128)(2,1)S(1)}, u32[]{:S(2)}, u32[]{:S(2)}) %collective-permute-start.12) | collective-permute-done | bytes 32800 | tf_op jit(solution)/shard_map/ppermute | solution.py:242
  49.5 2.4 %collective-permute-start.15 = (bf16[16,1024]{1,0:T(8,128)(2,1)S(1)}, bf16[16,1024]{1,0:T(8,128)(2,1)S(1)}, u32[]{:S(2)}, u32[]{:S(2)}) collective-permute-start(bf16[16,1024]{1,0:T(8,128)(2,1)S(1)} %add_convert_fusion.a), channel_id=1, source_target_pairs={{0,6},{1,7},{2,4},{3,5},{4,2},{5,3},{6,0},{7,1},{8,14},{9,15},{10,... | collective-permute-start | bytes 98312 | tf_op jit(solution)/shard_map/ppermute | solution.py:238
  51.9 0.0 collective-permute-start.14
  51.9 2.1 %collective-permute-start.13 = (bf16[16,1024]{1,0:T(8,128)(2,1)S(1)}, bf16[16,1024]{1,0:T(8,128)(2,1)S(1)}, u32[]{:S(2)}, u32[]{:S(2)}) collective-permute-start(bf16[16,1024]{1,0:T(8,128)(2,1)S(1)} %add_convert_fusion.a), channel_id=1, source_target_pairs={{0,2},{1,3},{2,0},{3,1},{4,6},{5,7},{6,4},{7,5},{8,10},{9,11},{10,... | collective-permute-start | bytes 98312 | tf_op jit(solution)/shard_map/ppermute | solution.py:238
  54.0 1.3 %collective-permute-done.15.d = bf16[16,1024]{1,0:T(8,128)(2,1)S(1)} collective-permute-done((bf16[16,1024]{1,0:T(8,128)(2,1)S(1)}, bf16[16,1024]{1,0:T(8,128)(2,1)S(1)}, u32[]{:S(2)}, u32[]{:S(2)}) %collective-permute-start.15) | collective-permute-done | bytes 32800 | tf_op jit(solution)/shard_map/ppermute | solution.py:238
  55.3 1.4 %collective-permute-done.14.c = bf16[16,1024]{1,0:T(8,128)(2,1)S(1)} collective-permute-done((bf16[16,1024]{1,0:T(8,128)(2,1)S(1)}, bf16[16,1024]{1,0:T(8,128)(2,1)S(1)}, u32[]{:S(2)}, u32[]{:S(2)}) %collective-permute-start.14) | collective-permute-done | bytes 32800 | tf_op jit(solution)/shard_map/ppermute | solution.py:238
  56.7 0.0 collective-permute-done.13.b
  56.7 0.6 %final.1 = bf16[4,4,1024]{2,1,0:T(4,128)(2,1)} custom-call(f32[16,1024]{1,0:T(8,128)S(1)} %get-tuple-element.17.residual, bf16[16,1024]{1,0:T(8,128)(2,1)S(1)} %add_convert_fusion.a, bf16[16,1024]{1,0:T(8,128)(2,1)S(1)} %collective-permute-done.13.b, bf16[16,1024]{1,0:T(8,128)(2,1)S(1)} %collective-permute-done.14.c, ...), custom_call_target="tpu_custom_call" | custom-call | tf_op jit(solution)/shard_map/final/pallas_call | solution.py:40
  (2 shorter events, 0.0 us)
Async XLA Ops:
  0.0 28.3 %collective-permute-start.8 = (bf16[128,1024]{1,0:T(8,128)(2,1)}, bf16[128,1024]{1,0:T(8,128)(2,1)S(1)}, u32[]{:S(2)}, u32[]{:S(2)}) collective-permute-start(bf16[128,1024]{1,0:T(8,128)(2,1)} %weight.3), channel_id=1, source_target_pairs={{0,1},{1,0},{2,3},{3,2},{4,5},{5,4},{6,7},{7,6},{8,9},{9,8},{10,11... | collective-permute-start | bytes 786440 | tf_op jit(solution)/shard_map/ppermute | solution.py:242
  0.5 1.0 %copy-start.2 = (bf16[256,1024]{1,0:T(8,128)(2,1)S(1)}, bf16[256,1024]{1,0:T(8,128)(2,1)}, u32[]{:S(2)}) copy-start(bf16[256,1024]{1,0:T(8,128)(2,1)} %weight.2) | copy-start | bytes 1572868
  1.5 0.8 %copy-start.6 = (bf16[4,4,1024]{2,1,0:T(4,128)(2,1)S(1)}, bf16[4,4,1024]{2,1,0:T(4,128)(2,1)}, u32[]{:S(2)}) copy-start(bf16[4,4,1024]{2,1,0:T(4,128)(2,1)} %hidden.3) | copy-start | bytes 98308
  2.3 0.7 %copy-start.10 = (s32[4]{0:T(128)S(1)}, s32[4]{0:T(128)}, u32[]{:S(2)}) copy-start(s32[4]{0:T(128)} %lengths.3) | copy-start | bytes 52
  3.9 6.2 %collective-permute-start.2 = (bf16[32,128]{1,0:T(8,128)(2,1)S(1)}, bf16[32,128]{1,0:T(8,128)(2,1)S(1)}, u32[]{:S(2)}, u32[]{:S(2)}) collective-permute-start(bf16[32,128]{1,0:T(8,128)(2,1)S(1)} %project.1), channel_id=1, source_target_pairs={{0,6},{1,7},{2,4},{3,5},{4,2},{5,3},{6,0},{7,1},{8,14},{9,15},{10,... | collective-permute-start | bytes 24584 | tf_op jit(solution)/shard_map/ppermute | solution.py:238
  8.5 4.5 %collective-permute-start.1 = (bf16[32,128]{1,0:T(8,128)(2,1)S(1)}, bf16[32,128]{1,0:T(8,128)(2,1)S(1)}, u32[]{:S(2)}, u32[]{:S(2)}) collective-permute-start(bf16[32,128]{1,0:T(8,128)(2,1)S(1)} %project.1), channel_id=1, source_target_pairs={{0,4},{1,5},{2,6},{3,7},{4,0},{5,1},{6,2},{7,3},{8,12},{9,13},{10,... | collective-permute-start | bytes 24584 | tf_op jit(solution)/shard_map/ppermute | solution.py:238
  8.5 4.5 %collective-permute-start = (bf16[32,128]{1,0:T(8,128)(2,1)S(1)}, bf16[32,128]{1,0:T(8,128)(2,1)S(1)}, u32[]{:S(2)}, u32[]{:S(2)}) collective-permute-start(bf16[32,128]{1,0:T(8,128)(2,1)S(1)} %project.1), channel_id=1, source_target_pairs={{0,2},{1,3},{2,0},{3,1},{4,6},{5,7},{6,4},{7,5},{8,10},{9,11},{10,... | collective-permute-start | bytes 24584 | tf_op jit(solution)/shard_map/ppermute | solution.py:238
  13.1 1.3 %collective-permute-start.3 = (bf16[4,32,128]{2,1,0:T(8,128)(2,1)S(1)}, bf16[4,32,128]{2,1,0:T(8,128)(2,1)S(1)}, u32[]{:S(2)}, u32[]{:S(2)}) collective-permute-start(bf16[4,32,128]{2,1,0:T(8,128)(2,1)S(1)} %pad_maximum_fusion.own), channel_id=1, source_target_pairs={{0,1},{1,0},{2,3},{3,2},{4,5},{5,4},{6,7},{7,6},{8,9},{9,8},{10,11... | collective-permute-start | bytes 98312 | tf_op jit(solution)/shard_map/ppermute | solution.py:242
  14.3 1.0 %copy-start.3 = (bf16[4,128,512]{2,1,0:T(8,128)(2,1)S(1)}, bf16[4,128,512]{2,1,0:T(8,128)(2,1)}, u32[]{:S(2)}) copy-start(bf16[4,128,512]{2,1,0:T(8,128)(2,1)} %keys.1) | copy-start | bytes 1572868
  15.4 1.0 %copy-start.4 = (bf16[4,128,512]{2,1,0:T(8,128)(2,1)S(1)}, bf16[4,128,512]{2,1,0:T(8,128)(2,1)}, u32[]{:S(2)}) copy-start(bf16[4,128,512]{2,1,0:T(8,128)(2,1)} %values.1) | copy-start | bytes 1572868
  16.4 0.7 %copy-start.11 = (s32[4]{0:T(128)S(1)}, s32[4]{0:T(128)}, u32[]{:S(2)}) copy-start(s32[4]{0:T(128)} %lengths.3) | copy-start | bytes 52
  19.1 4.4 %collective-permute-start.4 = (f32[64,128]{1,0:T(8,128)S(1)}, f32[64,128]{1,0:T(8,128)S(1)}, u32[]{:S(2)}, u32[]{:S(2)}) collective-permute-start(f32[64,128]{1,0:T(8,128)S(1)} %get-tuple-element.13), channel_id=1, source_target_pairs={{0,2},{1,3},{2,0},{3,1},{4,6},{5,7},{6,4},{7,5},{8,10},{9,11},{10,... | collective-permute-start | bytes 98312 | tf_op jit(solution)/shard_map/ppermute | solution.py:238
  19.2 4.9 %collective-permute-start.5 = (f32[64,128]{1,0:T(8,128)S(1)}, f32[64,128]{1,0:T(8,128)S(1)}, u32[]{:S(2)}, u32[]{:S(2)}) collective-permute-start(f32[64,128]{1,0:T(8,128)S(1)} %get-tuple-element.14), channel_id=1, source_target_pairs={{0,4},{1,5},{2,6},{3,7},{4,0},{5,1},{6,2},{7,3},{8,12},{9,13},{10,... | collective-permute-start | bytes 98312 | tf_op jit(solution)/shard_map/ppermute | solution.py:238
  21.2 5.7 %collective-permute-start.6 = (f32[64,128]{1,0:T(8,128)S(1)}, f32[64,128]{1,0:T(8,128)S(1)}, u32[]{:S(2)}, u32[]{:S(2)}) collective-permute-start(f32[64,128]{1,0:T(8,128)S(1)} %get-tuple-element.15), channel_id=1, source_target_pairs={{0,6},{1,7},{2,4},{3,5},{4,2},{5,3},{6,0},{7,1},{8,14},{9,15},{10,... | collective-permute-start | bytes 98312 | tf_op jit(solution)/shard_map/ppermute | solution.py:238
  27.1 1.3 %collective-permute-start.7 = (f32[64,128]{1,0:T(8,128)S(1)}, f32[64,128]{1,0:T(8,128)S(1)}, u32[]{:S(2)}, u32[]{:S(2)}) collective-permute-start(f32[64,128]{1,0:T(8,128)S(1)} %join.1.own), channel_id=1, source_target_pairs={{0,1},{1,0},{2,3},{3,2},{4,5},{5,4},{6,7},{7,6},{8,9},{9,8},{10,11... | collective-permute-start | bytes 98312 | tf_op jit(solution)/shard_map/ppermute | solution.py:242
  28.3 1.0 %copy-start.5 = (bf16[128,1024]{1,0:T(8,128)(2,1)S(1)}, bf16[128,1024]{1,0:T(8,128)(2,1)}, u32[]{:S(2)}) copy-start(bf16[128,1024]{1,0:T(8,128)(2,1)} %weight.3) | copy-start | bytes 786436
  29.6 6.8 %collective-permute-start.11 = (f32[16,1024]{1,0:T(8,128)S(1)}, f32[16,1024]{1,0:T(8,128)S(1)}, u32[]{:S(2)}, u32[]{:S(2)}) collective-permute-start(f32[16,1024]{1,0:T(8,128)S(1)} %output.1.a), channel_id=1, source_target_pairs={{0,6},{1,7},{2,4},{3,5},{4,2},{5,3},{6,0},{7,1},{8,14},{9,15},{10,... | collective-permute-start | bytes 196616 | tf_op jit(solution)/shard_map/ppermute | solution.py:238
  31.9 6.5 %collective-permute-start.10 = (f32[16,1024]{1,0:T(8,128)S(1)}, f32[16,1024]{1,0:T(8,128)S(1)}, u32[]{:S(2)}, u32[]{:S(2)}) collective-permute-start(f32[16,1024]{1,0:T(8,128)S(1)} %output.1.a), channel_id=1, source_target_pairs={{0,4},{1,5},{2,6},{3,7},{4,0},{5,1},{6,2},{7,3},{8,12},{9,13},{10,... | collective-permute-start | bytes 196616 | tf_op jit(solution)/shard_map/ppermute | solution.py:238
  31.9 6.5 %collective-permute-start.9 = (f32[16,1024]{1,0:T(8,128)S(1)}, f32[16,1024]{1,0:T(8,128)S(1)}, u32[]{:S(2)}, u32[]{:S(2)}) collective-permute-start(f32[16,1024]{1,0:T(8,128)S(1)} %output.1.a), channel_id=1, source_target_pairs={{0,2},{1,3},{2,0},{3,1},{4,6},{5,7},{6,4},{7,5},{8,10},{9,11},{10,... | collective-permute-start | bytes 196616 | tf_op jit(solution)/shard_map/ppermute | solution.py:238
  38.4 3.4 %copy-start = (bf16[4,1024,1024]{2,1,0:T(8,128)(2,1)S(1)}, bf16[4,1024,1024]{2,1,0:T(8,128)(2,1)}, u32[]{:S(2)}) copy-start(bf16[4,1024,1024]{2,1,0:T(8,128)(2,1)} %gate_up.1) | copy-start | bytes 25165828
  41.8 2.2 %copy-start.1 = (bf16[4,512,1024]{2,1,0:T(8,128)(2,1)S(1)}, bf16[4,512,1024]{2,1,0:T(8,128)(2,1)}, u32[]{:S(2)}) copy-start(bf16[4,512,1024]{2,1,0:T(8,128)(2,1)} %down.1) | copy-start | bytes 12582916
  44.0 0.8 %copy-start.7 = (bf16[4,4,1024]{2,1,0:T(4,128)(2,1)S(1)}, bf16[4,4,1024]{2,1,0:T(4,128)(2,1)}, u32[]{:S(2)}) copy-start(bf16[4,4,1024]{2,1,0:T(4,128)(2,1)} %hidden.3) | copy-start | bytes 98308
  44.7 0.7 %copy-start.8 = (s32[4,4,8]{2,1,0:T(4,128)S(1)}, s32[4,4,8]{2,1,0:T(4,128)}, u32[]{:S(2)}) copy-start(s32[4,4,8]{2,1,0:T(4,128)} %ids.1) | copy-start | bytes 1540
  45.4 0.7 %copy-start.9 = (s32[4,4,8]{2,1,0:T(4,128)S(1)}, s32[4,4,8]{2,1,0:T(4,128)}, u32[]{:S(2)}) copy-start(s32[4,4,8]{2,1,0:T(4,128)} %shares.1) | copy-start | bytes 1540
  48.3 1.2 %collective-permute-start.12 = (bf16[16,1024]{1,0:T(8,128)(2,1)S(1)}, bf16[16,1024]{1,0:T(8,128)(2,1)S(1)}, u32[]{:S(2)}, u32[]{:S(2)}) collective-permute-start(bf16[16,1024]{1,0:T(8,128)(2,1)S(1)} %get-tuple-element.18), channel_id=1, source_target_pairs={{0,1},{1,0},{2,3},{3,2},{4,5},{5,4},{6,7},{7,6},{8,9},{9,8},{10,11... | collective-permute-start | bytes 98312 | tf_op jit(solution)/shard_map/ppermute | solution.py:242
  49.5 5.8 %collective-permute-start.15 = (bf16[16,1024]{1,0:T(8,128)(2,1)S(1)}, bf16[16,1024]{1,0:T(8,128)(2,1)S(1)}, u32[]{:S(2)}, u32[]{:S(2)}) collective-permute-start(bf16[16,1024]{1,0:T(8,128)(2,1)S(1)} %add_convert_fusion.a), channel_id=1, source_target_pairs={{0,6},{1,7},{2,4},{3,5},{4,2},{5,3},{6,0},{7,1},{8,14},{9,15},{10,... | collective-permute-start | bytes 98312 | tf_op jit(solution)/shard_map/ppermute | solution.py:238
  51.9 4.8 %collective-permute-start.14 = (bf16[16,1024]{1,0:T(8,128)(2,1)S(1)}, bf16[16,1024]{1,0:T(8,128)(2,1)S(1)}, u32[]{:S(2)}, u32[]{:S(2)}) collective-permute-start(bf16[16,1024]{1,0:T(8,128)(2,1)S(1)} %add_convert_fusion.a), channel_id=1, source_target_pairs={{0,4},{1,5},{2,6},{3,7},{4,0},{5,1},{6,2},{7,3},{8,12},{9,13},{10,... | collective-permute-start | bytes 98312 | tf_op jit(solution)/shard_map/ppermute | solution.py:238
  51.9 4.8 %collective-permute-start.13 = (bf16[16,1024]{1,0:T(8,128)(2,1)S(1)}, bf16[16,1024]{1,0:T(8,128)(2,1)S(1)}, u32[]{:S(2)}, u32[]{:S(2)}) collective-permute-start(bf16[16,1024]{1,0:T(8,128)(2,1)S(1)} %add_convert_fusion.a), channel_id=1, source_target_pairs={{0,2},{1,3},{2,0},{3,1},{4,6},{5,7},{6,4},{7,5},{8,10},{9,11},{10,... | collective-permute-start | bytes 98312 | tf_op jit(solution)/shard_map/ppermute | solution.py:238

commit v2 on v1

--- a/solution.py
+++ b/solution.py
@@ -16,7 +16,9 @@
 NEGATIVE = -1e30
 F32 = jnp.float32
 BF16 = jnp.bfloat16
-VMEM_LIMIT = 8 * 1024 * 1024
+VMEM_LIMIT = 16 * 1024 * 1024
+ORDER = ((3, 2, 1),) * 4
+COST = (8_000_000, 6_000_000, 1_000_000, 12_000_000)
 
 
 def iota(shape, dim):
@@ -27,42 +29,87 @@
     return jnp.concatenate(blocks, axis=0)
 
 
-def in_vmem(x):
-    return pltpu.with_memory_space_constraint(x, pltpu.VMEM)
-
-
-def whole(memory_space=pltpu.VMEM):
-    return pl.BlockSpec(memory_space=memory_space)
-
-
-def call(kernel, outs, operands, name, scratch=(), smem=(), hbm_out=False):
-    args = [x if i in smem else in_vmem(x) for i, x in enumerate(operands)]
+def on(space):
+    return pl.BlockSpec(memory_space=space)
+
+
+def call(kernel, outs, operands, name, stay=(), scratch=(), hbm_out=False, cost=0):
+    operands = [
+        pltpu.with_memory_space_constraint(x, pltpu.HBM) if i in stay else x for i, x in enumerate(operands)
+    ]
     return pl.pallas_call(
         kernel,
         out_shape=[
             jax.ShapeDtypeStruct(s, d) if hbm_out else pltpu.VMEM(s, d) for s, d in outs
         ],
-        in_specs=[whole(pltpu.SMEM if i in smem else pltpu.VMEM) for i in range(len(args))],
-        out_specs=[whole() for _ in outs],
+        in_specs=[on(pltpu.HBM if i in stay else pltpu.VMEM) for i in range(len(operands))],
+        out_specs=[on(pltpu.VMEM) for _ in outs],
         scratch_shapes=list(scratch),
         compiler_params=pltpu.CompilerParams(vmem_limit_bytes=VMEM_LIMIT),
+        cost_estimate=pl.CostEstimate(flops=0, bytes_accessed=cost, transcendentals=0),
         name=name,
-    )(*args)
-
-
-def project_kernel(requests, steps, lengths, hidden, weight, out):
+    )(*operands)
+
+
+def start_all(pairs, semaphores):
+    copies = [
+        pltpu.make_async_copy(source, target, semaphores.at[i]) for i, (source, target) in enumerate(pairs)
+    ]
+    for copy in copies:
+        copy.start()
+    return copies
+
+
+def project_kernel(
+    lengths_in,
+    hidden_in,
+    weight_in,
+    keys_in,
+    values_in,
+    out_weight_in,
+    ids_in,
+    shares_in,
+    out,
+    limits,
+    inputs,
+    keys,
+    values,
+    out_weight,
+    ids,
+    shares,
+    lengths,
+    hidden,
+    weight,
+    semaphores,
+):
+    copies = start_all(
+        [
+            (lengths_in, lengths),
+            (hidden_in, hidden),
+            (weight_in, weight),
+            (keys_in, keys),
+            (values_in, values),
+            (out_weight_in, out_weight),
+            (ids_in, ids),
+            (shares_in, shares),
+        ],
+        semaphores,
+    )
+    requests, steps, _ = hidden.shape
     device = lax.axis_index("tp")
     devices = lax.axis_size("tp")
+    copies[1].wait()
     x = merge_rows([hidden[b].astype(F32) for b in range(requests)])
+    inputs[...] = x
     normed = (x * lax.rsqrt(jnp.mean(x * x, axis=-1, keepdims=True) + EPSILON)).astype(BF16)
-    y = lax.dot_general(normed, weight[...], (((1,), (1,)), ((), ())), preferred_element_type=F32)
-    y = y.astype(BF16).astype(F32)
-    tokens, width = y.shape
+    copies[0].wait()
+    tokens = requests * steps
     row = iota((tokens, 128), 0)
     lane = iota((tokens, 128), 1)
     position = jnp.zeros((tokens, 128), jnp.int32)
     for b in range(requests):
         position = jnp.where(row // steps == b, lengths[b] + row - b * steps, position)
+        limits[b] = jnp.full(limits.shape[1:], lengths[b], jnp.int32)
     half = HEAD_DIMENSION // 2
     rates = jnp.exp((lane % half).astype(F32) * (-2.0 / HEAD_DIMENSION * 9.210340371976184))
     angles = position.astype(F32) * rates
@@ -71,8 +118,11 @@
     sine = jnp.where(turned, jnp.sin(angles), 0.0)
     first = lane % HEAD_DIMENSION < half
     sine = jnp.where(first, -sine, sine)
+    copies[2].wait()
+    y = lax.dot_general(normed, weight[...], (((1,), (1,)), ((), ())), preferred_element_type=F32)
+    y = y.astype(BF16).astype(F32)
     parts = []
-    for k in range(width // 128):
+    for k in range(y.shape[1] // 128):
         v = y[:, k * 128 : (k + 1) * 128]
         other = jnp.where(first, pltpu.roll(v, 128 - half, 1), pltpu.roll(v, half, 1))
         parts.append(v * cosine + other * sine)
@@ -86,6 +136,26 @@
     query = merge_rows(rows)
     plain = merge_rows([a, b])
     out[...] = jnp.where(device < devices // 2, query, plain).astype(BF16)
+    for copy in copies[3:]:
+        copy.wait()
+
+
+def fetch_kernel(after, source, target, semaphores):
+    for copy in start_all([(source.at[i], target.at[i]) for i in range(target.shape[0])], semaphores):
+        copy.wait()
+
+
+def fetch(x, after, name):
+    (there,) = call(
+        fetch_kernel,
+        [(x.shape, x.dtype)],
+        [after, x],
+        name,
+        stay=(1,),
+        scratch=[pltpu.SemaphoreType.DMA((x.shape[0],))],
+        cost=x.size * 2,
+    )
+    return there
 
 
 def fold(x, rows, lanes):
@@ -126,8 +196,21 @@
 
 
 def attend_kernel(
-    requests, steps, lengths, own, sibling, keys, values, out0, out1, out2, out3, fresh, heads, blocks
+    steps,
+    limits,
+    own,
+    sibling,
+    keys,
+    values,
+    out0,
+    out1,
+    out2,
+    out3,
+    fresh,
+    heads,
+    blocks,
 ):
+    requests = keys.shape[0]
     device = lax.axis_index("tp")
     chip, core = device // 2, device % 2
     chips = own.shape[0]
@@ -144,7 +227,7 @@
     for r in range(requests):
         q = spread(query[r * rows : (r + 1) * rows], groups)
         scores = lax.dot_general(q, keys[r], (((1,), (1,)), ((), ())), preferred_element_type=F32)
-        peak, total, summed = soft(scores, position < lengths[r], values[r])
+        peak, total, summed = soft(scores, position < limits[r, 0:1], values[r])
         summed = fold(summed, rows, lanes)
         stats = pack_stats(fold(peak, rows, lanes), fold(total, rows, lanes))
         for k in range(chips):
@@ -180,7 +263,8 @@
     return (*unpack_stats(ref[n:]), ref[0:n])
 
 
-def join_kernel(a, b, c, d, out):
+def join_kernel(order, a, b, c, d, fetched, out):
+    a, b, c, d = sort_chips(order, a, (b, c, d))
     peak, total, summed = join(join(read_part(a), read_part(b)), join(read_part(c), read_part(d)))
     n = summed.shape[0]
     out[0:n] = summed
@@ -200,26 +284,42 @@
     one = jnp.where(low, pltpu.roll(heads[0], HEAD_DIMENSION, 1), heads[1])
     mine = jnp.where(core == 0, zero, one).astype(BF16)
     theirs = jnp.where(core == 0, one, zero).astype(BF16)
-    out[...] = jnp.dot(mine, weight[...], preferred_element_type=F32) + jnp.dot(
+    projected = jnp.dot(mine, weight[...], preferred_element_type=F32) + jnp.dot(
         theirs, sibling_weight[...], preferred_element_type=F32
     )
-
-
-def expert_kernel(requests, hidden, a, b, c, d, ids, shares, gate_up, down, out, residual_out):
+    out[...] = projected.astype(BF16)
+
+
+def sort_chips(order, first, parts):
+    return [first] + [part for _, part in sorted(zip(order, parts), key=lambda pair: pair[0])]
+
+
+def gather_kernel(order, a, b, c, d, fetched, out):
+    for k, x in enumerate(sort_chips(order, a, (b, c, d))):
+        out[k] = x[...]
+
+
+def sum_chips(order, a, b, c, d):
+    a, b, c, d = sort_chips(order, a, (b, c, d))
+    return (a[...].astype(F32) + b[...].astype(F32)) + (c[...].astype(F32) + d[...].astype(F32))
+
+
+def expert_kernel(order, inputs, a, b, c, d, ids, shares, gate_up, down, out, residual_out):
     device = lax.axis_index("tp")
-    x = merge_rows([hidden[r].astype(F32) for r in range(requests)])
-    residual = x + ((a[...] + b[...]) + (c[...] + d[...]))
+    residual = inputs[...] + sum_chips(order, a, b, c, d)
     residual_out[...] = residual
     normed = (
         residual * lax.rsqrt(jnp.mean(residual * residual, axis=-1, keepdims=True) + EPSILON)
     ).astype(BF16)
+    requests = ids.shape[0]
     chosen = merge_rows([ids[r] for r in range(requests)])
     share = merge_rows([shares[r].astype(F32) for r in range(requests)]) * (1.0 / 65536.0)
-    experts, _, width = gate_up.shape
+    experts = gate_up.shape[0]
     total = None
     for e in range(experts):
         united = jnp.dot(normed, gate_up[e], preferred_element_type=F32)
-        gate, up = united[:, : width // 2], united[:, width // 2 :]
+        width = united.shape[1] // 2
+        gate, up = united[:, :width], united[:, width:]
         active = (gate / (1.0 + jnp.exp(-gate)) * up).astype(BF16)
         outcome = jnp.dot(active, down[e], preferred_element_type=F32)
         factor = jnp.sum(jnp.where(chosen == device * experts + e, share, 0.0), axis=-1, keepdims=True)
@@ -227,15 +327,18 @@
     out[...] = total.astype(BF16)
 
 
-def final_kernel(requests, steps, residual, a, b, c, d, out):
-    mixture = (a[...].astype(F32) + b[...].astype(F32)) + (c[...].astype(F32) + d[...].astype(F32))
-    result = residual[...] + mixture
+def final_kernel(order, requests, steps, residual, a, b, c, d, out):
+    result = residual[...] + sum_chips(order, a, b, c, d)
     for r in range(requests):
         out[r] = result[r * steps : (r + 1) * steps].astype(BF16)
 
 
 def other_chip(x, k, devices):
     return lax.ppermute(x, "tp", [(i, i ^ (2 * k)) for i in range(devices)])
+
+
+def to_chips(parts, devices, order):
+    return [parts[0]] + [other_chip(parts[k], k, devices) for k in order]
 
 
 def other_core(x, devices):
@@ -260,42 +363,63 @@
     chips = devices // 2
     rows = tokens * GROUP
     sibling_weight = other_core(out_weight, devices)
-    (heads,) = call(
-        functools.partial(project_kernel, requests, steps),
-        [((rows, 128), BF16)],
-        [lengths, hidden_states, qkv_weight],
+    copied = [rotated_key_cache, earlier_value_cache, out_weight, expert_ids, combine_weights]
+    heads, limits, inputs, keys, values, own_weight, ids, shares = call(
+        project_kernel,
+        [((rows, 128), BF16), ((requests, 8, 128), jnp.int32), ((tokens, model_width), F32)]
+        + [(x.shape, x.dtype) for x in copied],
+        [lengths, hidden_states, qkv_weight, *copied],
         "project",
-        smem=(0,),
-    )
-    gathered = jnp.stack([heads] + [other_chip(heads, k, devices) for k in range(1, chips)])
+        cost=COST[0],
+        stay=range(8),
+        scratch=[
+            pltpu.SMEM(lengths.shape, jnp.int32),
+            pltpu.VMEM(hidden_states.shape, BF16),
+            pltpu.VMEM(qkv_weight.shape, BF16),
+            pltpu.SemaphoreType.DMA((8,)),
+        ],
+    )
+    gate_up = fetch(gate_up_weight, heads, "fetch_gate_up")
+    (gathered,) = call(
+        functools.partial(gather_kernel, ORDER[0]),
+        [((chips, rows, 128), BF16)],
+        [*to_chips([heads] * chips, devices, ORDER[0]), gate_up],
+        "gather",
+    )
     parts = call(
-        functools.partial(attend_kernel, requests, steps),
+        functools.partial(attend_kernel, steps),
         [((2 * rows, 128), F32)] * (chips + 1),
-        [lengths, gathered, other_core(gathered, devices), rotated_key_cache, earlier_value_cache],
+        [limits, gathered, other_core(gathered, devices), keys, values],
         "attend",
-        scratch=[pltpu.VMEM((devices, rows, 128), BF16), pltpu.VMEM((chips, 2 * rows, 128), F32)],
-        smem=(0,),
+        cost=COST[1],
+        scratch=[
+            pltpu.VMEM((devices, rows, 128), BF16),
+            pltpu.VMEM((chips, 2 * rows, 128), F32),
+        ],
     )
     fresh = parts[chips]
-    arrived = [parts[0]] + [other_chip(parts[k], k, devices) for k in range(1, chips)]
-    (joined,) = call(join_kernel, [((2 * rows, 128), F32)], arrived, "join")
+    down = fetch(down_weight, fresh, "fetch_down")
+    arrived = to_chips(parts[:chips], devices, ORDER[1])
+    (joined,) = call(functools.partial(join_kernel, ORDER[1]), [((2 * rows, 128), F32)], [*arrived, down], "join", cost=COST[2])
     (projected,) = call(
         functools.partial(output_kernel, requests, steps),
-        [((tokens, model_width), F32)],
-        [joined, other_core(joined, devices), fresh, out_weight, sibling_weight],
+        [((tokens, model_width), BF16)],
+        [joined, other_core(joined, devices), fresh, own_weight, sibling_weight],
         "output",
-    )
-    projections = [projected] + [other_chip(projected, k, devices) for k in range(1, chips)]
+        cost=COST[2],
+    )
+    projections = to_chips([projected] * chips, devices, ORDER[2])
     mixture, residual = call(
-        functools.partial(expert_kernel, requests),
+        functools.partial(expert_kernel, ORDER[2]),
         [((tokens, model_width), BF16), ((tokens, model_width), F32)],
-        [hidden_states, *projections, expert_ids, combine_weights, gate_up_weight, down_weight],
+        [inputs, *projections, ids, shares, gate_up, down],
         "experts",
+        cost=COST[3],
     )
     mixture = (mixture.astype(F32) + other_core(mixture, devices).astype(F32)).astype(BF16)
-    mixtures = [mixture] + [other_chip(mixture, k, devices) for k in range(1, chips)]
+    mixtures = to_chips([mixture] * chips, devices, ORDER[3])
     (result,) = call(
-        functools.partial(final_kernel, requests, steps),
+        functools.partial(final_kernel, ORDER[3], requests, steps),
         [(hidden_states.shape, BF16)],
         [residual, *mixtures],
         "final",

time: 57.9 us -> 43.2 us (0.75)
  local copies, waits for them, and re-layouts: 13.9 us -> 0 us
  waiting for transfers between devices: 18 us -> 11.9 us
  Pallas kernels: 6.22 us -> 12 us
    unnamed x24 -> x0, local copies, waits for them, and re-layouts: 13.9 us -> none
    ppermute x12, waiting for transfers between devices: 14.4 us -> 8.3 us  [other_chip(): return lax.ppermute(x, 'tp', [(i, i ^ 2 * k) for i in range(devices)])]
    pallas_call x6 -> x9, Pallas kernels: 6.22 us -> 12 us  [call(): pl.pallas_call(kernel, out_shape=[jax.ShapeDtypeStruct(s, d) if hbm_out e...]
  transfers between devices with their start and end apart: 16 -> 16, of which waited for: 11 -> 11; matrix products, arithmetic and copies ran while one was open for 0% -> 0% of each run, Pallas kernels for 5% -> 21%
where the time goes in v2:
time: 43.2 us; the launch traced here: 43.1 us
  starting transfers between devices  19.1 us (44%)
  Pallas kernels  12 us (28%)
  waiting for transfers between devices  11.9 us (28%)
    ppermute x12, starting transfers between devices, other_chip(): return lax.ppermute(x, 'tp', [(i, i ^ 2 * k) for i in range(devices)])  18.6 us
    pallas_call x9, Pallas kernels, call(): pl.pallas_call(kernel, out_shape=[jax.ShapeDtypeStruct(s, d) if hbm_out e...  12 us
    ppermute x12, waiting for transfers between devices, other_chip(): return lax.ppermute(x, 'tp', [(i, i ^ 2 * k) for i in range(devices)])  8.3 us
    ppermute x4, waiting for transfers between devices, other_core(): return lax.ppermute(x, 'tp', [(i, i ^ 1) for i in range(devices)])  3.59 us
  transfers between devices with their start and end apart: 16, of which 11 were waited for; matrix products, arithmetic and copies ran while one was open for 0% of the time, Pallas kernels for 21%

profile of v2, /device:TPU:0, one launch (start us, length us, event | category | flops | bytes accessed | tf_op | source)
XLA Modules:
  0.0 43.1 jit_solution(991772569074324150)
XLA Ops:
  0.0 0.5 %collective-permute-start.8 = (bf16[128,1024]{1,0:T(8,128)(2,1)}, bf16[128,1024]{1,0:T(8,128)(2,1)S(1)}, u32[]{:S(2)}, u32[]{:S(2)}) collective-permute-start(bf16[128,1024]{1,0:T(8,128)(2,1)} %out_weight_in.1), channel_id=1, source_target_pairs={{0,1},{1,0},{2,3},{3,2},{4,5},{5,4},{6,7},{7,6},{8,9},{9,8},{10,11... | collective-permute-start | bytes 786440 | tf_op jit(solution)/shard_map/ppermute | solution.py:345
  0.5 1.5 %project.1 = (bf16[32,128]{1,0:T(8,128)(2,1)S(1)}, s32[4,8,128]{2,1,0:T(8,128)S(1)}, f32[16,1024]{1,0:T(8,128)S(1)}, bf16[4,128,512]{2,1,0:T(8,128)(2,1)S(1)}, b...) custom-call(s32[4]{0:T(128)} %lengths_in.1, ...), custom_call_target="tpu_custom_call" | custom-call | bytes 8000000 | tf_op jit(solution)/shard_map/project/pallas_call | solution.py:40
  2.0 4.7 %collective-permute-start = (bf16[32,128]{1,0:T(8,128)(2,1)S(1)}, bf16[32,128]{1,0:T(8,128)(2,1)S(1)}, u32[]{:S(2)}, u32[]{:S(2)}) collective-permute-start(bf16[32,128]{1,0:T(8,128)(2,1)S(1)} %get-tuple-element.22.after.a), channel_id=1, source_target_pairs={{0,6},{1,7},{2,4},{3,5},{4,2},{5,3},{6,0},{7,1},{8,14},{9,15},{10,... | collective-permute-start | bytes 24584 | tf_op jit(solution)/shard_map/ppermute | solution.py:337
  6.7 0.0 collective-permute-start.1
  6.7 0.6 %collective-permute-start.2 = (bf16[32,128]{1,0:T(8,128)(2,1)S(1)}, bf16[32,128]{1,0:T(8,128)(2,1)S(1)}, u32[]{:S(2)}, u32[]{:S(2)}) collective-permute-start(bf16[32,128]{1,0:T(8,128)(2,1)S(1)} %get-tuple-element.22.after.a), channel_id=1, source_target_pairs={{0,2},{1,3},{2,0},{3,1},{4,6},{5,7},{6,4},{7,5},{8,10},{9,11},{10,... | collective-permute-start | bytes 24584 | tf_op jit(solution)/shard_map/ppermute | solution.py:337
  7.3 3.5 %fetch_gate_up.1.fetched.gate_up = bf16[4,1024,1024]{2,1,0:T(8,128)(2,1)S(1)} custom-call(bf16[32,128]{1,0:T(8,128)(2,1)S(1)} %get-tuple-element.22.after.a, bf16[4,1024,1024]{2,1,0:T(8,128)(2,1)} %source.2), custom_call_target="tpu_custom_call" | custom-call | bytes 8388608 | tf_op jit(solution)/shard_map/fetch_gate_up/pallas_call | solution.py:40
  10.8 0.0 collective-permute-done.b
  10.8 0.4 collective-permute-done.1.c
  11.2 0.0 collective-permute-done.2.d
  11.2 0.0 collective-permute-start.3
  11.2 1.2 %collective-permute-done.3.sibling = bf16[4,32,128]{2,1,0:T(8,128)(2,1)S(1)} collective-permute-done((bf16[4,32,128]{2,1,0:T(8,128)(2,1)S(1)}, bf16[4,32,128]{2,1,0:T(8,128)(2,1)S(1)}, u32[]{:S(2)}, u32[]{:S(2)}) %collective-permute-start.3) | collective-permute-done | bytes 32800 | tf_op jit(solution)/shard_map/ppermute | solution.py:345
  12.4 1.5 %attend.1 = (f32[64,128]{1,0:T(8,128)S(1)}, f32[64,128]{1,0:T(8,128)S(1)}, f32[64,128]{1,0:T(8,128)S(1)}, f32[64,128]{1,0:T(8,128)S(1)}, f32[64,128]{1,0:T(8,128)S(1)}) custom-call(s32[4,8,128]{2,1,0:T(8,128)S(1)} %get-tuple-element.21.limits, bf16[4,32,128]{2,1,0:T(8,128)(2,1)S(1)} %gather.1.own, bf16[4,32,128]{2,1,0:T(8,128)(2,1)S(1)} %collective-permute-done.3.sibling, ...), custom_call_target="tpu_custom_call" | custom-call | bytes 6000000 | tf_op jit(solution)/shard_map/attend/pallas_call | solution.py:40
  13.9 3.5 %collective-permute-start.4 = (f32[64,128]{1,0:T(8,128)S(1)}, f32[64,128]{1,0:T(8,128)S(1)}, u32[]{:S(2)}, u32[]{:S(2)}) collective-permute-start(f32[64,128]{1,0:T(8,128)S(1)} %get-tuple-element.26), channel_id=1, source_target_pairs={{0,6},{1,7},{2,4},{3,5},{4,2},{5,3},{6,0},{7,1},{8,14},{9,15},{10,... | collective-permute-start | bytes 98312 | tf_op jit(solution)/shard_map/ppermute | solution.py:337
  17.4 0.0 collective-permute-start.5
  17.4 0.9 %collective-permute-start.6 = (f32[64,128]{1,0:T(8,128)S(1)}, f32[64,128]{1,0:T(8,128)S(1)}, u32[]{:S(2)}, u32[]{:S(2)}) collective-permute-start(f32[64,128]{1,0:T(8,128)S(1)} %get-tuple-element.28), channel_id=1, source_target_pairs={{0,2},{1,3},{2,0},{3,1},{4,6},{5,7},{6,4},{7,5},{8,10},{9,11},{10,... | collective-permute-start | bytes 98312 | tf_op jit(solution)/shard_map/ppermute | solution.py:337
  18.4 2.2 %fetch_down.1.fetched.down = bf16[4,512,1024]{2,1,0:T(8,128)(2,1)S(1)} custom-call(f32[64,128]{1,0:T(8,128)S(1)} %get-tuple-element.29.after.fresh, bf16[4,512,1024]{2,1,0:T(8,128)(2,1)} %source.3), custom_call_target="tpu_custom_call" | custom-call | bytes 4194304 | tf_op jit(solution)/shard_map/fetch_down/pallas_call | solution.py:40
  20.6 0.0 collective-permute-done.4.b
  20.6 1.7 %collective-permute-done.5.c = f32[64,128]{1,0:T(8,128)S(1)} collective-permute-done((f32[64,128]{1,0:T(8,128)S(1)}, f32[64,128]{1,0:T(8,128)S(1)}, u32[]{:S(2)}, u32[]{:S(2)}) %collective-permute-start.5) | collective-permute-done | bytes 32800 | tf_op jit(solution)/shard_map/ppermute | solution.py:337
  22.2 0.0 collective-permute-done.6.d
  22.2 0.1 join.1.own
  22.3 0.1 collective-permute-start.7
  22.4 1.2 %collective-permute-done.7.sibling = f32[64,128]{1,0:T(8,128)S(1)} collective-permute-done((f32[64,128]{1,0:T(8,128)S(1)}, f32[64,128]{1,0:T(8,128)S(1)}, u32[]{:S(2)}, u32[]{:S(2)}) %collective-permute-start.7) | collective-permute-done | bytes 32800 | tf_op jit(solution)/shard_map/ppermute | solution.py:345
  23.6 0.0 collective-permute-done.8.sibling_weight
  23.6 0.3 output.1.a
  24.0 2.0 %collective-permute-start.10 = (bf16[16,1024]{1,0:T(8,128)(2,1)S(1)}, bf16[16,1024]{1,0:T(8,128)(2,1)S(1)}, u32[]{:S(2)}, u32[]{:S(2)}) collective-permute-start(bf16[16,1024]{1,0:T(8,128)(2,1)S(1)} %output.1.a), channel_id=1, source_target_pairs={{0,4},{1,5},{2,6},{3,7},{4,0},{5,1},{6,2},{7,3},{8,12},{9,13},{10,... | collective-permute-start | bytes 98312 | tf_op jit(solution)/shard_map/ppermute | solution.py:337
  26.0 0.4 collective-permute-start.11
  26.4 2.0 %collective-permute-start.9 = (bf16[16,1024]{1,0:T(8,128)(2,1)S(1)}, bf16[16,1024]{1,0:T(8,128)(2,1)S(1)}, u32[]{:S(2)}, u32[]{:S(2)}) collective-permute-start(bf16[16,1024]{1,0:T(8,128)(2,1)S(1)} %output.1.a), channel_id=1, source_target_pairs={{0,6},{1,7},{2,4},{3,5},{4,2},{5,3},{6,0},{7,1},{8,14},{9,15},{10,... | collective-permute-start | bytes 98312 | tf_op jit(solution)/shard_map/ppermute | solution.py:337
  28.4 0.5 %collective-permute-done.10.c = bf16[16,1024]{1,0:T(8,128)(2,1)S(1)} collective-permute-done((bf16[16,1024]{1,0:T(8,128)(2,1)S(1)}, bf16[16,1024]{1,0:T(8,128)(2,1)S(1)}, u32[]{:S(2)}, u32[]{:S(2)}) %collective-permute-start.10) | collective-permute-done | bytes 32800 | tf_op jit(solution)/shard_map/ppermute | solution.py:337
  28.8 1.1 %collective-permute-done.11.d = bf16[16,1024]{1,0:T(8,128)(2,1)S(1)} collective-permute-done((bf16[16,1024]{1,0:T(8,128)(2,1)S(1)}, bf16[16,1024]{1,0:T(8,128)(2,1)S(1)}, u32[]{:S(2)}, u32[]{:S(2)}) %collective-permute-start.11) | collective-permute-done | bytes 32800 | tf_op jit(solution)/shard_map/ppermute | solution.py:337
  29.9 2.2 %collective-permute-done.9.b = bf16[16,1024]{1,0:T(8,128)(2,1)S(1)} collective-permute-done((bf16[16,1024]{1,0:T(8,128)(2,1)S(1)}, bf16[16,1024]{1,0:T(8,128)(2,1)S(1)}, u32[]{:S(2)}, u32[]{:S(2)}) %collective-permute-start.9) | collective-permute-done | bytes 32800 | tf_op jit(solution)/shard_map/ppermute | solution.py:337
  32.1 2.2 %experts.1 = (bf16[16,1024]{1,0:T(8,128)(2,1)S(1)}, f32[16,1024]{1,0:T(8,128)S(1)}) custom-call(f32[16,1024]{1,0:T(8,128)S(1)} %get-tuple-element.20.inputs, bf16[16,1024]{1,0:T(8,128)(2,1)S(1)} %output.1.a, bf16[16,1024]{1,0:T(8,128)(2,1)S(1)} %collective-permute-done.9.b, bf16[16,1024]{1,0:T(8,128)(2,1)S(1)} %collective-permute-done.10.c, ...), custom_call_target="tpu_custom_call" | custom-call | bytes 12000000 | tf_op jit(solution)/shard_map/experts/pallas_call | solution.py:40
  34.2 0.0 collective-permute-start.12
  34.2 1.2 %collective-permute-done.12 = bf16[16,1024]{1,0:T(8,128)(2,1)S(1)} collective-permute-done((bf16[16,1024]{1,0:T(8,128)(2,1)S(1)}, bf16[16,1024]{1,0:T(8,128)(2,1)S(1)}, u32[]{:S(2)}, u32[]{:S(2)}) %collective-permute-start.12) | collective-permute-done | bytes 32800 | tf_op jit(solution)/shard_map/ppermute | solution.py:345
  35.5 2.1 %collective-permute-start.13 = (bf16[16,1024]{1,0:T(8,128)(2,1)S(1)}, bf16[16,1024]{1,0:T(8,128)(2,1)S(1)}, u32[]{:S(2)}, u32[]{:S(2)}) collective-permute-start(bf16[16,1024]{1,0:T(8,128)(2,1)S(1)} %add_convert_fusion.a), channel_id=1, source_target_pairs={{0,6},{1,7},{2,4},{3,5},{4,2},{5,3},{6,0},{7,1},{8,14},{9,15},{10,... | collective-permute-start | bytes 98312 | tf_op jit(solution)/shard_map/ppermute | solution.py:337
  37.5 0.0 collective-permute-start.14
  37.5 2.4 %collective-permute-start.15 = (bf16[16,1024]{1,0:T(8,128)(2,1)S(1)}, bf16[16,1024]{1,0:T(8,128)(2,1)S(1)}, u32[]{:S(2)}, u32[]{:S(2)}) collective-permute-start(bf16[16,1024]{1,0:T(8,128)(2,1)S(1)} %add_convert_fusion.a), channel_id=1, source_target_pairs={{0,2},{1,3},{2,0},{3,1},{4,6},{5,7},{6,4},{7,5},{8,10},{9,11},{10,... | collective-permute-start | bytes 98312 | tf_op jit(solution)/shard_map/ppermute | solution.py:337
  39.9 1.4 %collective-permute-done.13.b = bf16[16,1024]{1,0:T(8,128)(2,1)S(1)} collective-permute-done((bf16[16,1024]{1,0:T(8,128)(2,1)S(1)}, bf16[16,1024]{1,0:T(8,128)(2,1)S(1)}, u32[]{:S(2)}, u32[]{:S(2)}) %collective-permute-start.13) | collective-permute-done | bytes 32800 | tf_op jit(solution)/shard_map/ppermute | solution.py:337
  41.3 1.1 %collective-permute-done.14.c = bf16[16,1024]{1,0:T(8,128)(2,1)S(1)} collective-permute-done((bf16[16,1024]{1,0:T(8,128)(2,1)S(1)}, bf16[16,1024]{1,0:T(8,128)(2,1)S(1)}, u32[]{:S(2)}, u32[]{:S(2)}) %collective-permute-start.14) | collective-permute-done | bytes 32800 | tf_op jit(solution)/shard_map/ppermute | solution.py:337
  42.4 0.1 collective-permute-done.15.d
  42.5 0.6 %final.1 = bf16[4,4,1024]{2,1,0:T(4,128)(2,1)} custom-call(f32[16,1024]{1,0:T(8,128)S(1)} %get-tuple-element.33.residual, bf16[16,1024]{1,0:T(8,128)(2,1)S(1)} %add_convert_fusion.a, bf16[16,1024]{1,0:T(8,128)(2,1)S(1)} %collective-permute-done.13.b, bf16[16,1024]{1,0:T(8,128)(2,1)S(1)} %collective-permute-done.14.c, ...), custom_call_target="tpu_custom_call" | custom-call | tf_op jit(solution)/shard_map/final/pallas_call | solution.py:40
  (2 shorter events, 0.0 us)
Async XLA Ops:
  0.0 23.6 %collective-permute-start.8 = (bf16[128,1024]{1,0:T(8,128)(2,1)}, bf16[128,1024]{1,0:T(8,128)(2,1)S(1)}, u32[]{:S(2)}, u32[]{:S(2)}) collective-permute-start(bf16[128,1024]{1,0:T(8,128)(2,1)} %out_weight_in.1), channel_id=1, source_target_pairs={{0,1},{1,0},{2,3},{3,2},{4,5},{5,4},{6,7},{7,6},{8,9},{9,8},{10,11... | collective-permute-start | bytes 786440 | tf_op jit(solution)/shard_map/ppermute | solution.py:345
  2.0 8.8 %collective-permute-start = (bf16[32,128]{1,0:T(8,128)(2,1)S(1)}, bf16[32,128]{1,0:T(8,128)(2,1)S(1)}, u32[]{:S(2)}, u32[]{:S(2)}) collective-permute-start(bf16[32,128]{1,0:T(8,128)(2,1)S(1)} %get-tuple-element.22.after.a), channel_id=1, source_target_pairs={{0,6},{1,7},{2,4},{3,5},{4,2},{5,3},{6,0},{7,1},{8,14},{9,15},{10,... | collective-permute-start | bytes 24584 | tf_op jit(solution)/shard_map/ppermute | solution.py:337
  6.7 4.5 %collective-permute-start.1 = (bf16[32,128]{1,0:T(8,128)(2,1)S(1)}, bf16[32,128]{1,0:T(8,128)(2,1)S(1)}, u32[]{:S(2)}, u32[]{:S(2)}) collective-permute-start(bf16[32,128]{1,0:T(8,128)(2,1)S(1)} %get-tuple-element.22.after.a), channel_id=1, source_target_pairs={{0,4},{1,5},{2,6},{3,7},{4,0},{5,1},{6,2},{7,3},{8,12},{9,13},{10,... | collective-permute-start | bytes 24584 | tf_op jit(solution)/shard_map/ppermute | solution.py:337
  6.7 4.5 %collective-permute-start.2 = (bf16[32,128]{1,0:T(8,128)(2,1)S(1)}, bf16[32,128]{1,0:T(8,128)(2,1)S(1)}, u32[]{:S(2)}, u32[]{:S(2)}) collective-permute-start(bf16[32,128]{1,0:T(8,128)(2,1)S(1)} %get-tuple-element.22.after.a), channel_id=1, source_target_pairs={{0,2},{1,3},{2,0},{3,1},{4,6},{5,7},{6,4},{7,5},{8,10},{9,11},{10,... | collective-permute-start | bytes 24584 | tf_op jit(solution)/shard_map/ppermute | solution.py:337
  11.2 1.2 %collective-permute-start.3 = (bf16[4,32,128]{2,1,0:T(8,128)(2,1)S(1)}, bf16[4,32,128]{2,1,0:T(8,128)(2,1)S(1)}, u32[]{:S(2)}, u32[]{:S(2)}) collective-permute-start(bf16[4,32,128]{2,1,0:T(8,128)(2,1)S(1)} %gather.1.own), channel_id=1, source_target_pairs={{0,1},{1,0},{2,3},{3,2},{4,5},{5,4},{6,7},{7,6},{8,9},{9,8},{10,11... | collective-permute-start | bytes 98312 | tf_op jit(solution)/shard_map/ppermute | solution.py:345
  13.9 6.7 %collective-permute-start.4 = (f32[64,128]{1,0:T(8,128)S(1)}, f32[64,128]{1,0:T(8,128)S(1)}, u32[]{:S(2)}, u32[]{:S(2)}) collective-permute-start(f32[64,128]{1,0:T(8,128)S(1)} %get-tuple-element.26), channel_id=1, source_target_pairs={{0,6},{1,7},{2,4},{3,5},{4,2},{5,3},{6,0},{7,1},{8,14},{9,15},{10,... | collective-permute-start | bytes 98312 | tf_op jit(solution)/shard_map/ppermute | solution.py:337
  17.4 4.8 %collective-permute-start.5 = (f32[64,128]{1,0:T(8,128)S(1)}, f32[64,128]{1,0:T(8,128)S(1)}, u32[]{:S(2)}, u32[]{:S(2)}) collective-permute-start(f32[64,128]{1,0:T(8,128)S(1)} %get-tuple-element.27), channel_id=1, source_target_pairs={{0,4},{1,5},{2,6},{3,7},{4,0},{5,1},{6,2},{7,3},{8,12},{9,13},{10,... | collective-permute-start | bytes 98312 | tf_op jit(solution)/shard_map/ppermute | solution.py:337
  17.4 4.8 %collective-permute-start.6 = (f32[64,128]{1,0:T(8,128)S(1)}, f32[64,128]{1,0:T(8,128)S(1)}, u32[]{:S(2)}, u32[]{:S(2)}) collective-permute-start(f32[64,128]{1,0:T(8,128)S(1)} %get-tuple-element.28), channel_id=1, source_target_pairs={{0,2},{1,3},{2,0},{3,1},{4,6},{5,7},{6,4},{7,5},{8,10},{9,11},{10,... | collective-permute-start | bytes 98312 | tf_op jit(solution)/shard_map/ppermute | solution.py:337
  22.3 1.3 %collective-permute-start.7 = (f32[64,128]{1,0:T(8,128)S(1)}, f32[64,128]{1,0:T(8,128)S(1)}, u32[]{:S(2)}, u32[]{:S(2)}) collective-permute-start(f32[64,128]{1,0:T(8,128)S(1)} %join.1.own), channel_id=1, source_target_pairs={{0,1},{1,0},{2,3},{3,2},{4,5},{5,4},{6,7},{7,6},{8,9},{9,8},{10,11... | collective-permute-start | bytes 98312 | tf_op jit(solution)/shard_map/ppermute | solution.py:345
  24.0 4.9 %collective-permute-start.10 = (bf16[16,1024]{1,0:T(8,128)(2,1)S(1)}, bf16[16,1024]{1,0:T(8,128)(2,1)S(1)}, u32[]{:S(2)}, u32[]{:S(2)}) collective-permute-start(bf16[16,1024]{1,0:T(8,128)(2,1)S(1)} %output.1.a), channel_id=1, source_target_pairs={{0,4},{1,5},{2,6},{3,7},{4,0},{5,1},{6,2},{7,3},{8,12},{9,13},{10,... | collective-permute-start | bytes 98312 | tf_op jit(solution)/shard_map/ppermute | solution.py:337
  26.0 3.9 %collective-permute-start.11 = (bf16[16,1024]{1,0:T(8,128)(2,1)S(1)}, bf16[16,1024]{1,0:T(8,128)(2,1)S(1)}, u32[]{:S(2)}, u32[]{:S(2)}) collective-permute-start(bf16[16,1024]{1,0:T(8,128)(2,1)S(1)} %output.1.a), channel_id=1, source_target_pairs={{0,2},{1,3},{2,0},{3,1},{4,6},{5,7},{6,4},{7,5},{8,10},{9,11},{10,... | collective-permute-start | bytes 98312 | tf_op jit(solution)/shard_map/ppermute | solution.py:337
  26.4 5.7 %collective-permute-start.9 = (bf16[16,1024]{1,0:T(8,128)(2,1)S(1)}, bf16[16,1024]{1,0:T(8,128)(2,1)S(1)}, u32[]{:S(2)}, u32[]{:S(2)}) collective-permute-start(bf16[16,1024]{1,0:T(8,128)(2,1)S(1)} %output.1.a), channel_id=1, source_target_pairs={{0,6},{1,7},{2,4},{3,5},{4,2},{5,3},{6,0},{7,1},{8,14},{9,15},{10,... | collective-permute-start | bytes 98312 | tf_op jit(solution)/shard_map/ppermute | solution.py:337
  34.2 1.2 %collective-permute-start.12 = (bf16[16,1024]{1,0:T(8,128)(2,1)S(1)}, bf16[16,1024]{1,0:T(8,128)(2,1)S(1)}, u32[]{:S(2)}, u32[]{:S(2)}) collective-permute-start(bf16[16,1024]{1,0:T(8,128)(2,1)S(1)} %get-tuple-element.34), channel_id=1, source_target_pairs={{0,1},{1,0},{2,3},{3,2},{4,5},{5,4},{6,7},{7,6},{8,9},{9,8},{10,11... | collective-permute-start | bytes 98312 | tf_op jit(solution)/shard_map/ppermute | solution.py:345
  35.5 5.8 %collective-permute-start.13 = (bf16[16,1024]{1,0:T(8,128)(2,1)S(1)}, bf16[16,1024]{1,0:T(8,128)(2,1)S(1)}, u32[]{:S(2)}, u32[]{:S(2)}) collective-permute-start(bf16[16,1024]{1,0:T(8,128)(2,1)S(1)} %add_convert_fusion.a), channel_id=1, source_target_pairs={{0,6},{1,7},{2,4},{3,5},{4,2},{5,3},{6,0},{7,1},{8,14},{9,15},{10,... | collective-permute-start | bytes 98312 | tf_op jit(solution)/shard_map/ppermute | solution.py:337
  37.5 4.9 %collective-permute-start.14 = (bf16[16,1024]{1,0:T(8,128)(2,1)S(1)}, bf16[16,1024]{1,0:T(8,128)(2,1)S(1)}, u32[]{:S(2)}, u32[]{:S(2)}) collective-permute-start(bf16[16,1024]{1,0:T(8,128)(2,1)S(1)} %add_convert_fusion.a), channel_id=1, source_target_pairs={{0,4},{1,5},{2,6},{3,7},{4,0},{5,1},{6,2},{7,3},{8,12},{9,13},{10,... | collective-permute-start | bytes 98312 | tf_op jit(solution)/shard_map/ppermute | solution.py:337
  37.5 4.9 %collective-permute-start.15 = (bf16[16,1024]{1,0:T(8,128)(2,1)S(1)}, bf16[16,1024]{1,0:T(8,128)(2,1)S(1)}, u32[]{:S(2)}, u32[]{:S(2)}) collective-permute-start(bf16[16,1024]{1,0:T(8,128)(2,1)S(1)} %add_convert_fusion.a), channel_id=1, source_target_pairs={{0,2},{1,3},{2,0},{3,1},{4,6},{5,7},{6,4},{7,5},{8,10},{9,11},{10,... | collective-permute-start | bytes 98312 | tf_op jit(solution)/shard_map/ppermute | solution.py:337

commit v3 on v2

--- a/solution.py
+++ b/solution.py
@@ -17,7 +17,8 @@
 F32 = jnp.float32
 BF16 = jnp.bfloat16
 VMEM_LIMIT = 16 * 1024 * 1024
-ORDER = ((3, 2, 1),) * 4
+SPLIT = (1, 3)
+ORDER = ((1, 2, 3), (3, 2, 1), (1, 2, 3), (1, 2, 3))
 COST = (8_000_000, 6_000_000, 1_000_000, 12_000_000)
 
 
@@ -64,19 +65,9 @@
     lengths_in,
     hidden_in,
     weight_in,
-    keys_in,
-    values_in,
-    out_weight_in,
-    ids_in,
-    shares_in,
     out,
     limits,
     inputs,
-    keys,
-    values,
-    out_weight,
-    ids,
-    shares,
     lengths,
     hidden,
     weight,
@@ -87,11 +78,6 @@
             (lengths_in, lengths),
             (hidden_in, hidden),
             (weight_in, weight),
-            (keys_in, keys),
-            (values_in, values),
-            (out_weight_in, out_weight),
-            (ids_in, ids),
-            (shares_in, shares),
         ],
         semaphores,
     )
@@ -136,26 +122,36 @@
     query = merge_rows(rows)
     plain = merge_rows([a, b])
     out[...] = jnp.where(device < devices // 2, query, plain).astype(BF16)
-    for copy in copies[3:]:
+
+
+def fetch_kernel(pieces, beside, operands, *refs):
+    count = len(pieces)
+    inputs, sources = refs[:operands], refs[operands : operands + count]
+    outs, semaphores = refs[operands + count : -1], refs[-1]
+    targets = outs[:count]
+    pairs = [
+        (source.at[first + i], target.at[i])
+        for source, target, (first, size) in zip(sources, targets, pieces)
+        for i in range(size)
+    ]
+    copies = start_all(pairs, semaphores)
+    if beside is not None:
+        beside(*inputs, *outs[count:])
+    for copy in copies:
         copy.wait()
 
 
-def fetch_kernel(after, source, target, semaphores):
-    for copy in start_all([(source.at[i], target.at[i]) for i in range(target.shape[0])], semaphores):
-        copy.wait()
-
-
-def fetch(x, after, name):
-    (there,) = call(
-        fetch_kernel,
-        [(x.shape, x.dtype)],
-        [after, x],
+def fetch(pieces, after, name, beside=None, outs=()):
+    rows = [(first, size) for _, first, size in pieces]
+    return call(
+        functools.partial(fetch_kernel, rows, beside, len(after)),
+        [((size,) + x.shape[1:], x.dtype) for x, _, size in pieces] + list(outs),
+        [*after] + [x for x, _, _ in pieces],
         name,
-        stay=(1,),
-        scratch=[pltpu.SemaphoreType.DMA((x.shape[0],))],
-        cost=x.size * 2,
-    )
-    return there
+        stay=range(len(after), len(after) + len(pieces)),
+        scratch=[pltpu.SemaphoreType.DMA((sum(size for _, size in rows),))],
+        cost=sum(x.size * 2 // x.shape[0] * size for x, _, size in pieces),
+    )
 
 
 def fold(x, rows, lanes):
@@ -187,69 +183,84 @@
     )
 
 
-def soft(scores, live, values):
+def soft(scores, live):
     masked = jnp.where(live, scores, NEGATIVE)
     peak = jnp.max(masked, axis=-1, keepdims=True)
     weights = jnp.where(live, jnp.exp(masked - peak), 0.0)
-    total = jnp.sum(weights, axis=-1, keepdims=True)
-    return peak, total, jnp.dot(weights.astype(BF16), values, preferred_element_type=F32)
-
-
-def attend_kernel(
-    steps,
-    limits,
-    own,
-    sibling,
-    keys,
-    values,
-    out0,
-    out1,
-    out2,
-    out3,
-    fresh,
-    heads,
-    blocks,
-):
-    requests = keys.shape[0]
+    return peak, weights.astype(BF16), jnp.sum(weights, axis=-1, keepdims=True)
+
+
+def attend_blocks(steps, limits, heads, core, keys, values, store):
+    device = lax.axis_index("tp")
+    requests, count, _ = keys.shape
+    rows = steps * GROUP
+    scale = HEAD_DIMENSION**-0.5
+    pairs = [(s, r) for s in range(2) for r in range(requests)]
+    columns = [pl.ds(pl.multiple_of((2 * s + core) * 128, 128), 128) for s in range(2)]
+    scores = []
+    for s, r in pairs:
+        q = spread(heads[s, r * rows : (r + 1) * rows].astype(F32) * scale, GROUP)
+        scores.append(
+            lax.dot_general(q, keys[r, :, columns[s]], (((1,), (1,)), ((), ())), preferred_element_type=F32)
+        )
+    scores = merge_rows(scores)
+    position = device * count + iota(scores.shape, 1)
+    limit = merge_rows([limits[r, 0:rows] for _, r in pairs for _ in range(GROUP)])
+    peak, weights, total = soft(scores, position < limit)
+    n = GROUP * rows
+    for i, (s, r) in enumerate(pairs):
+        own = slice(i * n, (i + 1) * n)
+        summed = jnp.dot(weights[own], values[r, :, columns[s]], preferred_element_type=F32)
+        store(s, r * rows, fold(summed, rows, 128))
+        store(s, (requests + r) * rows, pack_stats(fold(peak[own], rows, 128), fold(total[own], rows, 128)))
+
+
+def attend_own_kernel(steps, limits, own, keys, values, out):
+    core = lax.axis_index("tp") % 2
+
+    def store(s, row, x):
+        out[s, row : row + x.shape[0], :] = x
+
+    attend_blocks(steps, limits, own, core, keys, values, store)
+
+
+def attend_sibling_kernel(steps, limits, sibling, keys, values, blocks_own, out0, out1, out2, out3, blocks):
     device = lax.axis_index("tp")
     chip, core = device // 2, device % 2
-    chips = own.shape[0]
-    for k in range(chips):
-        heads[2 * (chip ^ k) + core] = own[k]
-        heads[2 * (chip ^ k) + 1 - core] = sibling[k]
+
+    def store(s, row, x):
+        blocks[2 * s + 1 - core, row : row + x.shape[0], :] = x
+
+    for s in range(2):
+        blocks[2 * s + core] = blocks_own[s]
+    attend_blocks(steps, limits, sibling, 1 - core, keys, values, store)
+    out0[...] = blocks[chip]
+    for k, out in ((1, out1), (2, out2), (3, out3)):
+        out[...] = blocks[partner(chip, k)]
+
+
+def fresh_part(requests, steps, own, sibling, after, out):
+    device = lax.axis_index("tp")
+    chip, core = device // 2, device % 2
     rows = steps * GROUP
-    count = keys.shape[1]
-    scale = HEAD_DIMENSION**-0.5
-    query = jnp.concatenate([heads[t].astype(F32) for t in range(chips)], axis=1) * scale
-    lanes = query.shape[1]
-    groups = lanes // HEAD_DIMENSION
-    position = device * count + iota((groups * rows, count), 1)
-    for r in range(requests):
-        q = spread(query[r * rows : (r + 1) * rows], groups)
-        scores = lax.dot_general(q, keys[r], (((1,), (1,)), ((), ())), preferred_element_type=F32)
-        peak, total, summed = soft(scores, position < limits[r, 0:1], values[r])
-        summed = fold(summed, rows, lanes)
-        stats = pack_stats(fold(peak, rows, lanes), fold(total, rows, lanes))
-        for k in range(chips):
-            blocks[k, r * rows : (r + 1) * rows, :] = summed[:, k * 128 : (k + 1) * 128]
-            blocks[k, (requests + r) * rows : (requests + r + 1) * rows, :] = stats[:, k * 128 : (k + 1) * 128]
-    for k, out in enumerate((out0, out1, out2, out3)):
-        out[...] = blocks[chip ^ k]
     tokens = requests * steps
-    place = chips + chip // 2
-    second = chip % 2 == 1
-    pick = lambda x: jnp.where(second, x[tokens:].astype(F32), x[:tokens].astype(F32)).astype(BF16)
-    new_keys = pick(heads[place])
-    new_values = pick(heads[place + chips // 2])
-    q = spread(heads[chip].astype(F32) * scale, 2)
+    n = requests * rows
+
+    def held(s, at_core):
+        return jnp.where(core == at_core, own[s].astype(F32), sibling[s].astype(F32))
+
+    def pick(x):
+        return jnp.where(chip % 2 == 1, x[tokens:], x[:tokens]).astype(BF16)
+
+    new_keys, new_values = pick(held(2, chip // 2)), pick(held(3, chip // 2))
+    q = spread(held(chip // 2, chip % 2) * HEAD_DIMENSION**-0.5, GROUP)
     scores = lax.dot_general(q, new_keys, (((1,), (1,)), ((), ())), preferred_element_type=F32)
-    shape = scores.shape
-    row, column = iota(shape, 0) % (requests * rows), iota(shape, 1)
+    row, column = iota(scores.shape, 0) % n, iota(scores.shape, 1)
     live = (row // rows == column // steps) & (column % steps <= row % steps)
-    peak, total, summed = soft(scores, live, new_values)
-    n = requests * rows
-    fresh[0:n] = fold(summed, n, 128)
-    fresh[n : 2 * n] = pack_stats(fold(peak, n, 128), fold(total, n, 128))
+    peak, weights, total = soft(scores, live)
+    summed = jnp.dot(weights, new_values, preferred_element_type=F32)
+    out[0:n] = fold(summed, n, 128)
+    out[n : 2 * n] = pack_stats(fold(peak, n, 128), fold(total, n, 128))
 
 
 def join(a, b):
@@ -265,7 +276,7 @@
 
 def join_kernel(order, a, b, c, d, fetched, out):
     a, b, c, d = sort_chips(order, a, (b, c, d))
-    peak, total, summed = join(join(read_part(a), read_part(b)), join(read_part(c), read_part(d)))
+    peak, total, summed = join(join(read_part(a), read_part(d)), join(read_part(b), read_part(c)))
     n = summed.shape[0]
     out[0:n] = summed
     out[n:] = pack_stats(peak, total)
@@ -295,16 +306,20 @@
 
 
 def gather_kernel(order, a, b, c, d, fetched, out):
-    for k, x in enumerate(sort_chips(order, a, (b, c, d))):
-        out[k] = x[...]
+    chip = lax.axis_index("tp") // 2
+    own, *others = sort_chips(order, a, (b, c, d))
+    out[chip] = own[...]
+    for back, x in zip((2, 1, 3), others):
+        out[partner(chip, back)] = x[...]
 
 
 def sum_chips(order, a, b, c, d):
     a, b, c, d = sort_chips(order, a, (b, c, d))
-    return (a[...].astype(F32) + b[...].astype(F32)) + (c[...].astype(F32) + d[...].astype(F32))
-
-
-def expert_kernel(order, inputs, a, b, c, d, ids, shares, gate_up, down, out, residual_out):
+    return (a[...].astype(F32) + d[...].astype(F32)) + (b[...].astype(F32) + c[...].astype(F32))
+
+
+def expert_kernel(order, inputs, a, b, c, d, ids, shares, down, *refs):
+    *gate_up, out, residual_out = refs
     device = lax.axis_index("tp")
     residual = inputs[...] + sum_chips(order, a, b, c, d)
     residual_out[...] = residual
@@ -314,10 +329,11 @@
     requests = ids.shape[0]
     chosen = merge_rows([ids[r] for r in range(requests)])
     share = merge_rows([shares[r].astype(F32) for r in range(requests)]) * (1.0 / 65536.0)
-    experts = gate_up.shape[0]
+    gate_up = [ref.at[i] for ref in gate_up for i in range(ref.shape[0])]
+    experts = len(gate_up)
     total = None
     for e in range(experts):
-        united = jnp.dot(normed, gate_up[e], preferred_element_type=F32)
+        united = jnp.dot(normed, gate_up[e][...], preferred_element_type=F32)
         width = united.shape[1] // 2
         gate, up = united[:, :width], united[:, width:]
         active = (gate / (1.0 + jnp.exp(-gate)) * up).astype(BF16)
@@ -333,8 +349,16 @@
         out[r] = result[r * steps : (r + 1) * steps].astype(BF16)
 
 
+def partner(chip, k):
+    outer = (chip == 0) | (chip == 3)
+    if k == 3:
+        return chip ^ 3
+    return jnp.where(outer, chip ^ k, chip ^ (3 - k))
+
+
 def other_chip(x, k, devices):
-    return lax.ppermute(x, "tp", [(i, i ^ (2 * k)) for i in range(devices)])
+    to = {1: (1, 3, 0, 2), 2: (2, 0, 3, 1), 3: (3, 2, 1, 0)}[k]
+    return lax.ppermute(x, "tp", [(i, 2 * to[i // 2] + i % 2) for i in range(devices)])
 
 
 def to_chips(parts, devices, order):
@@ -363,56 +387,70 @@
     chips = devices // 2
     rows = tokens * GROUP
     sibling_weight = other_core(out_weight, devices)
-    copied = [rotated_key_cache, earlier_value_cache, out_weight, expert_ids, combine_weights]
-    heads, limits, inputs, keys, values, own_weight, ids, shares = call(
+    heads, limits, inputs = call(
         project_kernel,
-        [((rows, 128), BF16), ((requests, 8, 128), jnp.int32), ((tokens, model_width), F32)]
-        + [(x.shape, x.dtype) for x in copied],
-        [lengths, hidden_states, qkv_weight, *copied],
+        [((rows, 128), BF16), ((requests, 8, 128), jnp.int32), ((tokens, model_width), F32)],
+        [lengths, hidden_states, qkv_weight],
         "project",
         cost=COST[0],
-        stay=range(8),
+        stay=range(3),
         scratch=[
             pltpu.SMEM(lengths.shape, jnp.int32),
             pltpu.VMEM(hidden_states.shape, BF16),
             pltpu.VMEM(qkv_weight.shape, BF16),
-            pltpu.SemaphoreType.DMA((8,)),
+            pltpu.SemaphoreType.DMA((3,)),
         ],
     )
-    gate_up = fetch(gate_up_weight, heads, "fetch_gate_up")
+    caches = [(rotated_key_cache, 0, requests), (earlier_value_cache, 0, requests)]
+    small = [(x[None], 0, 1) for x in (out_weight, expert_ids, combine_weights)]
+    experts = gate_up_weight.shape[0]
+    cuts = [(0, SPLIT[0]), (SPLIT[0], SPLIT[1] - SPLIT[0]), (SPLIT[1], experts - SPLIT[1])]
+    gate_up = [[(gate_up_weight, *cut)] if cut[1] else [] for cut in cuts]
+    keys, values, own_weight, ids, shares, *gate_up_a = fetch(caches + small + gate_up[0], [heads], "fetch_cache")
     (gathered,) = call(
         functools.partial(gather_kernel, ORDER[0]),
         [((chips, rows, 128), BF16)],
-        [*to_chips([heads] * chips, devices, ORDER[0]), gate_up],
+        [*to_chips([heads] * chips, devices, ORDER[0]), keys],
         "gather",
     )
+    sibling = other_core(gathered, devices)
+    (blocks_own,) = call(
+        functools.partial(attend_own_kernel, steps),
+        [((chips // 2, 2 * rows, 128), F32)],
+        [limits, gathered, keys, values],
+        "attend_own",
+        cost=COST[1],
+    )
     parts = call(
-        functools.partial(attend_kernel, steps),
-        [((2 * rows, 128), F32)] * (chips + 1),
-        [limits, gathered, other_core(gathered, devices), keys, values],
+        functools.partial(attend_sibling_kernel, steps),
+        [((2 * rows, 128), F32)] * chips,
+        [limits, sibling, keys, values, blocks_own],
         "attend",
         cost=COST[1],
-        scratch=[
-            pltpu.VMEM((devices, rows, 128), BF16),
-            pltpu.VMEM((chips, 2 * rows, 128), F32),
-        ],
-    )
-    fresh = parts[chips]
-    down = fetch(down_weight, fresh, "fetch_down")
+        scratch=[pltpu.VMEM((chips, 2 * rows, 128), F32)],
+    )
+    *gate_up_b, fresh = fetch(
+        gate_up[1],
+        [gathered, sibling, parts[0]],
+        "fetch_b",
+        beside=functools.partial(fresh_part, requests, steps),
+        outs=[((2 * rows, 128), F32)],
+    )
     arrived = to_chips(parts[:chips], devices, ORDER[1])
-    (joined,) = call(functools.partial(join_kernel, ORDER[1]), [((2 * rows, 128), F32)], [*arrived, down], "join", cost=COST[2])
+    (joined,) = call(functools.partial(join_kernel, ORDER[1]), [((2 * rows, 128), F32)], [*arrived, gate_up_b[0]], "join", cost=COST[2])
     (projected,) = call(
         functools.partial(output_kernel, requests, steps),
         [((tokens, model_width), BF16)],
-        [joined, other_core(joined, devices), fresh, own_weight, sibling_weight],
+        [joined, other_core(joined, devices), fresh, own_weight[0], sibling_weight],
         "output",
         cost=COST[2],
     )
     projections = to_chips([projected] * chips, devices, ORDER[2])
+    *gate_up_c, down = fetch(gate_up[2] + [(down_weight, 0, experts)], [projected], "fetch_c")
     mixture, residual = call(
         functools.partial(expert_kernel, ORDER[2]),
         [((tokens, model_width), BF16), ((tokens, model_width), F32)],
-        [inputs, *projections, ids, shares, gate_up, down],
+        [inputs, *projections, ids[0], shares[0], down, *gate_up_a, *gate_up_b, *gate_up_c],
         "experts",
         cost=COST[3],
     )

time: 43.2 us -> 40 us (0.926)
  waiting for transfers between devices: 11.9 us -> 7.99 us
  Pallas kernels: 12 us -> 12.9 us
    ppermute x12, waiting for transfers between devices: 8.3 us -> 4.85 us  [other_chip(): lax.ppermute(x, 'tp', [(i, 2 * to[i // 2] + i % 2) for i in range(devices)])]
    pallas_call x9 -> x11, Pallas kernels: 12 us -> 12.9 us  [call(): pl.pallas_call(kernel, out_shape=[jax.ShapeDtypeStruct(s, d) if hbm_out e...]
    ppermute x4, waiting for transfers between devices: 3.59 us -> 3.14 us  [other_core(): return lax.ppermute(x, 'tp', [(i, i ^ 1) for i in range(devices)])]
  transfers between devices with their start and end apart: 16 -> 16, of which waited for: 11 -> 9; matrix products, arithmetic and copies ran while one was open for 0% -> 0% of each run, Pallas kernels for 21% -> 25%
where the time goes in v3:
time: 40 us; the launch traced here: 39.9 us
  starting transfers between devices  18.8 us (47%)
  Pallas kernels  12.9 us (32%)
  waiting for transfers between devices  7.99 us (20%)
    ppermute x12, starting transfers between devices, other_chip(): lax.ppermute(x, 'tp', [(i, 2 * to[i // 2] + i % 2) for i in range(devices)])  18.3 us
    pallas_call x11, Pallas kernels, call(): pl.pallas_call(kernel, out_shape=[jax.ShapeDtypeStruct(s, d) if hbm_out e...  12.9 us
    ppermute x12, waiting for transfers between devices, other_chip(): lax.ppermute(x, 'tp', [(i, 2 * to[i // 2] + i % 2) for i in range(devices)])  4.85 us
    ppermute x4, waiting for transfers between devices, other_core(): return lax.ppermute(x, 'tp', [(i, i ^ 1) for i in range(devices)])  3.14 us
  transfers between devices with their start and end apart: 16, of which 9 were waited for; matrix products, arithmetic and copies ran while one was open for 0% of the time, Pallas kernels for 25%

profile of v3, /device:TPU:0, one launch (start us, length us, event | category | flops | bytes accessed | tf_op | source)
XLA Modules:
  0.0 39.9 jit_solution(14562126486805502968)
XLA Ops:
  0.0 0.5 %collective-permute-start.8 = (bf16[128,1024]{1,0:T(8,128)(2,1)}, bf16[128,1024]{1,0:T(8,128)(2,1)S(1)}, u32[]{:S(2)}, u32[]{:S(2)}) collective-permute-start(bf16[128,1024]{1,0:T(8,128)(2,1)} %param.15), channel_id=1, source_target_pairs={{0,1},{1,0},{2,3},{3,2},{4,5},{5,4},{6,7},{7,6},{8,9},{9,8},{10,11... | collective-permute-start | bytes 786440 | tf_op jit(solution)/shard_map/ppermute | solution.py:369
  0.5 1.5 %project.1 = (bf16[32,128]{1,0:T(8,128)(2,1)S(1)}, s32[4,8,128]{2,1,0:T(8,128)S(1)}, f32[16,1024]{1,0:T(8,128)S(1)}) custom-call(s32[4]{0:T(128)} %lengths_in.1, bf16[4,4,1024]{2,1,0:T(4,128)(2,1)} %hidden_in.1, bf16[256,1024]{1,0:T(8,128)(2,1)} %weight_in.1), custom_call_target="tpu_custom_call" | custom-call | bytes 8000000 | tf_op jit(solution)/shard_map/project/pallas_call | solution.py:41
  2.0 4.7 %collective-permute-start.2 = (bf16[32,128]{1,0:T(8,128)(2,1)S(1)}, bf16[32,128]{1,0:T(8,128)(2,1)S(1)}, u32[]{:S(2)}, u32[]{:S(2)}) collective-permute-start(bf16[32,128]{1,0:T(8,128)(2,1)S(1)} %get-tuple-element.26.refs_0_.a), channel_id=1, source_target_pairs={{0,6},{1,7},{2,4},{3,5},{4,2},{5,3},{6,0},{7,1},{8,14},{9,15},{10,... | collective-permute-start | bytes 24584 | tf_op jit(solution)/shard_map/ppermute | solution.py:361
  6.6 0.0 collective-permute-start.1
  6.6 2.0 %collective-permute-start = (bf16[32,128]{1,0:T(8,128)(2,1)S(1)}, bf16[32,128]{1,0:T(8,128)(2,1)S(1)}, u32[]{:S(2)}, u32[]{:S(2)}) collective-permute-start(bf16[32,128]{1,0:T(8,128)(2,1)S(1)} %get-tuple-element.26.refs_0_.a), channel_id=1, source_target_pairs={{0,2},{1,3},{2,6},{3,7},{4,0},{5,1},{6,4},{7,5},{8,10},{9,11},{10,... | collective-permute-start | bytes 24584 | tf_op jit(solution)/shard_map/ppermute | solution.py:361
  8.6 2.2 %fetch_cache.1 = (bf16[4,128,512]{2,1,0:T(8,128)(2,1)S(1)}, bf16[4,128,512]{2,1,0:T(8,128)(2,1)S(1)}, bf16[1,128,1024]{2,1,0:T(8,128)(2,1)S(1)}, s32[1,4,4,8]{3,...) custom-call(bf16[32,128]{1,0:T(8,128)(2,1)S(1)} %get-tuple-element.26.refs_0_.a, ...), custom_call_target="tpu_custom_call" | custom-call | bytes 3408384 | tf_op jit(solution)/shard_map/fetch_cache/pallas_call | solution.py:41
  10.9 0.0 collective-permute-done.2.d
  10.9 0.0 collective-permute-done.1.c
  10.9 0.3 collective-permute-done.b
  11.2 0.0 collective-permute-start.3
  11.2 0.5 %attend_own.1.blocks_own = f32[2,64,128]{2,1,0:T(8,128)S(1)} custom-call(s32[4,8,128]{2,1,0:T(8,128)S(1)} %get-tuple-element.25.limits, bf16[4,32,128]{2,1,0:T(8,128)(2,1)S(1)} %gather.1.own.refs_0_, bf16[4,128,512]{2,1,0:T(8,128)(2,1)S(1)} %get-tuple-element.27.fetched.keys, bf16[4,128,512]{2,1,0:T(8,128)(2,1)S(1)} %get-tuple-element.28.values), custom_call_target="tpu_custom_call" | custom-call | bytes 6000000 | tf_op jit(solution)/shard_map/attend_own/pallas_call | solution.py:41
  11.6 0.7 %collective-permute-done.3.sibling.refs_1_ = bf16[4,32,128]{2,1,0:T(8,128)(2,1)S(1)} collective-permute-done((bf16[4,32,128]{2,1,0:T(8,128)(2,1)S(1)}, bf16[4,32,128]{2,1,0:T(8,128)(2,1)S(1)}, u32[]{:S(2)}, u32[]{:S(2)}) %collective-permute-start.3) | collective-permute-done | bytes 32800 | tf_op jit(solution)/shard_map/ppermute | solution.py:369
  12.4 0.5 %attend.1 = (f32[64,128]{1,0:T(8,128)S(1)}, f32[64,128]{1,0:T(8,128)S(1)}, f32[64,128]{1,0:T(8,128)S(1)}, f32[64,128]{1,0:T(8,128)S(1)}) custom-call(s32[4,8,128]{2,1,0:T(8,128)S(1)} %get-tuple-element.25.limits, bf16[4,32,128]{2,1,0:T(8,128)(2,1)S(1)} %collective-permute-done.3.sibling.refs_1_, bf16[4,128,512]{2,1,0:T(8,128)(2,1)S(1)} %get-tuple-element.27.fetched.keys, ...), custom_call_target="tpu_custom_call" | custom-call | bytes 6000000 | tf_op jit(solution)/shard_map/attend/pallas_call | solution.py:41
  12.9 2.0 %collective-permute-start.4 = (f32[64,128]{1,0:T(8,128)S(1)}, f32[64,128]{1,0:T(8,128)S(1)}, u32[]{:S(2)}, u32[]{:S(2)}) collective-permute-start(f32[64,128]{1,0:T(8,128)S(1)} %get-tuple-element.30), channel_id=1, source_target_pairs={{0,6},{1,7},{2,4},{3,5},{4,2},{5,3},{6,0},{7,1},{8,14},{9,15},{10,... | collective-permute-start | bytes 98312 | tf_op jit(solution)/shard_map/ppermute | solution.py:361
  14.8 0.7 %collective-permute-start.5 = (f32[64,128]{1,0:T(8,128)S(1)}, f32[64,128]{1,0:T(8,128)S(1)}, u32[]{:S(2)}, u32[]{:S(2)}) collective-permute-start(f32[64,128]{1,0:T(8,128)S(1)} %get-tuple-element.31), channel_id=1, source_target_pairs={{0,4},{1,5},{2,0},{3,1},{4,6},{5,7},{6,2},{7,3},{8,12},{9,13},{10,... | collective-permute-start | bytes 98312 | tf_op jit(solution)/shard_map/ppermute | solution.py:361
  15.5 1.4 %collective-permute-start.6 = (f32[64,128]{1,0:T(8,128)S(1)}, f32[64,128]{1,0:T(8,128)S(1)}, u32[]{:S(2)}, u32[]{:S(2)}) collective-permute-start(f32[64,128]{1,0:T(8,128)S(1)} %get-tuple-element.32), channel_id=1, source_target_pairs={{0,2},{1,3},{2,6},{3,7},{4,0},{5,1},{6,4},{7,5},{8,10},{9,11},{10,... | collective-permute-start | bytes 98312 | tf_op jit(solution)/shard_map/ppermute | solution.py:361
  16.9 2.2 %fetch_b.1 = (bf16[2,1024,1024]{2,1,0:T(8,128)(2,1)S(1)}, f32[64,128]{1,0:T(8,128)S(1)}) custom-call(bf16[4,32,128]{2,1,0:T(8,128)(2,1)S(1)} %gather.1.own.refs_0_, bf16[4,32,128]{2,1,0:T(8,128)(2,1)S(1)} %collective-permute-done.3.sibling.refs_1_, f32[64,128]{1,0:T(8,128)S(1)} %get-tuple-element.29.refs_2_.a, bf16[4,1024,1024]{2,1,0:T(8,128)(2,1)} %refs_1_.3), custom_call_target="tpu_custom_call" | custom-call | bytes 4194304 | tf_op jit(solution)/shard_map/fetch_b/pallas_call | solution.py:41
  19.1 0.0 collective-permute-done.4.b
  19.1 0.0 collective-permute-done.5.c
  19.1 1.2 %collective-permute-done.6.d = f32[64,128]{1,0:T(8,128)S(1)} collective-permute-done((f32[64,128]{1,0:T(8,128)S(1)}, f32[64,128]{1,0:T(8,128)S(1)}, u32[]{:S(2)}, u32[]{:S(2)}) %collective-permute-start.6) | collective-permute-done | bytes 32800 | tf_op jit(solution)/shard_map/ppermute | solution.py:361
  20.3 0.1 join.1.own
  20.4 0.1 collective-permute-start.7
  20.5 1.2 %collective-permute-done.7.sibling = f32[64,128]{1,0:T(8,128)S(1)} collective-permute-done((f32[64,128]{1,0:T(8,128)S(1)}, f32[64,128]{1,0:T(8,128)S(1)}, u32[]{:S(2)}, u32[]{:S(2)}) %collective-permute-start.7) | collective-permute-done | bytes 32800 | tf_op jit(solution)/shard_map/ppermute | solution.py:369
  21.7 0.0 collective-permute-done.8.sibling_weight
  21.7 0.3 output.1.refs_0_.a
  22.0 1.4 %collective-permute-start.11 = (bf16[16,1024]{1,0:T(8,128)(2,1)S(1)}, bf16[16,1024]{1,0:T(8,128)(2,1)S(1)}, u32[]{:S(2)}, u32[]{:S(2)}) collective-permute-start(bf16[16,1024]{1,0:T(8,128)(2,1)S(1)} %output.1.refs_0_.a), channel_id=1, source_target_pairs={{0,6},{1,7},{2,4},{3,5},{4,2},{5,3},{6,0},{7,1},{8,14},{9,15},{10,... | collective-permute-start | bytes 98312 | tf_op jit(solution)/shard_map/ppermute | solution.py:361
  23.5 0.5 %collective-permute-start.10 = (bf16[16,1024]{1,0:T(8,128)(2,1)S(1)}, bf16[16,1024]{1,0:T(8,128)(2,1)S(1)}, u32[]{:S(2)}, u32[]{:S(2)}) collective-permute-start(bf16[16,1024]{1,0:T(8,128)(2,1)S(1)} %output.1.refs_0_.a), channel_id=1, source_target_pairs={{0,4},{1,5},{2,0},{3,1},{4,6},{5,7},{6,2},{7,3},{8,12},{9,13},{10,... | collective-permute-start | bytes 98312 | tf_op jit(solution)/shard_map/ppermute | solution.py:361
  24.0 1.5 %collective-permute-start.9 = (bf16[16,1024]{1,0:T(8,128)(2,1)S(1)}, bf16[16,1024]{1,0:T(8,128)(2,1)S(1)}, u32[]{:S(2)}, u32[]{:S(2)}) collective-permute-start(bf16[16,1024]{1,0:T(8,128)(2,1)S(1)} %output.1.refs_0_.a), channel_id=1, source_target_pairs={{0,2},{1,3},{2,6},{3,7},{4,0},{5,1},{6,4},{7,5},{8,10},{9,11},{10,... | collective-permute-start | bytes 98312 | tf_op jit(solution)/shard_map/ppermute | solution.py:361
  25.5 2.8 %fetch_c.1 = (bf16[1,1024,1024]{2,1,0:T(8,128)(2,1)S(1)}, bf16[4,512,1024]{2,1,0:T(8,128)(2,1)S(1)}) custom-call(bf16[16,1024]{1,0:T(8,128)(2,1)S(1)} %output.1.refs_0_.a, bf16[4,1024,1024]{2,1,0:T(8,128)(2,1)} %refs_1_.3, bf16[4,512,1024]{2,1,0:T(8,128)(2,1)} %refs_2_.3), custom_call_target="tpu_custom_call" | custom-call | bytes 6291456 | tf_op jit(solution)/shard_map/fetch_c/pallas_call | solution.py:41
  28.3 0.0 collective-permute-done.11.d
  28.4 0.0 collective-permute-done.10.c
  28.4 0.4 %collective-permute-done.9.b = bf16[16,1024]{1,0:T(8,128)(2,1)S(1)} collective-permute-done((bf16[16,1024]{1,0:T(8,128)(2,1)S(1)}, bf16[16,1024]{1,0:T(8,128)(2,1)S(1)}, u32[]{:S(2)}, u32[]{:S(2)}) %collective-permute-start.9) | collective-permute-done | bytes 32800 | tf_op jit(solution)/shard_map/ppermute | solution.py:361
  28.8 2.2 %experts.1 = (bf16[16,1024]{1,0:T(8,128)(2,1)S(1)}, f32[16,1024]{1,0:T(8,128)S(1)}) custom-call(f32[16,1024]{1,0:T(8,128)S(1)} %get-tuple-element.24.inputs, bf16[16,1024]{1,0:T(8,128)(2,1)S(1)} %output.1.refs_0_.a, bf16[16,1024]{1,0:T(8,128)(2,1)S(1)} %collective-permute-done.9.b, bf16[16,1024]{1,0:T(8,128)(2,1)S(1)} %collective-permute-done.10.c, ...), custom_call_target="tpu_custom_call" | custom-call | bytes 12000000 | tf_op jit(solution)/shard_map/experts/pallas_call | solution.py:41
  30.9 0.0 collective-permute-start.12
  31.0 1.2 %collective-permute-done.12 = bf16[16,1024]{1,0:T(8,128)(2,1)S(1)} collective-permute-done((bf16[16,1024]{1,0:T(8,128)(2,1)S(1)}, bf16[16,1024]{1,0:T(8,128)(2,1)S(1)}, u32[]{:S(2)}, u32[]{:S(2)}) %collective-permute-start.12) | collective-permute-done | bytes 32800 | tf_op jit(solution)/shard_map/ppermute | solution.py:369
  32.2 2.1 %collective-permute-start.15 = (bf16[16,1024]{1,0:T(8,128)(2,1)S(1)}, bf16[16,1024]{1,0:T(8,128)(2,1)S(1)}, u32[]{:S(2)}, u32[]{:S(2)}) collective-permute-start(bf16[16,1024]{1,0:T(8,128)(2,1)S(1)} %add_convert_fusion.a), channel_id=1, source_target_pairs={{0,6},{1,7},{2,4},{3,5},{4,2},{5,3},{6,0},{7,1},{8,14},{9,15},{10,... | collective-permute-start | bytes 98312 | tf_op jit(solution)/shard_map/ppermute | solution.py:361
  34.2 0.1 collective-permute-start.14
  34.3 1.9 %collective-permute-start.13 = (bf16[16,1024]{1,0:T(8,128)(2,1)S(1)}, bf16[16,1024]{1,0:T(8,128)(2,1)S(1)}, u32[]{:S(2)}, u32[]{:S(2)}) collective-permute-start(bf16[16,1024]{1,0:T(8,128)(2,1)S(1)} %add_convert_fusion.a), channel_id=1, source_target_pairs={{0,2},{1,3},{2,6},{3,7},{4,0},{5,1},{6,4},{7,5},{8,10},{9,11},{10,... | collective-permute-start | bytes 98312 | tf_op jit(solution)/shard_map/ppermute | solution.py:361
  36.3 1.7 %collective-permute-done.15.d = bf16[16,1024]{1,0:T(8,128)(2,1)S(1)} collective-permute-done((bf16[16,1024]{1,0:T(8,128)(2,1)S(1)}, bf16[16,1024]{1,0:T(8,128)(2,1)S(1)}, u32[]{:S(2)}, u32[]{:S(2)}) %collective-permute-start.15) | collective-permute-done | bytes 32800 | tf_op jit(solution)/shard_map/ppermute | solution.py:361
  38.0 0.7 %collective-permute-done.14.c = bf16[16,1024]{1,0:T(8,128)(2,1)S(1)} collective-permute-done((bf16[16,1024]{1,0:T(8,128)(2,1)S(1)}, bf16[16,1024]{1,0:T(8,128)(2,1)S(1)}, u32[]{:S(2)}, u32[]{:S(2)}) %collective-permute-start.14) | collective-permute-done | bytes 32800 | tf_op jit(solution)/shard_map/ppermute | solution.py:361
  38.7 0.6 %collective-permute-done.13.b = bf16[16,1024]{1,0:T(8,128)(2,1)S(1)} collective-permute-done((bf16[16,1024]{1,0:T(8,128)(2,1)S(1)}, bf16[16,1024]{1,0:T(8,128)(2,1)S(1)}, u32[]{:S(2)}, u32[]{:S(2)}) %collective-permute-start.13) | collective-permute-done | bytes 32800 | tf_op jit(solution)/shard_map/ppermute | solution.py:361
  39.2 0.6 %final.1 = bf16[4,4,1024]{2,1,0:T(4,128)(2,1)} custom-call(f32[16,1024]{1,0:T(8,128)S(1)} %get-tuple-element.41.residual, bf16[16,1024]{1,0:T(8,128)(2,1)S(1)} %add_convert_fusion.a, bf16[16,1024]{1,0:T(8,128)(2,1)S(1)} %collective-permute-done.13.b, bf16[16,1024]{1,0:T(8,128)(2,1)S(1)} %collective-permute-done.14.c, ...), custom_call_target="tpu_custom_call" | custom-call | tf_op jit(solution)/shard_map/final/pallas_call | solution.py:41
  (2 shorter events, 0.0 us)
Async XLA Ops:
  0.0 21.7 %collective-permute-start.8 = (bf16[128,1024]{1,0:T(8,128)(2,1)}, bf16[128,1024]{1,0:T(8,128)(2,1)S(1)}, u32[]{:S(2)}, u32[]{:S(2)}) collective-permute-start(bf16[128,1024]{1,0:T(8,128)(2,1)} %param.15), channel_id=1, source_target_pairs={{0,1},{1,0},{2,3},{3,2},{4,5},{5,4},{6,7},{7,6},{8,9},{9,8},{10,11... | collective-permute-start | bytes 786440 | tf_op jit(solution)/shard_map/ppermute | solution.py:369
  2.0 8.9 %collective-permute-start.2 = (bf16[32,128]{1,0:T(8,128)(2,1)S(1)}, bf16[32,128]{1,0:T(8,128)(2,1)S(1)}, u32[]{:S(2)}, u32[]{:S(2)}) collective-permute-start(bf16[32,128]{1,0:T(8,128)(2,1)S(1)} %get-tuple-element.26.refs_0_.a), channel_id=1, source_target_pairs={{0,6},{1,7},{2,4},{3,5},{4,2},{5,3},{6,0},{7,1},{8,14},{9,15},{10,... | collective-permute-start | bytes 24584 | tf_op jit(solution)/shard_map/ppermute | solution.py:361
  6.6 4.3 %collective-permute-start.1 = (bf16[32,128]{1,0:T(8,128)(2,1)S(1)}, bf16[32,128]{1,0:T(8,128)(2,1)S(1)}, u32[]{:S(2)}, u32[]{:S(2)}) collective-permute-start(bf16[32,128]{1,0:T(8,128)(2,1)S(1)} %get-tuple-element.26.refs_0_.a), channel_id=1, source_target_pairs={{0,4},{1,5},{2,0},{3,1},{4,6},{5,7},{6,2},{7,3},{8,12},{9,13},{10,... | collective-permute-start | bytes 24584 | tf_op jit(solution)/shard_map/ppermute | solution.py:361
  6.6 4.5 %collective-permute-start = (bf16[32,128]{1,0:T(8,128)(2,1)S(1)}, bf16[32,128]{1,0:T(8,128)(2,1)S(1)}, u32[]{:S(2)}, u32[]{:S(2)}) collective-permute-start(bf16[32,128]{1,0:T(8,128)(2,1)S(1)} %get-tuple-element.26.refs_0_.a), channel_id=1, source_target_pairs={{0,2},{1,3},{2,6},{3,7},{4,0},{5,1},{6,4},{7,5},{8,10},{9,11},{10,... | collective-permute-start | bytes 24584 | tf_op jit(solution)/shard_map/ppermute | solution.py:361
  11.2 1.2 %collective-permute-start.3 = (bf16[4,32,128]{2,1,0:T(8,128)(2,1)S(1)}, bf16[4,32,128]{2,1,0:T(8,128)(2,1)S(1)}, u32[]{:S(2)}, u32[]{:S(2)}) collective-permute-start(bf16[4,32,128]{2,1,0:T(8,128)(2,1)S(1)} %gather.1.own.refs_0_), channel_id=1, source_target_pairs={{0,1},{1,0},{2,3},{3,2},{4,5},{5,4},{6,7},{7,6},{8,9},{9,8},{10,11... | collective-permute-start | bytes 98312 | tf_op jit(solution)/shard_map/ppermute | solution.py:369
  12.9 6.3 %collective-permute-start.4 = (f32[64,128]{1,0:T(8,128)S(1)}, f32[64,128]{1,0:T(8,128)S(1)}, u32[]{:S(2)}, u32[]{:S(2)}) collective-permute-start(f32[64,128]{1,0:T(8,128)S(1)} %get-tuple-element.30), channel_id=1, source_target_pairs={{0,6},{1,7},{2,4},{3,5},{4,2},{5,3},{6,0},{7,1},{8,14},{9,15},{10,... | collective-permute-start | bytes 98312 | tf_op jit(solution)/shard_map/ppermute | solution.py:361
  14.8 4.3 %collective-permute-start.5 = (f32[64,128]{1,0:T(8,128)S(1)}, f32[64,128]{1,0:T(8,128)S(1)}, u32[]{:S(2)}, u32[]{:S(2)}) collective-permute-start(f32[64,128]{1,0:T(8,128)S(1)} %get-tuple-element.31), channel_id=1, source_target_pairs={{0,4},{1,5},{2,0},{3,1},{4,6},{5,7},{6,2},{7,3},{8,12},{9,13},{10,... | collective-permute-start | bytes 98312 | tf_op jit(solution)/shard_map/ppermute | solution.py:361
  15.5 4.8 %collective-permute-start.6 = (f32[64,128]{1,0:T(8,128)S(1)}, f32[64,128]{1,0:T(8,128)S(1)}, u32[]{:S(2)}, u32[]{:S(2)}) collective-permute-start(f32[64,128]{1,0:T(8,128)S(1)} %get-tuple-element.32), channel_id=1, source_target_pairs={{0,2},{1,3},{2,6},{3,7},{4,0},{5,1},{6,4},{7,5},{8,10},{9,11},{10,... | collective-permute-start | bytes 98312 | tf_op jit(solution)/shard_map/ppermute | solution.py:361
  20.4 1.3 %collective-permute-start.7 = (f32[64,128]{1,0:T(8,128)S(1)}, f32[64,128]{1,0:T(8,128)S(1)}, u32[]{:S(2)}, u32[]{:S(2)}) collective-permute-start(f32[64,128]{1,0:T(8,128)S(1)} %join.1.own), channel_id=1, source_target_pairs={{0,1},{1,0},{2,3},{3,2},{4,5},{5,4},{6,7},{7,6},{8,9},{9,8},{10,11... | collective-permute-start | bytes 98312 | tf_op jit(solution)/shard_map/ppermute | solution.py:369
  22.0 6.3 %collective-permute-start.11 = (bf16[16,1024]{1,0:T(8,128)(2,1)S(1)}, bf16[16,1024]{1,0:T(8,128)(2,1)S(1)}, u32[]{:S(2)}, u32[]{:S(2)}) collective-permute-start(bf16[16,1024]{1,0:T(8,128)(2,1)S(1)} %output.1.refs_0_.a), channel_id=1, source_target_pairs={{0,6},{1,7},{2,4},{3,5},{4,2},{5,3},{6,0},{7,1},{8,14},{9,15},{10,... | collective-permute-start | bytes 98312 | tf_op jit(solution)/shard_map/ppermute | solution.py:361
  23.5 4.9 %collective-permute-start.10 = (bf16[16,1024]{1,0:T(8,128)(2,1)S(1)}, bf16[16,1024]{1,0:T(8,128)(2,1)S(1)}, u32[]{:S(2)}, u32[]{:S(2)}) collective-permute-start(bf16[16,1024]{1,0:T(8,128)(2,1)S(1)} %output.1.refs_0_.a), channel_id=1, source_target_pairs={{0,4},{1,5},{2,0},{3,1},{4,6},{5,7},{6,2},{7,3},{8,12},{9,13},{10,... | collective-permute-start | bytes 98312 | tf_op jit(solution)/shard_map/ppermute | solution.py:361
  24.0 4.8 %collective-permute-start.9 = (bf16[16,1024]{1,0:T(8,128)(2,1)S(1)}, bf16[16,1024]{1,0:T(8,128)(2,1)S(1)}, u32[]{:S(2)}, u32[]{:S(2)}) collective-permute-start(bf16[16,1024]{1,0:T(8,128)(2,1)S(1)} %output.1.refs_0_.a), channel_id=1, source_target_pairs={{0,2},{1,3},{2,6},{3,7},{4,0},{5,1},{6,4},{7,5},{8,10},{9,11},{10,... | collective-permute-start | bytes 98312 | tf_op jit(solution)/shard_map/ppermute | solution.py:361
  30.9 1.2 %collective-permute-start.12 = (bf16[16,1024]{1,0:T(8,128)(2,1)S(1)}, bf16[16,1024]{1,0:T(8,128)(2,1)S(1)}, u32[]{:S(2)}, u32[]{:S(2)}) collective-permute-start(bf16[16,1024]{1,0:T(8,128)(2,1)S(1)} %get-tuple-element.42), channel_id=1, source_target_pairs={{0,1},{1,0},{2,3},{3,2},{4,5},{5,4},{6,7},{7,6},{8,9},{9,8},{10,11... | collective-permute-start | bytes 98312 | tf_op jit(solution)/shard_map/ppermute | solution.py:369
  32.2 5.8 %collective-permute-start.15 = (bf16[16,1024]{1,0:T(8,128)(2,1)S(1)}, bf16[16,1024]{1,0:T(8,128)(2,1)S(1)}, u32[]{:S(2)}, u32[]{:S(2)}) collective-permute-start(bf16[16,1024]{1,0:T(8,128)(2,1)S(1)} %add_convert_fusion.a), channel_id=1, source_target_pairs={{0,6},{1,7},{2,4},{3,5},{4,2},{5,3},{6,0},{7,1},{8,14},{9,15},{10,... | collective-permute-start | bytes 98312 | tf_op jit(solution)/shard_map/ppermute | solution.py:361
  34.2 4.4 %collective-permute-start.14 = (bf16[16,1024]{1,0:T(8,128)(2,1)S(1)}, bf16[16,1024]{1,0:T(8,128)(2,1)S(1)}, u32[]{:S(2)}, u32[]{:S(2)}) collective-permute-start(bf16[16,1024]{1,0:T(8,128)(2,1)S(1)} %add_convert_fusion.a), channel_id=1, source_target_pairs={{0,4},{1,5},{2,0},{3,1},{4,6},{5,7},{6,2},{7,3},{8,12},{9,13},{10,... | collective-permute-start | bytes 98312 | tf_op jit(solution)/shard_map/ppermute | solution.py:361
  34.3 4.9 %collective-permute-start.13 = (bf16[16,1024]{1,0:T(8,128)(2,1)S(1)}, bf16[16,1024]{1,0:T(8,128)(2,1)S(1)}, u32[]{:S(2)}, u32[]{:S(2)}) collective-permute-start(bf16[16,1024]{1,0:T(8,128)(2,1)S(1)} %add_convert_fusion.a), channel_id=1, source_target_pairs={{0,2},{1,3},{2,6},{3,7},{4,0},{5,1},{6,4},{7,5},{8,10},{9,11},{10,... | collective-permute-start | bytes 98312 | tf_op jit(solution)/shard_map/ppermute | solution.py:361

commit v4 on v3

--- a/solution.py
+++ b/solution.py
@@ -17,8 +17,8 @@
 F32 = jnp.float32
 BF16 = jnp.bfloat16
 VMEM_LIMIT = 16 * 1024 * 1024
-SPLIT = (1, 3)
-ORDER = ((1, 2, 3), (3, 2, 1), (1, 2, 3), (1, 2, 3))
+SPLIT = (0, 3)
+ORDER = ((1, 2, 3), (3, 2, 1), (1, 2, 3), (2, 3, 1))
 COST = (8_000_000, 6_000_000, 1_000_000, 12_000_000)
 
 
@@ -34,7 +34,7 @@
     return pl.BlockSpec(memory_space=space)
 
 
-def call(kernel, outs, operands, name, stay=(), scratch=(), hbm_out=False, cost=0):
+def call(kernel, outs, operands, name, stay=(), scratch=(), hbm_out=False, cost=0, same=()):
     operands = [
         pltpu.with_memory_space_constraint(x, pltpu.HBM) if i in stay else x for i, x in enumerate(operands)
     ]
@@ -46,6 +46,7 @@
         in_specs=[on(pltpu.HBM if i in stay else pltpu.VMEM) for i in range(len(operands))],
         out_specs=[on(pltpu.VMEM) for _ in outs],
         scratch_shapes=list(scratch),
+        input_output_aliases=dict(same),
         compiler_params=pltpu.CompilerParams(vmem_limit_bytes=VMEM_LIMIT),
         cost_estimate=pl.CostEstimate(flops=0, bytes_accessed=cost, transcendentals=0),
         name=name,
@@ -190,13 +191,13 @@
     return peak, weights.astype(BF16), jnp.sum(weights, axis=-1, keepdims=True)
 
 
-def attend_blocks(steps, limits, heads, core, keys, values, store):
+def attend_blocks(steps, limits, heads, cores, keys, values, store):
     device = lax.axis_index("tp")
     requests, count, _ = keys.shape
     rows = steps * GROUP
     scale = HEAD_DIMENSION**-0.5
     pairs = [(s, r) for s in range(2) for r in range(requests)]
-    columns = [pl.ds(pl.multiple_of((2 * s + core) * 128, 128), 128) for s in range(2)]
+    columns = [pl.ds(pl.multiple_of((2 * s + cores[s]) * 128, 128), 128) for s in range(2)]
     scores = []
     for s, r in pairs:
         q = spread(heads[s, r * rows : (r + 1) * rows].astype(F32) * scale, GROUP)
@@ -216,24 +217,23 @@
 
 
 def attend_own_kernel(steps, limits, own, keys, values, out):
-    core = lax.axis_index("tp") % 2
-
     def store(s, row, x):
         out[s, row : row + x.shape[0], :] = x
 
-    attend_blocks(steps, limits, own, core, keys, values, store)
+    attend_blocks(steps, limits, own, [near_core(s) for s in range(2)], keys, values, store)
 
 
 def attend_sibling_kernel(steps, limits, sibling, keys, values, blocks_own, out0, out1, out2, out3, blocks):
     device = lax.axis_index("tp")
-    chip, core = device // 2, device % 2
+    chip = device // 2
+    near = [near_core(s) for s in range(2)]
 
     def store(s, row, x):
-        blocks[2 * s + 1 - core, row : row + x.shape[0], :] = x
+        blocks[2 * s + 1 - near[s], row : row + x.shape[0], :] = x
 
     for s in range(2):
-        blocks[2 * s + core] = blocks_own[s]
-    attend_blocks(steps, limits, sibling, 1 - core, keys, values, store)
+        blocks[2 * s + near[s]] = blocks_own[s]
+    attend_blocks(steps, limits, sibling, [1 - x for x in near], keys, values, store)
     out0[...] = blocks[chip]
     for k, out in ((1, out1), (2, out2), (3, out3)):
         out[...] = blocks[partner(chip, k)]
@@ -241,13 +241,13 @@
 
 def fresh_part(requests, steps, own, sibling, after, out):
     device = lax.axis_index("tp")
-    chip, core = device // 2, device % 2
+    chip = device // 2
     rows = steps * GROUP
     tokens = requests * steps
     n = requests * rows
 
     def held(s, at_core):
-        return jnp.where(core == at_core, own[s].astype(F32), sibling[s].astype(F32))
+        return jnp.where(near_core(s) == at_core, own[s].astype(F32), sibling[s].astype(F32))
 
     def pick(x):
         return jnp.where(chip % 2 == 1, x[tokens:], x[:tokens]).astype(BF16)
@@ -305,7 +305,7 @@
     return [first] + [part for _, part in sorted(zip(order, parts), key=lambda pair: pair[0])]
 
 
-def gather_kernel(order, a, b, c, d, fetched, out):
+def gather_kernel(order, a, b, c, d, weight, out, same_weight):
     chip = lax.axis_index("tp") // 2
     own, *others = sort_chips(order, a, (b, c, d))
     out[chip] = own[...]
@@ -358,7 +358,13 @@
 
 def other_chip(x, k, devices):
     to = {1: (1, 3, 0, 2), 2: (2, 0, 3, 1), 3: (3, 2, 1, 0)}[k]
-    return lax.ppermute(x, "tp", [(i, 2 * to[i // 2] + i % 2) for i in range(devices)])
+    return lax.ppermute(x, "tp", [(i, 2 * to[i // 2] + 1 - i % 2) for i in range(devices)])
+
+
+def near_core(s):
+    device = lax.axis_index("tp")
+    core = device % 2
+    return jnp.where(device // 2 == s, core, 1 - core)
 
 
 def to_chips(parts, devices, order):
@@ -386,7 +392,6 @@
     devices = lax.axis_size("tp")
     chips = devices // 2
     rows = tokens * GROUP
-    sibling_weight = other_core(out_weight, devices)
     heads, limits, inputs = call(
         project_kernel,
         [((rows, 128), BF16), ((requests, 8, 128), jnp.int32), ((tokens, model_width), F32)],
@@ -407,12 +412,14 @@
     cuts = [(0, SPLIT[0]), (SPLIT[0], SPLIT[1] - SPLIT[0]), (SPLIT[1], experts - SPLIT[1])]
     gate_up = [[(gate_up_weight, *cut)] if cut[1] else [] for cut in cuts]
     keys, values, own_weight, ids, shares, *gate_up_a = fetch(caches + small + gate_up[0], [heads], "fetch_cache")
-    (gathered,) = call(
+    gathered, own_weight = call(
         functools.partial(gather_kernel, ORDER[0]),
-        [((chips, rows, 128), BF16)],
-        [*to_chips([heads] * chips, devices, ORDER[0]), keys],
+        [((chips, rows, 128), BF16), (own_weight.shape, BF16)],
+        [*to_chips([heads] * chips, devices, ORDER[0]), own_weight],
         "gather",
-    )
+        same={chips: 1},
+    )
+    sibling_weight = other_core(own_weight[0], devices)
     sibling = other_core(gathered, devices)
     (blocks_own,) = call(
         functools.partial(attend_own_kernel, steps),

time: 40 us -> 38 us (0.950)
  waiting for transfers between devices: 7.99 us -> 6.7 us
  starting transfers between devices: 18.8 us -> 18.2 us
    ppermute x12, starting transfers between devices: 18.3 us -> 17.2 us  [other_chip(): lax.ppermute(x, 'tp', [(i, 2 * to[i // 2] + 1 - i % 2) for i in range(dev...]
    ppermute x12, waiting for transfers between devices: 4.85 us -> 3.88 us  [other_chip(): lax.ppermute(x, 'tp', [(i, 2 * to[i // 2] + 1 - i % 2) for i in range(dev...]
    ppermute x4, starting transfers between devices: 0.54 us -> 1.07 us  [other_core(): return lax.ppermute(x, 'tp', [(i, i ^ 1) for i in range(devices)])]
  transfers between devices with their start and end apart: 16 -> 16, of which waited for: 9 -> 9; matrix products, arithmetic and copies ran while one was open for 0% -> 0% of each run, Pallas kernels for 25% -> 22%
where the time goes in v4:
time: 38 us; the launch traced here: 37.9 us
  starting transfers between devices  18.2 us (48%)
  Pallas kernels  12.8 us (34%)
  waiting for transfers between devices  6.7 us (18%)
    ppermute x12, starting transfers between devices, other_chip(): lax.ppermute(x, 'tp', [(i, 2 * to[i // 2] + 1 - i % 2) for i in range(dev...  17.2 us
    pallas_call x11, Pallas kernels, call(): pl.pallas_call(kernel, out_shape=[jax.ShapeDtypeStruct(s, d) if hbm_out e...  12.8 us
    ppermute x12, waiting for transfers between devices, other_chip(): lax.ppermute(x, 'tp', [(i, 2 * to[i // 2] + 1 - i % 2) for i in range(dev...  3.88 us
    ppermute x4, waiting for transfers between devices, other_core(): return lax.ppermute(x, 'tp', [(i, i ^ 1) for i in range(devices)])  2.82 us
    ppermute x4, starting transfers between devices, other_core(): return lax.ppermute(x, 'tp', [(i, i ^ 1) for i in range(devices)])  1.07 us
  transfers between devices with their start and end apart: 16, of which 9 were waited for; matrix products, arithmetic and copies ran while one was open for 0% of the time, Pallas kernels for 22%

profile of v4, /device:TPU:0, one launch (start us, length us, event | category | flops | bytes accessed | tf_op | source)
XLA Modules:
  0.0 37.9 jit_solution(6733305988957387860)
XLA Ops:
  0.0 1.5 %project.1 = (bf16[32,128]{1,0:T(8,128)(2,1)S(1)}, s32[4,8,128]{2,1,0:T(8,128)S(1)}, f32[16,1024]{1,0:T(8,128)S(1)}) custom-call(s32[4]{0:T(128)} %lengths_in.1, bf16[4,4,1024]{2,1,0:T(4,128)(2,1)} %hidden_in.1, bf16[256,1024]{1,0:T(8,128)(2,1)} %weight_in.1), custom_call_target="tpu_custom_call" | custom-call | bytes 8000000 | tf_op jit(solution)/shard_map/project/pallas_call | solution.py:41
  1.5 4.6 %collective-permute-start.2 = (bf16[32,128]{1,0:T(8,128)(2,1)S(1)}, bf16[32,128]{1,0:T(8,128)(2,1)S(1)}, u32[]{:S(2)}, u32[]{:S(2)}) collective-permute-start(bf16[32,128]{1,0:T(8,128)(2,1)S(1)} %get-tuple-element.27.refs_0_.a), channel_id=1, source_target_pairs={{0,7},{1,6},{2,5},{3,4},{4,3},{5,2},{6,1},{7,0},{8,15},{9,14},{10,... | collective-permute-start | bytes 24584 | tf_op jit(solution)/shard_map/ppermute | solution.py:361
  6.1 0.0 collective-permute-start.1
  6.1 1.7 %collective-permute-start = (bf16[32,128]{1,0:T(8,128)(2,1)S(1)}, bf16[32,128]{1,0:T(8,128)(2,1)S(1)}, u32[]{:S(2)}, u32[]{:S(2)}) collective-permute-start(bf16[32,128]{1,0:T(8,128)(2,1)S(1)} %get-tuple-element.27.refs_0_.a), channel_id=1, source_target_pairs={{0,3},{1,2},{2,7},{3,6},{4,1},{5,0},{6,5},{7,4},{8,11},{9,10},{10,... | collective-permute-start | bytes 24584 | tf_op jit(solution)/shard_map/ppermute | solution.py:361
  7.8 1.5 %fetch_cache.1 = (bf16[4,128,512]{2,1,0:T(8,128)(2,1)S(1)}, bf16[4,128,512]{2,1,0:T(8,128)(2,1)S(1)}, bf16[1,128,1024]{2,1,0:T(8,128)(2,1)S(1)}, s32[1,4,4,8]{3,2,1,0:T(4,128)S(1)}, s32[1,4,4,8]{3,2,1,0:T(4,128)S(1)}) custom-call(bf16[32,128]{1,0:T(8,128)(2,1)S(1)} %get-tuple-element.27.refs_0_.a, bf16[4,128,512]{2,1,0:T(8,128)(2,1)} %refs_1_.2, ...), custom_call_target="tpu_custom_call" | custom-call | bytes 1311232 | tf_op jit(solution)/shard_map/fetch_cache/pallas_call | solution.py:41
  9.3 0.0 collective-permute-done.2.d
  9.3 0.0 collective-permute-done.1.c
  9.3 0.8 %collective-permute-done.b = bf16[32,128]{1,0:T(8,128)(2,1)S(1)} collective-permute-done((bf16[32,128]{1,0:T(8,128)(2,1)S(1)}, bf16[32,128]{1,0:T(8,128)(2,1)S(1)}, u32[]{:S(2)}, u32[]{:S(2)}) %collective-permute-start) | collective-permute-done | bytes 8224 | tf_op jit(solution)/shard_map/ppermute | solution.py:361
  10.1 0.6 %collective-permute-start.8 = (bf16[128,1024]{1,0:T(8,128)(2,1)S(1)}, bf16[128,1024]{1,0:T(8,128)(2,1)S(1)}, u32[]{:S(2)}, u32[]{:S(2)}) collective-permute-start(bf16[128,1024]{1,0:T(8,128)(2,1)S(1)} %bitcast.6), channel_id=1, source_target_pairs={{0,1},{1,0},{2,3},{3,2},{4,5},{5,4},{6,7},{7,6},{8,9},{9,8},{10,11... | collective-permute-start | bytes 786440 | tf_op jit(solution)/shard_map/ppermute | solution.py:375
  10.7 0.1 collective-permute-start.3
  10.8 0.4 %attend_own.1.blocks_own = f32[2,64,128]{2,1,0:T(8,128)S(1)} custom-call(s32[4,8,128]{2,1,0:T(8,128)S(1)} %get-tuple-element.26.limits, bf16[4,32,128]{2,1,0:T(8,128)(2,1)S(1)} %get-tuple-element.29.own.refs_0_, bf16[4,128,512]{2,1,0:T(8,128)(2,1)S(1)} %get-tuple-element.30.keys, bf16[4,128,512]{2,1,0:T(8,128)(2,1)S(1)} %get-tuple-element.31.values), custom_call_target="tpu_custom_call" | custom-call | bytes 6000000 | tf_op jit(solution)/shard_map/attend_own/pallas_call | solution.py:41
  11.2 0.7 %collective-permute-done.3.sibling.refs_1_ = bf16[4,32,128]{2,1,0:T(8,128)(2,1)S(1)} collective-permute-done((bf16[4,32,128]{2,1,0:T(8,128)(2,1)S(1)}, bf16[4,32,128]{2,1,0:T(8,128)(2,1)S(1)}, u32[]{:S(2)}, u32[]{:S(2)}) %collective-permute-start.3) | collective-permute-done | bytes 32800 | tf_op jit(solution)/shard_map/ppermute | solution.py:375
  11.9 0.5 %attend.1 = (f32[64,128]{1,0:T(8,128)S(1)}, f32[64,128]{1,0:T(8,128)S(1)}, f32[64,128]{1,0:T(8,128)S(1)}, f32[64,128]{1,0:T(8,128)S(1)}) custom-call(s32[4,8,128]{2,1,0:T(8,128)S(1)} %get-tuple-element.26.limits, bf16[4,32,128]{2,1,0:T(8,128)(2,1)S(1)} %collective-permute-done.3.sibling.refs_1_, bf16[4,128,512]{2,1,0:T(8,128)(2,1)S(1)} %get-tuple-element.30.keys, ...), custom_call_target="tpu_custom_call" | custom-call | bytes 6000000 | tf_op jit(solution)/shard_map/attend/pallas_call | solution.py:41
  12.4 1.7 %collective-permute-start.4 = (f32[64,128]{1,0:T(8,128)S(1)}, f32[64,128]{1,0:T(8,128)S(1)}, u32[]{:S(2)}, u32[]{:S(2)}) collective-permute-start(f32[64,128]{1,0:T(8,128)S(1)} %get-tuple-element.33), channel_id=1, source_target_pairs={{0,7},{1,6},{2,5},{3,4},{4,3},{5,2},{6,1},{7,0},{8,15},{9,14},{10,... | collective-permute-start | bytes 98312 | tf_op jit(solution)/shard_map/ppermute | solution.py:361
  14.1 0.7 %collective-permute-start.5 = (f32[64,128]{1,0:T(8,128)S(1)}, f32[64,128]{1,0:T(8,128)S(1)}, u32[]{:S(2)}, u32[]{:S(2)}) collective-permute-start(f32[64,128]{1,0:T(8,128)S(1)} %get-tuple-element.34), channel_id=1, source_target_pairs={{0,5},{1,4},{2,1},{3,0},{4,7},{5,6},{6,3},{7,2},{8,13},{9,12},{10,... | collective-permute-start | bytes 98312 | tf_op jit(solution)/shard_map/ppermute | solution.py:361
  14.8 1.0 %collective-permute-start.6 = (f32[64,128]{1,0:T(8,128)S(1)}, f32[64,128]{1,0:T(8,128)S(1)}, u32[]{:S(2)}, u32[]{:S(2)}) collective-permute-start(f32[64,128]{1,0:T(8,128)S(1)} %get-tuple-element.35), channel_id=1, source_target_pairs={{0,3},{1,2},{2,7},{3,6},{4,1},{5,0},{6,5},{7,4},{8,11},{9,10},{10,... | collective-permute-start | bytes 98312 | tf_op jit(solution)/shard_map/ppermute | solution.py:361
  15.8 2.9 %fetch_b.1 = (bf16[3,1024,1024]{2,1,0:T(8,128)(2,1)S(1)}, f32[64,128]{1,0:T(8,128)S(1)}) custom-call(bf16[4,32,128]{2,1,0:T(8,128)(2,1)S(1)} %get-tuple-element.29.own.refs_0_, bf16[4,32,128]{2,1,0:T(8,128)(2,1)S(1)} %collective-permute-done.3.sibling.refs_1_, f32[64,128]{1,0:T(8,128)S(1)} %get-tuple-element.32.refs_2_.a, bf16[4,1024,1024]{2,1,0:T(8,128)(2,1)} %refs_1_.3), custom_call_target="tpu_custom_call" | custom-call | bytes 6291456 | tf_op jit(solution)/shard_map/fetch_b/pallas_call | solution.py:41
  18.8 0.0 collective-permute-done.4.b
  18.8 0.0 collective-permute-done.5.c
  18.8 0.3 collective-permute-done.6.d
  19.1 0.1 join.1.own
  19.2 0.2 collective-permute-start.7
  19.4 1.1 %collective-permute-done.7.sibling = f32[64,128]{1,0:T(8,128)S(1)} collective-permute-done((f32[64,128]{1,0:T(8,128)S(1)}, f32[64,128]{1,0:T(8,128)S(1)}, u32[]{:S(2)}, u32[]{:S(2)}) %collective-permute-start.7) | collective-permute-done | bytes 32800 | tf_op jit(solution)/shard_map/ppermute | solution.py:375
  20.5 0.0 collective-permute-done.8.sibling_weight
  20.5 0.3 output.1.refs_0_.a
  20.8 1.9 %collective-permute-start.11 = (bf16[16,1024]{1,0:T(8,128)(2,1)S(1)}, bf16[16,1024]{1,0:T(8,128)(2,1)S(1)}, u32[]{:S(2)}, u32[]{:S(2)}) collective-permute-start(bf16[16,1024]{1,0:T(8,128)(2,1)S(1)} %output.1.refs_0_.a), channel_id=1, source_target_pairs={{0,7},{1,6},{2,5},{3,4},{4,3},{5,2},{6,1},{7,0},{8,15},{9,14},{10,... | collective-permute-start | bytes 98312 | tf_op jit(solution)/shard_map/ppermute | solution.py:361
  22.7 0.0 collective-permute-start.10
  22.7 1.7 %collective-permute-start.9 = (bf16[16,1024]{1,0:T(8,128)(2,1)S(1)}, bf16[16,1024]{1,0:T(8,128)(2,1)S(1)}, u32[]{:S(2)}, u32[]{:S(2)}) collective-permute-start(bf16[16,1024]{1,0:T(8,128)(2,1)S(1)} %output.1.refs_0_.a), channel_id=1, source_target_pairs={{0,3},{1,2},{2,7},{3,6},{4,1},{5,0},{6,5},{7,4},{8,11},{9,10},{10,... | collective-permute-start | bytes 98312 | tf_op jit(solution)/shard_map/ppermute | solution.py:361
  24.5 2.8 %fetch_c.1 = (bf16[1,1024,1024]{2,1,0:T(8,128)(2,1)S(1)}, bf16[4,512,1024]{2,1,0:T(8,128)(2,1)S(1)}) custom-call(bf16[16,1024]{1,0:T(8,128)(2,1)S(1)} %output.1.refs_0_.a, bf16[4,1024,1024]{2,1,0:T(8,128)(2,1)} %refs_1_.3, bf16[4,512,1024]{2,1,0:T(8,128)(2,1)} %refs_2_.3), custom_call_target="tpu_custom_call" | custom-call | bytes 6291456 | tf_op jit(solution)/shard_map/fetch_c/pallas_call | solution.py:41
  27.3 0.0 collective-permute-done.11.d
  27.3 0.0 collective-permute-done.10.c
  27.3 0.2 collective-permute-done.9.b
  27.6 2.2 %experts.1 = (bf16[16,1024]{1,0:T(8,128)(2,1)S(1)}, f32[16,1024]{1,0:T(8,128)S(1)}) custom-call(f32[16,1024]{1,0:T(8,128)S(1)} %get-tuple-element.25.inputs, bf16[16,1024]{1,0:T(8,128)(2,1)S(1)} %output.1.refs_0_.a, bf16[16,1024]{1,0:T(8,128)(2,1)S(1)} %collective-permute-done.9.b, bf16[16,1024]{1,0:T(8,128)(2,1)S(1)} %collective-permute-done.10.c, ...), custom_call_target="tpu_custom_call" | custom-call | bytes 12000000 | tf_op jit(solution)/shard_map/experts/pallas_call | solution.py:41
  29.7 0.1 collective-permute-start.12
  29.9 1.1 %collective-permute-done.12 = bf16[16,1024]{1,0:T(8,128)(2,1)S(1)} collective-permute-done((bf16[16,1024]{1,0:T(8,128)(2,1)S(1)}, bf16[16,1024]{1,0:T(8,128)(2,1)S(1)}, u32[]{:S(2)}, u32[]{:S(2)}) %collective-permute-start.12) | collective-permute-done | bytes 32800 | tf_op jit(solution)/shard_map/ppermute | solution.py:375
  30.9 0.5 %collective-permute-start.15 = (bf16[16,1024]{1,0:T(8,128)(2,1)S(1)}, bf16[16,1024]{1,0:T(8,128)(2,1)S(1)}, u32[]{:S(2)}, u32[]{:S(2)}) collective-permute-start(bf16[16,1024]{1,0:T(8,128)(2,1)S(1)} %add_convert_fusion.a), channel_id=1, source_target_pairs={{0,3},{1,2},{2,7},{3,6},{4,1},{5,0},{6,5},{7,4},{8,11},{9,10},{10,... | collective-permute-start | bytes 98312 | tf_op jit(solution)/shard_map/ppermute | solution.py:361
  31.4 1.7 %collective-permute-start.14 = (bf16[16,1024]{1,0:T(8,128)(2,1)S(1)}, bf16[16,1024]{1,0:T(8,128)(2,1)S(1)}, u32[]{:S(2)}, u32[]{:S(2)}) collective-permute-start(bf16[16,1024]{1,0:T(8,128)(2,1)S(1)} %add_convert_fusion.a), channel_id=1, source_target_pairs={{0,7},{1,6},{2,5},{3,4},{4,3},{5,2},{6,1},{7,0},{8,15},{9,14},{10,... | collective-permute-start | bytes 98312 | tf_op jit(solution)/shard_map/ppermute | solution.py:361
  33.1 1.6 %collective-permute-start.13 = (bf16[16,1024]{1,0:T(8,128)(2,1)S(1)}, bf16[16,1024]{1,0:T(8,128)(2,1)S(1)}, u32[]{:S(2)}, u32[]{:S(2)}) collective-permute-start(bf16[16,1024]{1,0:T(8,128)(2,1)S(1)} %add_convert_fusion.a), channel_id=1, source_target_pairs={{0,5},{1,4},{2,1},{3,0},{4,7},{5,6},{6,3},{7,2},{8,13},{9,12},{10,... | collective-permute-start | bytes 98312 | tf_op jit(solution)/shard_map/ppermute | solution.py:361
  34.7 0.6 %collective-permute-done.15.d = bf16[16,1024]{1,0:T(8,128)(2,1)S(1)} collective-permute-done((bf16[16,1024]{1,0:T(8,128)(2,1)S(1)}, bf16[16,1024]{1,0:T(8,128)(2,1)S(1)}, u32[]{:S(2)}, u32[]{:S(2)}) %collective-permute-start.15) | collective-permute-done | bytes 32800 | tf_op jit(solution)/shard_map/ppermute | solution.py:361
  35.2 1.4 %collective-permute-done.14.c = bf16[16,1024]{1,0:T(8,128)(2,1)S(1)} collective-permute-done((bf16[16,1024]{1,0:T(8,128)(2,1)S(1)}, bf16[16,1024]{1,0:T(8,128)(2,1)S(1)}, u32[]{:S(2)}, u32[]{:S(2)}) %collective-permute-start.14) | collective-permute-done | bytes 32800 | tf_op jit(solution)/shard_map/ppermute | solution.py:361
  36.7 0.6 %collective-permute-done.13.b = bf16[16,1024]{1,0:T(8,128)(2,1)S(1)} collective-permute-done((bf16[16,1024]{1,0:T(8,128)(2,1)S(1)}, bf16[16,1024]{1,0:T(8,128)(2,1)S(1)}, u32[]{:S(2)}, u32[]{:S(2)}) %collective-permute-start.13) | collective-permute-done | bytes 32800 | tf_op jit(solution)/shard_map/ppermute | solution.py:361
  37.2 0.6 %final.1 = bf16[4,4,1024]{2,1,0:T(4,128)(2,1)} custom-call(f32[16,1024]{1,0:T(8,128)S(1)} %get-tuple-element.43.residual, bf16[16,1024]{1,0:T(8,128)(2,1)S(1)} %add_convert_fusion.a, bf16[16,1024]{1,0:T(8,128)(2,1)S(1)} %collective-permute-done.13.b, bf16[16,1024]{1,0:T(8,128)(2,1)S(1)} %collective-permute-done.14.c, ...), custom_call_target="tpu_custom_call" | custom-call | tf_op jit(solution)/shard_map/final/pallas_call | solution.py:41
  (2 shorter events, 0.0 us)
Async XLA Ops:
  1.5 7.8 %collective-permute-start.2 = (bf16[32,128]{1,0:T(8,128)(2,1)S(1)}, bf16[32,128]{1,0:T(8,128)(2,1)S(1)}, u32[]{:S(2)}, u32[]{:S(2)}) collective-permute-start(bf16[32,128]{1,0:T(8,128)(2,1)S(1)} %get-tuple-element.27.refs_0_.a), channel_id=1, source_target_pairs={{0,7},{1,6},{2,5},{3,4},{4,3},{5,2},{6,1},{7,0},{8,15},{9,14},{10,... | collective-permute-start | bytes 24584 | tf_op jit(solution)/shard_map/ppermute | solution.py:361
  6.1 3.2 %collective-permute-start.1 = (bf16[32,128]{1,0:T(8,128)(2,1)S(1)}, bf16[32,128]{1,0:T(8,128)(2,1)S(1)}, u32[]{:S(2)}, u32[]{:S(2)}) collective-permute-start(bf16[32,128]{1,0:T(8,128)(2,1)S(1)} %get-tuple-element.27.refs_0_.a), channel_id=1, source_target_pairs={{0,5},{1,4},{2,1},{3,0},{4,7},{5,6},{6,3},{7,2},{8,13},{9,12},{10,... | collective-permute-start | bytes 24584 | tf_op jit(solution)/shard_map/ppermute | solution.py:361
  6.1 4.0 %collective-permute-start = (bf16[32,128]{1,0:T(8,128)(2,1)S(1)}, bf16[32,128]{1,0:T(8,128)(2,1)S(1)}, u32[]{:S(2)}, u32[]{:S(2)}) collective-permute-start(bf16[32,128]{1,0:T(8,128)(2,1)S(1)} %get-tuple-element.27.refs_0_.a), channel_id=1, source_target_pairs={{0,3},{1,2},{2,7},{3,6},{4,1},{5,0},{6,5},{7,4},{8,11},{9,10},{10,... | collective-permute-start | bytes 24584 | tf_op jit(solution)/shard_map/ppermute | solution.py:361
  10.1 10.4 %collective-permute-start.8 = (bf16[128,1024]{1,0:T(8,128)(2,1)S(1)}, bf16[128,1024]{1,0:T(8,128)(2,1)S(1)}, u32[]{:S(2)}, u32[]{:S(2)}) collective-permute-start(bf16[128,1024]{1,0:T(8,128)(2,1)S(1)} %bitcast.6), channel_id=1, source_target_pairs={{0,1},{1,0},{2,3},{3,2},{4,5},{5,4},{6,7},{7,6},{8,9},{9,8},{10,11... | collective-permute-start | bytes 786440 | tf_op jit(solution)/shard_map/ppermute | solution.py:375
  10.7 1.2 %collective-permute-start.3 = (bf16[4,32,128]{2,1,0:T(8,128)(2,1)S(1)}, bf16[4,32,128]{2,1,0:T(8,128)(2,1)S(1)}, u32[]{:S(2)}, u32[]{:S(2)}) collective-permute-start(bf16[4,32,128]{2,1,0:T(8,128)(2,1)S(1)} %get-tuple-element.29.own.refs_0_), channel_id=1, source_target_pairs={{0,1},{1,0},{2,3},{3,2},{4,5},{5,4},{6,7},{7,6},{8,9},{9,8},{10,11... | collective-permute-start | bytes 98312 | tf_op jit(solution)/shard_map/ppermute | solution.py:375
  12.4 6.4 %collective-permute-start.4 = (f32[64,128]{1,0:T(8,128)S(1)}, f32[64,128]{1,0:T(8,128)S(1)}, u32[]{:S(2)}, u32[]{:S(2)}) collective-permute-start(f32[64,128]{1,0:T(8,128)S(1)} %get-tuple-element.33), channel_id=1, source_target_pairs={{0,7},{1,6},{2,5},{3,4},{4,3},{5,2},{6,1},{7,0},{8,15},{9,14},{10,... | collective-permute-start | bytes 98312 | tf_op jit(solution)/shard_map/ppermute | solution.py:361
  14.1 4.7 %collective-permute-start.5 = (f32[64,128]{1,0:T(8,128)S(1)}, f32[64,128]{1,0:T(8,128)S(1)}, u32[]{:S(2)}, u32[]{:S(2)}) collective-permute-start(f32[64,128]{1,0:T(8,128)S(1)} %get-tuple-element.34), channel_id=1, source_target_pairs={{0,5},{1,4},{2,1},{3,0},{4,7},{5,6},{6,3},{7,2},{8,13},{9,12},{10,... | collective-permute-start | bytes 98312 | tf_op jit(solution)/shard_map/ppermute | solution.py:361
  14.8 4.3 %collective-permute-start.6 = (f32[64,128]{1,0:T(8,128)S(1)}, f32[64,128]{1,0:T(8,128)S(1)}, u32[]{:S(2)}, u32[]{:S(2)}) collective-permute-start(f32[64,128]{1,0:T(8,128)S(1)} %get-tuple-element.35), channel_id=1, source_target_pairs={{0,3},{1,2},{2,7},{3,6},{4,1},{5,0},{6,5},{7,4},{8,11},{9,10},{10,... | collective-permute-start | bytes 98312 | tf_op jit(solution)/shard_map/ppermute | solution.py:361
  19.2 1.3 %collective-permute-start.7 = (f32[64,128]{1,0:T(8,128)S(1)}, f32[64,128]{1,0:T(8,128)S(1)}, u32[]{:S(2)}, u32[]{:S(2)}) collective-permute-start(f32[64,128]{1,0:T(8,128)S(1)} %join.1.own), channel_id=1, source_target_pairs={{0,1},{1,0},{2,3},{3,2},{4,5},{5,4},{6,7},{7,6},{8,9},{9,8},{10,11... | collective-permute-start | bytes 98312 | tf_op jit(solution)/shard_map/ppermute | solution.py:375
  20.8 6.5 %collective-permute-start.11 = (bf16[16,1024]{1,0:T(8,128)(2,1)S(1)}, bf16[16,1024]{1,0:T(8,128)(2,1)S(1)}, u32[]{:S(2)}, u32[]{:S(2)}) collective-permute-start(bf16[16,1024]{1,0:T(8,128)(2,1)S(1)} %output.1.refs_0_.a), channel_id=1, source_target_pairs={{0,7},{1,6},{2,5},{3,4},{4,3},{5,2},{6,1},{7,0},{8,15},{9,14},{10,... | collective-permute-start | bytes 98312 | tf_op jit(solution)/shard_map/ppermute | solution.py:361
  22.7 4.6 %collective-permute-start.10 = (bf16[16,1024]{1,0:T(8,128)(2,1)S(1)}, bf16[16,1024]{1,0:T(8,128)(2,1)S(1)}, u32[]{:S(2)}, u32[]{:S(2)}) collective-permute-start(bf16[16,1024]{1,0:T(8,128)(2,1)S(1)} %output.1.refs_0_.a), channel_id=1, source_target_pairs={{0,5},{1,4},{2,1},{3,0},{4,7},{5,6},{6,3},{7,2},{8,13},{9,12},{10,... | collective-permute-start | bytes 98312 | tf_op jit(solution)/shard_map/ppermute | solution.py:361
  22.7 4.8 %collective-permute-start.9 = (bf16[16,1024]{1,0:T(8,128)(2,1)S(1)}, bf16[16,1024]{1,0:T(8,128)(2,1)S(1)}, u32[]{:S(2)}, u32[]{:S(2)}) collective-permute-start(bf16[16,1024]{1,0:T(8,128)(2,1)S(1)} %output.1.refs_0_.a), channel_id=1, source_target_pairs={{0,3},{1,2},{2,7},{3,6},{4,1},{5,0},{6,5},{7,4},{8,11},{9,10},{10,... | collective-permute-start | bytes 98312 | tf_op jit(solution)/shard_map/ppermute | solution.py:361
  29.7 1.2 %collective-permute-start.12 = (bf16[16,1024]{1,0:T(8,128)(2,1)S(1)}, bf16[16,1024]{1,0:T(8,128)(2,1)S(1)}, u32[]{:S(2)}, u32[]{:S(2)}) collective-permute-start(bf16[16,1024]{1,0:T(8,128)(2,1)S(1)} %get-tuple-element.44), channel_id=1, source_target_pairs={{0,1},{1,0},{2,3},{3,2},{4,5},{5,4},{6,7},{7,6},{8,9},{9,8},{10,11... | collective-permute-start | bytes 98312 | tf_op jit(solution)/shard_map/ppermute | solution.py:375
  30.9 4.3 %collective-permute-start.15 = (bf16[16,1024]{1,0:T(8,128)(2,1)S(1)}, bf16[16,1024]{1,0:T(8,128)(2,1)S(1)}, u32[]{:S(2)}, u32[]{:S(2)}) collective-permute-start(bf16[16,1024]{1,0:T(8,128)(2,1)S(1)} %add_convert_fusion.a), channel_id=1, source_target_pairs={{0,3},{1,2},{2,7},{3,6},{4,1},{5,0},{6,5},{7,4},{8,11},{9,10},{10,... | collective-permute-start | bytes 98312 | tf_op jit(solution)/shard_map/ppermute | solution.py:361
  31.4 5.3 %collective-permute-start.14 = (bf16[16,1024]{1,0:T(8,128)(2,1)S(1)}, bf16[16,1024]{1,0:T(8,128)(2,1)S(1)}, u32[]{:S(2)}, u32[]{:S(2)}) collective-permute-start(bf16[16,1024]{1,0:T(8,128)(2,1)S(1)} %add_convert_fusion.a), channel_id=1, source_target_pairs={{0,7},{1,6},{2,5},{3,4},{4,3},{5,2},{6,1},{7,0},{8,15},{9,14},{10,... | collective-permute-start | bytes 98312 | tf_op jit(solution)/shard_map/ppermute | solution.py:361
  33.1 4.1 %collective-permute-start.13 = (bf16[16,1024]{1,0:T(8,128)(2,1)S(1)}, bf16[16,1024]{1,0:T(8,128)(2,1)S(1)}, u32[]{:S(2)}, u32[]{:S(2)}) collective-permute-start(bf16[16,1024]{1,0:T(8,128)(2,1)S(1)} %add_convert_fusion.a), channel_id=1, source_target_pairs={{0,5},{1,4},{2,1},{3,0},{4,7},{5,6},{6,3},{7,2},{8,13},{9,12},{10,... | collective-permute-start | bytes 98312 | tf_op jit(solution)/shard_map/ppermute | solution.py:361

commit v5 on v4

--- a/solution.py
+++ b/solution.py
@@ -184,6 +184,38 @@
     )
 
 
+def section(shape):
+    return iota(shape, 1) % (HEAD_DIMENSION // 2) // 8
+
+
+def write_packed(out, part):
+    n = part.shape[0] // 2
+    out[0:n] = part[0:n].astype(BF16)
+    stats = part[n:]
+    high = stats.astype(BF16).astype(F32)
+    middle = (stats - high).astype(BF16).astype(F32)
+    place = section(stats.shape)
+    split = jnp.where(place == 0, high, jnp.where(place == 1, middle, stats - high - middle))
+    out[n:] = jnp.where(place == 3, 0.0, split).astype(BF16)
+
+
+def read_packed(ref):
+    n = ref.shape[0] // 2
+    split = ref[n:].astype(F32)
+    lanes = split.shape[1]
+    stats = split + pltpu.roll(split, lanes - 8, 1) + pltpu.roll(split, lanes - 16, 1)
+    lane = iota(split.shape, 1) % HEAD_DIMENSION
+    half = HEAD_DIMENSION // 2
+    peak = jnp.where(lane < 8, stats, 0.0)
+    total = jnp.where((lane >= half) & (lane < half + 8), stats, 0.0)
+    for step in (8, 16):
+        peak = peak + pltpu.roll(peak, step, 1)
+        total = total + pltpu.roll(total, step, 1)
+    peak = peak + pltpu.roll(peak, half, 1)
+    total = total + pltpu.roll(total, lanes - half, 1)
+    return peak, total, ref[0:n].astype(F32)
+
+
 def soft(scores, live):
     masked = jnp.where(live, scores, NEGATIVE)
     peak = jnp.max(masked, axis=-1, keepdims=True)
@@ -236,7 +268,7 @@
     attend_blocks(steps, limits, sibling, [1 - x for x in near], keys, values, store)
     out0[...] = blocks[chip]
     for k, out in ((1, out1), (2, out2), (3, out3)):
-        out[...] = blocks[partner(chip, k)]
+        write_packed(out, blocks[partner(chip, k)])
 
 
 def fresh_part(requests, steps, own, sibling, after, out):
@@ -276,7 +308,9 @@
 
 def join_kernel(order, a, b, c, d, fetched, out):
     a, b, c, d = sort_chips(order, a, (b, c, d))
-    peak, total, summed = join(join(read_part(a), read_part(d)), join(read_part(b), read_part(c)))
+    peak, total, summed = join(
+        join(read_part(a), read_packed(d)), join(read_packed(b), read_packed(c))
+    )
     n = summed.shape[0]
     out[0:n] = summed
     out[n:] = pack_stats(peak, total)
@@ -430,7 +464,7 @@
     )
     parts = call(
         functools.partial(attend_sibling_kernel, steps),
-        [((2 * rows, 128), F32)] * chips,
+        [((2 * rows, 128), F32)] + [((2 * rows, 128), BF16)] * (chips - 1),
         [limits, sibling, keys, values, blocks_own],
         "attend",
         cost=COST[1],

time: 38 us -> 37.7 us (level)
  starting transfers between devices: 18.2 us -> 17.8 us
    ppermute x12, starting transfers between devices: 17.2 us -> 16.6 us  [other_chip(): lax.ppermute(x, 'tp', [(i, 2 * to[i // 2] + 1 - i % 2) for i in range(dev...]
  transfers between devices with their start and end apart: 16 -> 16, of which waited for: 9 -> 8; matrix products, arithmetic and copies ran while one was open for 0% -> 0% of each run, Pallas kernels for 22% -> 22%
where the time goes in v5:
time: 37.7 us; the launch traced here: 37.6 us
  starting transfers between devices  17.8 us (47%)
  Pallas kernels  13.1 us (35%)
  waiting for transfers between devices  6.6 us (18%)
    ppermute x12, starting transfers between devices, other_chip(): lax.ppermute(x, 'tp', [(i, 2 * to[i // 2] + 1 - i % 2) for i in range(dev...  16.6 us
    pallas_call x11, Pallas kernels, call(): pl.pallas_call(kernel, out_shape=[jax.ShapeDtypeStruct(s, d) if hbm_out e...  13.1 us
    ppermute x12, waiting for transfers between devices, other_chip(): lax.ppermute(x, 'tp', [(i, 2 * to[i // 2] + 1 - i % 2) for i in range(dev...  3.88 us
    ppermute x4, waiting for transfers between devices, other_core(): return lax.ppermute(x, 'tp', [(i, i ^ 1) for i in range(devices)])  2.72 us
    ppermute x4, starting transfers between devices, other_core(): return lax.ppermute(x, 'tp', [(i, i ^ 1) for i in range(devices)])  1.17 us
  transfers between devices with their start and end apart: 16, of which 8 were waited for; matrix products, arithmetic and copies ran while one was open for 0% of the time, Pallas kernels for 22%

profile of v5, /device:TPU:0, one launch (start us, length us, event | category | flops | bytes accessed | tf_op | source)
XLA Modules:
  0.0 37.6 jit_solution(901047690300841886)
XLA Ops:
  0.0 1.5 %project.1 = (bf16[32,128]{1,0:T(8,128)(2,1)S(1)}, s32[4,8,128]{2,1,0:T(8,128)S(1)}, f32[16,1024]{1,0:T(8,128)S(1)}) custom-call(s32[4]{0:T(128)} %lengths_in.1, bf16[4,4,1024]{2,1,0:T(4,128)(2,1)} %hidden_in.1, bf16[256,1024]{1,0:T(8,128)(2,1)} %weight_in.1), custom_call_target="tpu_custom_call" | custom-call | bytes 8000000 | tf_op jit(solution)/shard_map/project/pallas_call | solution.py:41
  1.5 4.6 %collective-permute-start.2 = (bf16[32,128]{1,0:T(8,128)(2,1)S(1)}, bf16[32,128]{1,0:T(8,128)(2,1)S(1)}, u32[]{:S(2)}, u32[]{:S(2)}) collective-permute-start(bf16[32,128]{1,0:T(8,128)(2,1)S(1)} %get-tuple-element.27.refs_0_.a), channel_id=1, source_target_pairs={{0,7},{1,6},{2,5},{3,4},{4,3},{5,2},{6,1},{7,0},{8,15},{9,14},{10,... | collective-permute-start | bytes 24584 | tf_op jit(solution)/shard_map/ppermute | solution.py:395
  6.1 0.0 collective-permute-start.1
  6.1 1.7 %collective-permute-start = (bf16[32,128]{1,0:T(8,128)(2,1)S(1)}, bf16[32,128]{1,0:T(8,128)(2,1)S(1)}, u32[]{:S(2)}, u32[]{:S(2)}) collective-permute-start(bf16[32,128]{1,0:T(8,128)(2,1)S(1)} %get-tuple-element.27.refs_0_.a), channel_id=1, source_target_pairs={{0,3},{1,2},{2,7},{3,6},{4,1},{5,0},{6,5},{7,4},{8,11},{9,10},{10,... | collective-permute-start | bytes 24584 | tf_op jit(solution)/shard_map/ppermute | solution.py:395
  7.8 1.5 %fetch_cache.1 = (bf16[4,128,512]{2,1,0:T(8,128)(2,1)S(1)}, bf16[4,128,512]{2,1,0:T(8,128)(2,1)S(1)}, bf16[1,128,1024]{2,1,0:T(8,128)(2,1)S(1)}, s32[1,4,4,8]{3,2,1,0:T(4,128)S(1)}, s32[1,4,4,8]{3,2,1,0:T(4,128)S(1)}) custom-call(bf16[32,128]{1,0:T(8,128)(2,1)S(1)} %get-tuple-element.27.refs_0_.a, bf16[4,128,512]{2,1,0:T(8,128)(2,1)} %refs_1_.2, ...), custom_call_target="tpu_custom_call" | custom-call | bytes 1311232 | tf_op jit(solution)/shard_map/fetch_cache/pallas_call | solution.py:41
  9.3 0.0 collective-permute-done.2.d
  9.3 0.0 collective-permute-done.1.c
  9.3 0.8 %collective-permute-done.b = bf16[32,128]{1,0:T(8,128)(2,1)S(1)} collective-permute-done((bf16[32,128]{1,0:T(8,128)(2,1)S(1)}, bf16[32,128]{1,0:T(8,128)(2,1)S(1)}, u32[]{:S(2)}, u32[]{:S(2)}) %collective-permute-start) | collective-permute-done | bytes 8224 | tf_op jit(solution)/shard_map/ppermute | solution.py:395
  10.1 0.6 %collective-permute-start.8 = (bf16[128,1024]{1,0:T(8,128)(2,1)S(1)}, bf16[128,1024]{1,0:T(8,128)(2,1)S(1)}, u32[]{:S(2)}, u32[]{:S(2)}) collective-permute-start(bf16[128,1024]{1,0:T(8,128)(2,1)S(1)} %bitcast.6), channel_id=1, source_target_pairs={{0,1},{1,0},{2,3},{3,2},{4,5},{5,4},{6,7},{7,6},{8,9},{9,8},{10,11... | collective-permute-start | bytes 786440 | tf_op jit(solution)/shard_map/ppermute | solution.py:409
  10.7 0.1 collective-permute-start.3
  10.8 0.4 %attend_own.1.blocks_own = f32[2,64,128]{2,1,0:T(8,128)S(1)} custom-call(s32[4,8,128]{2,1,0:T(8,128)S(1)} %get-tuple-element.26.limits, bf16[4,32,128]{2,1,0:T(8,128)(2,1)S(1)} %get-tuple-element.29.own.refs_0_, bf16[4,128,512]{2,1,0:T(8,128)(2,1)S(1)} %get-tuple-element.30.keys, bf16[4,128,512]{2,1,0:T(8,128)(2,1)S(1)} %get-tuple-element.31.values), custom_call_target="tpu_custom_call" | custom-call | bytes 6000000 | tf_op jit(solution)/shard_map/attend_own/pallas_call | solution.py:41
  11.2 0.7 %collective-permute-done.3.sibling.refs_1_ = bf16[4,32,128]{2,1,0:T(8,128)(2,1)S(1)} collective-permute-done((bf16[4,32,128]{2,1,0:T(8,128)(2,1)S(1)}, bf16[4,32,128]{2,1,0:T(8,128)(2,1)S(1)}, u32[]{:S(2)}, u32[]{:S(2)}) %collective-permute-start.3) | collective-permute-done | bytes 32800 | tf_op jit(solution)/shard_map/ppermute | solution.py:409
  11.9 0.5 %attend.1 = (f32[64,128]{1,0:T(8,128)S(1)}, bf16[64,128]{1,0:T(8,128)(2,1)S(1)}, bf16[64,128]{1,0:T(8,128)(2,1)S(1)}, bf16[64,128]{1,0:T(8,128)(2,1)S(1)}) custom-call(s32[4,8,128]{2,1,0:T(8,128)S(1)} %get-tuple-element.26.limits, bf16[4,32,128]{2,1,0:T(8,128)(2,1)S(1)} %collective-permute-done.3.sibling.refs_1_, ...), custom_call_target="tpu_custom_call" | custom-call | bytes 6000000 | tf_op jit(solution)/shard_map/attend/pallas_call | solution.py:41
  12.4 1.7 %collective-permute-start.4 = (bf16[64,128]{1,0:T(8,128)(2,1)S(1)}, bf16[64,128]{1,0:T(8,128)(2,1)S(1)}, u32[]{:S(2)}, u32[]{:S(2)}) collective-permute-start(bf16[64,128]{1,0:T(8,128)(2,1)S(1)} %get-tuple-element.33), channel_id=1, source_target_pairs={{0,7},{1,6},{2,5},{3,4},{4,3},{5,2},{6,1},{7,0},{8,15},{9,14},{10,... | collective-permute-start | bytes 49160 | tf_op jit(solution)/shard_map/ppermute | solution.py:395
  14.1 0.7 %collective-permute-start.5 = (bf16[64,128]{1,0:T(8,128)(2,1)S(1)}, bf16[64,128]{1,0:T(8,128)(2,1)S(1)}, u32[]{:S(2)}, u32[]{:S(2)}) collective-permute-start(bf16[64,128]{1,0:T(8,128)(2,1)S(1)} %get-tuple-element.34), channel_id=1, source_target_pairs={{0,5},{1,4},{2,1},{3,0},{4,7},{5,6},{6,3},{7,2},{8,13},{9,12},{10,... | collective-permute-start | bytes 49160 | tf_op jit(solution)/shard_map/ppermute | solution.py:395
  14.8 1.0 %collective-permute-start.6 = (bf16[64,128]{1,0:T(8,128)(2,1)S(1)}, bf16[64,128]{1,0:T(8,128)(2,1)S(1)}, u32[]{:S(2)}, u32[]{:S(2)}) collective-permute-start(bf16[64,128]{1,0:T(8,128)(2,1)S(1)} %get-tuple-element.35), channel_id=1, source_target_pairs={{0,3},{1,2},{2,7},{3,6},{4,1},{5,0},{6,5},{7,4},{8,11},{9,10},{10,... | collective-permute-start | bytes 49160 | tf_op jit(solution)/shard_map/ppermute | solution.py:395
  15.9 2.9 %fetch_b.1 = (bf16[3,1024,1024]{2,1,0:T(8,128)(2,1)S(1)}, f32[64,128]{1,0:T(8,128)S(1)}) custom-call(bf16[4,32,128]{2,1,0:T(8,128)(2,1)S(1)} %get-tuple-element.29.own.refs_0_, bf16[4,32,128]{2,1,0:T(8,128)(2,1)S(1)} %collective-permute-done.3.sibling.refs_1_, f32[64,128]{1,0:T(8,128)S(1)} %get-tuple-element.32.refs_2_.a, bf16[4,1024,1024]{2,1,0:T(8,128)(2,1)} %refs_1_.3), custom_call_target="tpu_custom_call" | custom-call | bytes 6291456 | tf_op jit(solution)/shard_map/fetch_b/pallas_call | solution.py:41
  18.8 0.0 collective-permute-done.4.b
  18.8 0.0 collective-permute-done.5.c
  18.8 0.1 collective-permute-done.6.d
  18.9 0.3 join.1.own
  19.2 0.3 collective-permute-start.7
  19.6 0.9 %collective-permute-done.7.sibling = f32[64,128]{1,0:T(8,128)S(1)} collective-permute-done((f32[64,128]{1,0:T(8,128)S(1)}, f32[64,128]{1,0:T(8,128)S(1)}, u32[]{:S(2)}, u32[]{:S(2)}) %collective-permute-start.7) | collective-permute-done | bytes 32800 | tf_op jit(solution)/shard_map/ppermute | solution.py:409
  20.5 0.0 collective-permute-done.8.sibling_weight
  20.5 0.3 output.1.refs_0_.a
  20.8 1.9 %collective-permute-start.11 = (bf16[16,1024]{1,0:T(8,128)(2,1)S(1)}, bf16[16,1024]{1,0:T(8,128)(2,1)S(1)}, u32[]{:S(2)}, u32[]{:S(2)}) collective-permute-start(bf16[16,1024]{1,0:T(8,128)(2,1)S(1)} %output.1.refs_0_.a), channel_id=1, source_target_pairs={{0,7},{1,6},{2,5},{3,4},{4,3},{5,2},{6,1},{7,0},{8,15},{9,14},{10,... | collective-permute-start | bytes 98312 | tf_op jit(solution)/shard_map/ppermute | solution.py:395
  22.7 0.0 collective-permute-start.10
  22.7 1.7 %collective-permute-start.9 = (bf16[16,1024]{1,0:T(8,128)(2,1)S(1)}, bf16[16,1024]{1,0:T(8,128)(2,1)S(1)}, u32[]{:S(2)}, u32[]{:S(2)}) collective-permute-start(bf16[16,1024]{1,0:T(8,128)(2,1)S(1)} %output.1.refs_0_.a), channel_id=1, source_target_pairs={{0,3},{1,2},{2,7},{3,6},{4,1},{5,0},{6,5},{7,4},{8,11},{9,10},{10,... | collective-permute-start | bytes 98312 | tf_op jit(solution)/shard_map/ppermute | solution.py:395
  24.4 2.8 %fetch_c.1 = (bf16[1,1024,1024]{2,1,0:T(8,128)(2,1)S(1)}, bf16[4,512,1024]{2,1,0:T(8,128)(2,1)S(1)}) custom-call(bf16[16,1024]{1,0:T(8,128)(2,1)S(1)} %output.1.refs_0_.a, bf16[4,1024,1024]{2,1,0:T(8,128)(2,1)} %refs_1_.3, bf16[4,512,1024]{2,1,0:T(8,128)(2,1)} %refs_2_.3), custom_call_target="tpu_custom_call" | custom-call | bytes 6291456 | tf_op jit(solution)/shard_map/fetch_c/pallas_call | solution.py:41
  27.3 0.0 collective-permute-done.11.d
  27.3 0.0 collective-permute-done.10.c
  27.3 0.5 %collective-permute-done.9.b = bf16[16,1024]{1,0:T(8,128)(2,1)S(1)} collective-permute-done((bf16[16,1024]{1,0:T(8,128)(2,1)S(1)}, bf16[16,1024]{1,0:T(8,128)(2,1)S(1)}, u32[]{:S(2)}, u32[]{:S(2)}) %collective-permute-start.9) | collective-permute-done | bytes 32800 | tf_op jit(solution)/shard_map/ppermute | solution.py:395
  27.8 2.2 %experts.1 = (bf16[16,1024]{1,0:T(8,128)(2,1)S(1)}, f32[16,1024]{1,0:T(8,128)S(1)}) custom-call(f32[16,1024]{1,0:T(8,128)S(1)} %get-tuple-element.25.inputs, bf16[16,1024]{1,0:T(8,128)(2,1)S(1)} %output.1.refs_0_.a, bf16[16,1024]{1,0:T(8,128)(2,1)S(1)} %collective-permute-done.9.b, bf16[16,1024]{1,0:T(8,128)(2,1)S(1)} %collective-permute-done.10.c, ...), custom_call_target="tpu_custom_call" | custom-call | bytes 12000000 | tf_op jit(solution)/shard_map/experts/pallas_call | solution.py:41
  29.9 0.1 collective-permute-start.12
  30.1 1.1 %collective-permute-done.12 = bf16[16,1024]{1,0:T(8,128)(2,1)S(1)} collective-permute-done((bf16[16,1024]{1,0:T(8,128)(2,1)S(1)}, bf16[16,1024]{1,0:T(8,128)(2,1)S(1)}, u32[]{:S(2)}, u32[]{:S(2)}) %collective-permute-start.12) | collective-permute-done | bytes 32800 | tf_op jit(solution)/shard_map/ppermute | solution.py:409
  31.2 0.5 %collective-permute-start.15 = (bf16[16,1024]{1,0:T(8,128)(2,1)S(1)}, bf16[16,1024]{1,0:T(8,128)(2,1)S(1)}, u32[]{:S(2)}, u32[]{:S(2)}) collective-permute-start(bf16[16,1024]{1,0:T(8,128)(2,1)S(1)} %add_convert_fusion.a), channel_id=1, source_target_pairs={{0,3},{1,2},{2,7},{3,6},{4,1},{5,0},{6,5},{7,4},{8,11},{9,10},{10,... | collective-permute-start | bytes 98312 | tf_op jit(solution)/shard_map/ppermute | solution.py:395
  31.7 1.4 %collective-permute-start.14 = (bf16[16,1024]{1,0:T(8,128)(2,1)S(1)}, bf16[16,1024]{1,0:T(8,128)(2,1)S(1)}, u32[]{:S(2)}, u32[]{:S(2)}) collective-permute-start(bf16[16,1024]{1,0:T(8,128)(2,1)S(1)} %add_convert_fusion.a), channel_id=1, source_target_pairs={{0,7},{1,6},{2,5},{3,4},{4,3},{5,2},{6,1},{7,0},{8,15},{9,14},{10,... | collective-permute-start | bytes 98312 | tf_op jit(solution)/shard_map/ppermute | solution.py:395
  33.1 1.4 %collective-permute-start.13 = (bf16[16,1024]{1,0:T(8,128)(2,1)S(1)}, bf16[16,1024]{1,0:T(8,128)(2,1)S(1)}, u32[]{:S(2)}, u32[]{:S(2)}) collective-permute-start(bf16[16,1024]{1,0:T(8,128)(2,1)S(1)} %add_convert_fusion.a), channel_id=1, source_target_pairs={{0,5},{1,4},{2,1},{3,0},{4,7},{5,6},{6,3},{7,2},{8,13},{9,12},{10,... | collective-permute-start | bytes 98312 | tf_op jit(solution)/shard_map/ppermute | solution.py:395
  34.4 1.0 %collective-permute-done.15.d = bf16[16,1024]{1,0:T(8,128)(2,1)S(1)} collective-permute-done((bf16[16,1024]{1,0:T(8,128)(2,1)S(1)}, bf16[16,1024]{1,0:T(8,128)(2,1)S(1)}, u32[]{:S(2)}, u32[]{:S(2)}) %collective-permute-start.15) | collective-permute-done | bytes 32800 | tf_op jit(solution)/shard_map/ppermute | solution.py:395
  35.5 1.5 %collective-permute-done.14.c = bf16[16,1024]{1,0:T(8,128)(2,1)S(1)} collective-permute-done((bf16[16,1024]{1,0:T(8,128)(2,1)S(1)}, bf16[16,1024]{1,0:T(8,128)(2,1)S(1)}, u32[]{:S(2)}, u32[]{:S(2)}) %collective-permute-start.14) | collective-permute-done | bytes 32800 | tf_op jit(solution)/shard_map/ppermute | solution.py:395
  36.9 0.0 collective-permute-done.13.b
  36.9 0.6 %final.1 = bf16[4,4,1024]{2,1,0:T(4,128)(2,1)} custom-call(f32[16,1024]{1,0:T(8,128)S(1)} %get-tuple-element.43.residual, bf16[16,1024]{1,0:T(8,128)(2,1)S(1)} %add_convert_fusion.a, bf16[16,1024]{1,0:T(8,128)(2,1)S(1)} %collective-permute-done.13.b, bf16[16,1024]{1,0:T(8,128)(2,1)S(1)} %collective-permute-done.14.c, ...), custom_call_target="tpu_custom_call" | custom-call | tf_op jit(solution)/shard_map/final/pallas_call | solution.py:41
  (2 shorter events, 0.0 us)
Async XLA Ops:
  1.5 7.8 %collective-permute-start.2 = (bf16[32,128]{1,0:T(8,128)(2,1)S(1)}, bf16[32,128]{1,0:T(8,128)(2,1)S(1)}, u32[]{:S(2)}, u32[]{:S(2)}) collective-permute-start(bf16[32,128]{1,0:T(8,128)(2,1)S(1)} %get-tuple-element.27.refs_0_.a), channel_id=1, source_target_pairs={{0,7},{1,6},{2,5},{3,4},{4,3},{5,2},{6,1},{7,0},{8,15},{9,14},{10,... | collective-permute-start | bytes 24584 | tf_op jit(solution)/shard_map/ppermute | solution.py:395
  6.1 3.2 %collective-permute-start.1 = (bf16[32,128]{1,0:T(8,128)(2,1)S(1)}, bf16[32,128]{1,0:T(8,128)(2,1)S(1)}, u32[]{:S(2)}, u32[]{:S(2)}) collective-permute-start(bf16[32,128]{1,0:T(8,128)(2,1)S(1)} %get-tuple-element.27.refs_0_.a), channel_id=1, source_target_pairs={{0,5},{1,4},{2,1},{3,0},{4,7},{5,6},{6,3},{7,2},{8,13},{9,12},{10,... | collective-permute-start | bytes 24584 | tf_op jit(solution)/shard_map/ppermute | solution.py:395
  6.1 4.0 %collective-permute-start = (bf16[32,128]{1,0:T(8,128)(2,1)S(1)}, bf16[32,128]{1,0:T(8,128)(2,1)S(1)}, u32[]{:S(2)}, u32[]{:S(2)}) collective-permute-start(bf16[32,128]{1,0:T(8,128)(2,1)S(1)} %get-tuple-element.27.refs_0_.a), channel_id=1, source_target_pairs={{0,3},{1,2},{2,7},{3,6},{4,1},{5,0},{6,5},{7,4},{8,11},{9,10},{10,... | collective-permute-start | bytes 24584 | tf_op jit(solution)/shard_map/ppermute | solution.py:395
  10.1 10.4 %collective-permute-start.8 = (bf16[128,1024]{1,0:T(8,128)(2,1)S(1)}, bf16[128,1024]{1,0:T(8,128)(2,1)S(1)}, u32[]{:S(2)}, u32[]{:S(2)}) collective-permute-start(bf16[128,1024]{1,0:T(8,128)(2,1)S(1)} %bitcast.6), channel_id=1, source_target_pairs={{0,1},{1,0},{2,3},{3,2},{4,5},{5,4},{6,7},{7,6},{8,9},{9,8},{10,11... | collective-permute-start | bytes 786440 | tf_op jit(solution)/shard_map/ppermute | solution.py:409
  10.7 1.2 %collective-permute-start.3 = (bf16[4,32,128]{2,1,0:T(8,128)(2,1)S(1)}, bf16[4,32,128]{2,1,0:T(8,128)(2,1)S(1)}, u32[]{:S(2)}, u32[]{:S(2)}) collective-permute-start(bf16[4,32,128]{2,1,0:T(8,128)(2,1)S(1)} %get-tuple-element.29.own.refs_0_), channel_id=1, source_target_pairs={{0,1},{1,0},{2,3},{3,2},{4,5},{5,4},{6,7},{7,6},{8,9},{9,8},{10,11... | collective-permute-start | bytes 98312 | tf_op jit(solution)/shard_map/ppermute | solution.py:409
  12.4 6.4 %collective-permute-start.4 = (bf16[64,128]{1,0:T(8,128)(2,1)S(1)}, bf16[64,128]{1,0:T(8,128)(2,1)S(1)}, u32[]{:S(2)}, u32[]{:S(2)}) collective-permute-start(bf16[64,128]{1,0:T(8,128)(2,1)S(1)} %get-tuple-element.33), channel_id=1, source_target_pairs={{0,7},{1,6},{2,5},{3,4},{4,3},{5,2},{6,1},{7,0},{8,15},{9,14},{10,... | collective-permute-start | bytes 49160 | tf_op jit(solution)/shard_map/ppermute | solution.py:395
  14.1 4.7 %collective-permute-start.5 = (bf16[64,128]{1,0:T(8,128)(2,1)S(1)}, bf16[64,128]{1,0:T(8,128)(2,1)S(1)}, u32[]{:S(2)}, u32[]{:S(2)}) collective-permute-start(bf16[64,128]{1,0:T(8,128)(2,1)S(1)} %get-tuple-element.34), channel_id=1, source_target_pairs={{0,5},{1,4},{2,1},{3,0},{4,7},{5,6},{6,3},{7,2},{8,13},{9,12},{10,... | collective-permute-start | bytes 49160 | tf_op jit(solution)/shard_map/ppermute | solution.py:395
  14.8 4.1 %collective-permute-start.6 = (bf16[64,128]{1,0:T(8,128)(2,1)S(1)}, bf16[64,128]{1,0:T(8,128)(2,1)S(1)}, u32[]{:S(2)}, u32[]{:S(2)}) collective-permute-start(bf16[64,128]{1,0:T(8,128)(2,1)S(1)} %get-tuple-element.35), channel_id=1, source_target_pairs={{0,3},{1,2},{2,7},{3,6},{4,1},{5,0},{6,5},{7,4},{8,11},{9,10},{10,... | collective-permute-start | bytes 49160 | tf_op jit(solution)/shard_map/ppermute | solution.py:395
  19.2 1.3 %collective-permute-start.7 = (f32[64,128]{1,0:T(8,128)S(1)}, f32[64,128]{1,0:T(8,128)S(1)}, u32[]{:S(2)}, u32[]{:S(2)}) collective-permute-start(f32[64,128]{1,0:T(8,128)S(1)} %join.1.own), channel_id=1, source_target_pairs={{0,1},{1,0},{2,3},{3,2},{4,5},{5,4},{6,7},{7,6},{8,9},{9,8},{10,11... | collective-permute-start | bytes 98312 | tf_op jit(solution)/shard_map/ppermute | solution.py:409
  20.8 6.5 %collective-permute-start.11 = (bf16[16,1024]{1,0:T(8,128)(2,1)S(1)}, bf16[16,1024]{1,0:T(8,128)(2,1)S(1)}, u32[]{:S(2)}, u32[]{:S(2)}) collective-permute-start(bf16[16,1024]{1,0:T(8,128)(2,1)S(1)} %output.1.refs_0_.a), channel_id=1, source_target_pairs={{0,7},{1,6},{2,5},{3,4},{4,3},{5,2},{6,1},{7,0},{8,15},{9,14},{10,... | collective-permute-start | bytes 98312 | tf_op jit(solution)/shard_map/ppermute | solution.py:395
  22.7 4.6 %collective-permute-start.10 = (bf16[16,1024]{1,0:T(8,128)(2,1)S(1)}, bf16[16,1024]{1,0:T(8,128)(2,1)S(1)}, u32[]{:S(2)}, u32[]{:S(2)}) collective-permute-start(bf16[16,1024]{1,0:T(8,128)(2,1)S(1)} %output.1.refs_0_.a), channel_id=1, source_target_pairs={{0,5},{1,4},{2,1},{3,0},{4,7},{5,6},{6,3},{7,2},{8,13},{9,12},{10,... | collective-permute-start | bytes 98312 | tf_op jit(solution)/shard_map/ppermute | solution.py:395
  22.7 5.1 %collective-permute-start.9 = (bf16[16,1024]{1,0:T(8,128)(2,1)S(1)}, bf16[16,1024]{1,0:T(8,128)(2,1)S(1)}, u32[]{:S(2)}, u32[]{:S(2)}) collective-permute-start(bf16[16,1024]{1,0:T(8,128)(2,1)S(1)} %output.1.refs_0_.a), channel_id=1, source_target_pairs={{0,3},{1,2},{2,7},{3,6},{4,1},{5,0},{6,5},{7,4},{8,11},{9,10},{10,... | collective-permute-start | bytes 98312 | tf_op jit(solution)/shard_map/ppermute | solution.py:395
  29.9 1.2 %collective-permute-start.12 = (bf16[16,1024]{1,0:T(8,128)(2,1)S(1)}, bf16[16,1024]{1,0:T(8,128)(2,1)S(1)}, u32[]{:S(2)}, u32[]{:S(2)}) collective-permute-start(bf16[16,1024]{1,0:T(8,128)(2,1)S(1)} %get-tuple-element.44), channel_id=1, source_target_pairs={{0,1},{1,0},{2,3},{3,2},{4,5},{5,4},{6,7},{7,6},{8,9},{9,8},{10,11... | collective-permute-start | bytes 98312 | tf_op jit(solution)/shard_map/ppermute | solution.py:409
  31.2 4.3 %collective-permute-start.15 = (bf16[16,1024]{1,0:T(8,128)(2,1)S(1)}, bf16[16,1024]{1,0:T(8,128)(2,1)S(1)}, u32[]{:S(2)}, u32[]{:S(2)}) collective-permute-start(bf16[16,1024]{1,0:T(8,128)(2,1)S(1)} %add_convert_fusion.a), channel_id=1, source_target_pairs={{0,3},{1,2},{2,7},{3,6},{4,1},{5,0},{6,5},{7,4},{8,11},{9,10},{10,... | collective-permute-start | bytes 98312 | tf_op jit(solution)/shard_map/ppermute | solution.py:395
  31.7 5.3 %collective-permute-start.14 = (bf16[16,1024]{1,0:T(8,128)(2,1)S(1)}, bf16[16,1024]{1,0:T(8,128)(2,1)S(1)}, u32[]{:S(2)}, u32[]{:S(2)}) collective-permute-start(bf16[16,1024]{1,0:T(8,128)(2,1)S(1)} %add_convert_fusion.a), channel_id=1, source_target_pairs={{0,7},{1,6},{2,5},{3,4},{4,3},{5,2},{6,1},{7,0},{8,15},{9,14},{10,... | collective-permute-start | bytes 98312 | tf_op jit(solution)/shard_map/ppermute | solution.py:395
  33.1 3.9 %collective-permute-start.13 = (bf16[16,1024]{1,0:T(8,128)(2,1)S(1)}, bf16[16,1024]{1,0:T(8,128)(2,1)S(1)}, u32[]{:S(2)}, u32[]{:S(2)}) collective-permute-start(bf16[16,1024]{1,0:T(8,128)(2,1)S(1)} %add_convert_fusion.a), channel_id=1, source_target_pairs={{0,5},{1,4},{2,1},{3,0},{4,7},{5,6},{6,3},{7,2},{8,13},{9,12},{10,... | collective-permute-start | bytes 98312 | tf_op jit(solution)/shard_map/ppermute | solution.py:395

commit v6 on v5

--- a/solution.py
+++ b/solution.py
@@ -230,9 +230,10 @@
     scale = HEAD_DIMENSION**-0.5
     pairs = [(s, r) for s in range(2) for r in range(requests)]
     columns = [pl.ds(pl.multiple_of((2 * s + cores[s]) * 128, 128), 128) for s in range(2)]
+    queries = [heads[s].astype(F32) * scale for s in range(2)]
     scores = []
     for s, r in pairs:
-        q = spread(heads[s, r * rows : (r + 1) * rows].astype(F32) * scale, GROUP)
+        q = spread(queries[s][r * rows : (r + 1) * rows], GROUP)
         scores.append(
             lax.dot_general(q, keys[r, :, columns[s]], (((1,), (1,)), ((), ())), preferred_element_type=F32)
         )

time: 37.7 us -> 37.7 us (level)
  no operation moved by 1% of the time
where the time goes in v6:
time: 37.7 us; the launch traced here: 37.6 us
  starting transfers between devices  17.8 us (47%)
  Pallas kernels  13.1 us (35%)
  waiting for transfers between devices  6.6 us (18%)
    ppermute x12, starting transfers between devices, other_chip(): lax.ppermute(x, 'tp', [(i, 2 * to[i // 2] + 1 - i % 2) for i in range(dev...  16.6 us
    pallas_call x11, Pallas kernels, call(): pl.pallas_call(kernel, out_shape=[jax.ShapeDtypeStruct(s, d) if hbm_out e...  13.1 us
    ppermute x12, waiting for transfers between devices, other_chip(): lax.ppermute(x, 'tp', [(i, 2 * to[i // 2] + 1 - i % 2) for i in range(dev...  3.88 us
    ppermute x4, waiting for transfers between devices, other_core(): return lax.ppermute(x, 'tp', [(i, i ^ 1) for i in range(devices)])  2.72 us
    ppermute x4, starting transfers between devices, other_core(): return lax.ppermute(x, 'tp', [(i, i ^ 1) for i in range(devices)])  1.17 us
  transfers between devices with their start and end apart: 16, of which 8 were waited for; matrix products, arithmetic and copies ran while one was open for 0% of the time, Pallas kernels for 22%

profile of v6, /device:TPU:0, one launch (start us, length us, event | category | flops | bytes accessed | tf_op | source)
XLA Modules:
  0.0 37.6 jit_solution(901047690300841886)
XLA Ops:
  0.0 1.5 %project.1 = (bf16[32,128]{1,0:T(8,128)(2,1)S(1)}, s32[4,8,128]{2,1,0:T(8,128)S(1)}, f32[16,1024]{1,0:T(8,128)S(1)}) custom-call(s32[4]{0:T(128)} %lengths_in.1, bf16[4,4,1024]{2,1,0:T(4,128)(2,1)} %hidden_in.1, bf16[256,1024]{1,0:T(8,128)(2,1)} %weight_in.1), custom_call_target="tpu_custom_call" | custom-call | bytes 8000000 | tf_op jit(solution)/shard_map/project/pallas_call | solution.py:41
  1.5 4.6 %collective-permute-start.2 = (bf16[32,128]{1,0:T(8,128)(2,1)S(1)}, bf16[32,128]{1,0:T(8,128)(2,1)S(1)}, u32[]{:S(2)}, u32[]{:S(2)}) collective-permute-start(bf16[32,128]{1,0:T(8,128)(2,1)S(1)} %get-tuple-element.27.refs_0_.a), channel_id=1, source_target_pairs={{0,7},{1,6},{2,5},{3,4},{4,3},{5,2},{6,1},{7,0},{8,15},{9,14},{10,... | collective-permute-start | bytes 24584 | tf_op jit(solution)/shard_map/ppermute | solution.py:396
  6.1 0.0 collective-permute-start.1
  6.1 1.7 %collective-permute-start = (bf16[32,128]{1,0:T(8,128)(2,1)S(1)}, bf16[32,128]{1,0:T(8,128)(2,1)S(1)}, u32[]{:S(2)}, u32[]{:S(2)}) collective-permute-start(bf16[32,128]{1,0:T(8,128)(2,1)S(1)} %get-tuple-element.27.refs_0_.a), channel_id=1, source_target_pairs={{0,3},{1,2},{2,7},{3,6},{4,1},{5,0},{6,5},{7,4},{8,11},{9,10},{10,... | collective-permute-start | bytes 24584 | tf_op jit(solution)/shard_map/ppermute | solution.py:396
  7.8 1.5 %fetch_cache.1 = (bf16[4,128,512]{2,1,0:T(8,128)(2,1)S(1)}, bf16[4,128,512]{2,1,0:T(8,128)(2,1)S(1)}, bf16[1,128,1024]{2,1,0:T(8,128)(2,1)S(1)}, s32[1,4,4,8]{3,2,1,0:T(4,128)S(1)}, s32[1,4,4,8]{3,2,1,0:T(4,128)S(1)}) custom-call(bf16[32,128]{1,0:T(8,128)(2,1)S(1)} %get-tuple-element.27.refs_0_.a, bf16[4,128,512]{2,1,0:T(8,128)(2,1)} %refs_1_.2, ...), custom_call_target="tpu_custom_call" | custom-call | bytes 1311232 | tf_op jit(solution)/shard_map/fetch_cache/pallas_call | solution.py:41
  9.3 0.0 collective-permute-done.2.d
  9.3 0.0 collective-permute-done.1.c
  9.3 0.8 %collective-permute-done.b = bf16[32,128]{1,0:T(8,128)(2,1)S(1)} collective-permute-done((bf16[32,128]{1,0:T(8,128)(2,1)S(1)}, bf16[32,128]{1,0:T(8,128)(2,1)S(1)}, u32[]{:S(2)}, u32[]{:S(2)}) %collective-permute-start) | collective-permute-done | bytes 8224 | tf_op jit(solution)/shard_map/ppermute | solution.py:396
  10.1 0.6 %collective-permute-start.8 = (bf16[128,1024]{1,0:T(8,128)(2,1)S(1)}, bf16[128,1024]{1,0:T(8,128)(2,1)S(1)}, u32[]{:S(2)}, u32[]{:S(2)}) collective-permute-start(bf16[128,1024]{1,0:T(8,128)(2,1)S(1)} %bitcast.6), channel_id=1, source_target_pairs={{0,1},{1,0},{2,3},{3,2},{4,5},{5,4},{6,7},{7,6},{8,9},{9,8},{10,11... | collective-permute-start | bytes 786440 | tf_op jit(solution)/shard_map/ppermute | solution.py:410
  10.7 0.1 collective-permute-start.3
  10.8 0.4 %attend_own.1.blocks_own = f32[2,64,128]{2,1,0:T(8,128)S(1)} custom-call(s32[4,8,128]{2,1,0:T(8,128)S(1)} %get-tuple-element.26.limits, bf16[4,32,128]{2,1,0:T(8,128)(2,1)S(1)} %get-tuple-element.29.own.refs_0_, bf16[4,128,512]{2,1,0:T(8,128)(2,1)S(1)} %get-tuple-element.30.keys, bf16[4,128,512]{2,1,0:T(8,128)(2,1)S(1)} %get-tuple-element.31.values), custom_call_target="tpu_custom_call" | custom-call | bytes 6000000 | tf_op jit(solution)/shard_map/attend_own/pallas_call | solution.py:41
  11.2 0.7 %collective-permute-done.3.sibling.refs_1_ = bf16[4,32,128]{2,1,0:T(8,128)(2,1)S(1)} collective-permute-done((bf16[4,32,128]{2,1,0:T(8,128)(2,1)S(1)}, bf16[4,32,128]{2,1,0:T(8,128)(2,1)S(1)}, u32[]{:S(2)}, u32[]{:S(2)}) %collective-permute-start.3) | collective-permute-done | bytes 32800 | tf_op jit(solution)/shard_map/ppermute | solution.py:410
  11.9 0.5 %attend.1 = (f32[64,128]{1,0:T(8,128)S(1)}, bf16[64,128]{1,0:T(8,128)(2,1)S(1)}, bf16[64,128]{1,0:T(8,128)(2,1)S(1)}, bf16[64,128]{1,0:T(8,128)(2,1)S(1)}) custom-call(s32[4,8,128]{2,1,0:T(8,128)S(1)} %get-tuple-element.26.limits, bf16[4,32,128]{2,1,0:T(8,128)(2,1)S(1)} %collective-permute-done.3.sibling.refs_1_, ...), custom_call_target="tpu_custom_call" | custom-call | bytes 6000000 | tf_op jit(solution)/shard_map/attend/pallas_call | solution.py:41
  12.4 1.7 %collective-permute-start.4 = (bf16[64,128]{1,0:T(8,128)(2,1)S(1)}, bf16[64,128]{1,0:T(8,128)(2,1)S(1)}, u32[]{:S(2)}, u32[]{:S(2)}) collective-permute-start(bf16[64,128]{1,0:T(8,128)(2,1)S(1)} %get-tuple-element.33), channel_id=1, source_target_pairs={{0,7},{1,6},{2,5},{3,4},{4,3},{5,2},{6,1},{7,0},{8,15},{9,14},{10,... | collective-permute-start | bytes 49160 | tf_op jit(solution)/shard_map/ppermute | solution.py:396
  14.1 0.7 %collective-permute-start.5 = (bf16[64,128]{1,0:T(8,128)(2,1)S(1)}, bf16[64,128]{1,0:T(8,128)(2,1)S(1)}, u32[]{:S(2)}, u32[]{:S(2)}) collective-permute-start(bf16[64,128]{1,0:T(8,128)(2,1)S(1)} %get-tuple-element.34), channel_id=1, source_target_pairs={{0,5},{1,4},{2,1},{3,0},{4,7},{5,6},{6,3},{7,2},{8,13},{9,12},{10,... | collective-permute-start | bytes 49160 | tf_op jit(solution)/shard_map/ppermute | solution.py:396
  14.8 1.0 %collective-permute-start.6 = (bf16[64,128]{1,0:T(8,128)(2,1)S(1)}, bf16[64,128]{1,0:T(8,128)(2,1)S(1)}, u32[]{:S(2)}, u32[]{:S(2)}) collective-permute-start(bf16[64,128]{1,0:T(8,128)(2,1)S(1)} %get-tuple-element.35), channel_id=1, source_target_pairs={{0,3},{1,2},{2,7},{3,6},{4,1},{5,0},{6,5},{7,4},{8,11},{9,10},{10,... | collective-permute-start | bytes 49160 | tf_op jit(solution)/shard_map/ppermute | solution.py:396
  15.9 2.9 %fetch_b.1 = (bf16[3,1024,1024]{2,1,0:T(8,128)(2,1)S(1)}, f32[64,128]{1,0:T(8,128)S(1)}) custom-call(bf16[4,32,128]{2,1,0:T(8,128)(2,1)S(1)} %get-tuple-element.29.own.refs_0_, bf16[4,32,128]{2,1,0:T(8,128)(2,1)S(1)} %collective-permute-done.3.sibling.refs_1_, f32[64,128]{1,0:T(8,128)S(1)} %get-tuple-element.32.refs_2_.a, bf16[4,1024,1024]{2,1,0:T(8,128)(2,1)} %refs_1_.3), custom_call_target="tpu_custom_call" | custom-call | bytes 6291456 | tf_op jit(solution)/shard_map/fetch_b/pallas_call | solution.py:41
  18.8 0.0 collective-permute-done.4.b
  18.8 0.0 collective-permute-done.5.c
  18.8 0.1 collective-permute-done.6.d
  18.9 0.3 join.1.own
  19.2 0.3 collective-permute-start.7
  19.6 0.9 %collective-permute-done.7.sibling = f32[64,128]{1,0:T(8,128)S(1)} collective-permute-done((f32[64,128]{1,0:T(8,128)S(1)}, f32[64,128]{1,0:T(8,128)S(1)}, u32[]{:S(2)}, u32[]{:S(2)}) %collective-permute-start.7) | collective-permute-done | bytes 32800 | tf_op jit(solution)/shard_map/ppermute | solution.py:410
  20.5 0.0 collective-permute-done.8.sibling_weight
  20.5 0.3 output.1.refs_0_.a
  20.8 1.9 %collective-permute-start.11 = (bf16[16,1024]{1,0:T(8,128)(2,1)S(1)}, bf16[16,1024]{1,0:T(8,128)(2,1)S(1)}, u32[]{:S(2)}, u32[]{:S(2)}) collective-permute-start(bf16[16,1024]{1,0:T(8,128)(2,1)S(1)} %output.1.refs_0_.a), channel_id=1, source_target_pairs={{0,7},{1,6},{2,5},{3,4},{4,3},{5,2},{6,1},{7,0},{8,15},{9,14},{10,... | collective-permute-start | bytes 98312 | tf_op jit(solution)/shard_map/ppermute | solution.py:396
  22.7 0.0 collective-permute-start.10
  22.7 1.7 %collective-permute-start.9 = (bf16[16,1024]{1,0:T(8,128)(2,1)S(1)}, bf16[16,1024]{1,0:T(8,128)(2,1)S(1)}, u32[]{:S(2)}, u32[]{:S(2)}) collective-permute-start(bf16[16,1024]{1,0:T(8,128)(2,1)S(1)} %output.1.refs_0_.a), channel_id=1, source_target_pairs={{0,3},{1,2},{2,7},{3,6},{4,1},{5,0},{6,5},{7,4},{8,11},{9,10},{10,... | collective-permute-start | bytes 98312 | tf_op jit(solution)/shard_map/ppermute | solution.py:396
  24.4 2.8 %fetch_c.1 = (bf16[1,1024,1024]{2,1,0:T(8,128)(2,1)S(1)}, bf16[4,512,1024]{2,1,0:T(8,128)(2,1)S(1)}) custom-call(bf16[16,1024]{1,0:T(8,128)(2,1)S(1)} %output.1.refs_0_.a, bf16[4,1024,1024]{2,1,0:T(8,128)(2,1)} %refs_1_.3, bf16[4,512,1024]{2,1,0:T(8,128)(2,1)} %refs_2_.3), custom_call_target="tpu_custom_call" | custom-call | bytes 6291456 | tf_op jit(solution)/shard_map/fetch_c/pallas_call | solution.py:41
  27.3 0.0 collective-permute-done.11.d
  27.3 0.0 collective-permute-done.10.c
  27.3 0.5 %collective-permute-done.9.b = bf16[16,1024]{1,0:T(8,128)(2,1)S(1)} collective-permute-done((bf16[16,1024]{1,0:T(8,128)(2,1)S(1)}, bf16[16,1024]{1,0:T(8,128)(2,1)S(1)}, u32[]{:S(2)}, u32[]{:S(2)}) %collective-permute-start.9) | collective-permute-done | bytes 32800 | tf_op jit(solution)/shard_map/ppermute | solution.py:396
  27.8 2.2 %experts.1 = (bf16[16,1024]{1,0:T(8,128)(2,1)S(1)}, f32[16,1024]{1,0:T(8,128)S(1)}) custom-call(f32[16,1024]{1,0:T(8,128)S(1)} %get-tuple-element.25.inputs, bf16[16,1024]{1,0:T(8,128)(2,1)S(1)} %output.1.refs_0_.a, bf16[16,1024]{1,0:T(8,128)(2,1)S(1)} %collective-permute-done.9.b, bf16[16,1024]{1,0:T(8,128)(2,1)S(1)} %collective-permute-done.10.c, ...), custom_call_target="tpu_custom_call" | custom-call | bytes 12000000 | tf_op jit(solution)/shard_map/experts/pallas_call | solution.py:41
  29.9 0.1 collective-permute-start.12
  30.1 1.1 %collective-permute-done.12 = bf16[16,1024]{1,0:T(8,128)(2,1)S(1)} collective-permute-done((bf16[16,1024]{1,0:T(8,128)(2,1)S(1)}, bf16[16,1024]{1,0:T(8,128)(2,1)S(1)}, u32[]{:S(2)}, u32[]{:S(2)}) %collective-permute-start.12) | collective-permute-done | bytes 32800 | tf_op jit(solution)/shard_map/ppermute | solution.py:410
  31.2 0.5 %collective-permute-start.15 = (bf16[16,1024]{1,0:T(8,128)(2,1)S(1)}, bf16[16,1024]{1,0:T(8,128)(2,1)S(1)}, u32[]{:S(2)}, u32[]{:S(2)}) collective-permute-start(bf16[16,1024]{1,0:T(8,128)(2,1)S(1)} %add_convert_fusion.a), channel_id=1, source_target_pairs={{0,3},{1,2},{2,7},{3,6},{4,1},{5,0},{6,5},{7,4},{8,11},{9,10},{10,... | collective-permute-start | bytes 98312 | tf_op jit(solution)/shard_map/ppermute | solution.py:396
  31.7 1.4 %collective-permute-start.14 = (bf16[16,1024]{1,0:T(8,128)(2,1)S(1)}, bf16[16,1024]{1,0:T(8,128)(2,1)S(1)}, u32[]{:S(2)}, u32[]{:S(2)}) collective-permute-start(bf16[16,1024]{1,0:T(8,128)(2,1)S(1)} %add_convert_fusion.a), channel_id=1, source_target_pairs={{0,7},{1,6},{2,5},{3,4},{4,3},{5,2},{6,1},{7,0},{8,15},{9,14},{10,... | collective-permute-start | bytes 98312 | tf_op jit(solution)/shard_map/ppermute | solution.py:396
  33.1 1.4 %collective-permute-start.13 = (bf16[16,1024]{1,0:T(8,128)(2,1)S(1)}, bf16[16,1024]{1,0:T(8,128)(2,1)S(1)}, u32[]{:S(2)}, u32[]{:S(2)}) collective-permute-start(bf16[16,1024]{1,0:T(8,128)(2,1)S(1)} %add_convert_fusion.a), channel_id=1, source_target_pairs={{0,5},{1,4},{2,1},{3,0},{4,7},{5,6},{6,3},{7,2},{8,13},{9,12},{10,... | collective-permute-start | bytes 98312 | tf_op jit(solution)/shard_map/ppermute | solution.py:396
  34.4 1.0 %collective-permute-done.15.d = bf16[16,1024]{1,0:T(8,128)(2,1)S(1)} collective-permute-done((bf16[16,1024]{1,0:T(8,128)(2,1)S(1)}, bf16[16,1024]{1,0:T(8,128)(2,1)S(1)}, u32[]{:S(2)}, u32[]{:S(2)}) %collective-permute-start.15) | collective-permute-done | bytes 32800 | tf_op jit(solution)/shard_map/ppermute | solution.py:396
  35.5 1.5 %collective-permute-done.14.c = bf16[16,1024]{1,0:T(8,128)(2,1)S(1)} collective-permute-done((bf16[16,1024]{1,0:T(8,128)(2,1)S(1)}, bf16[16,1024]{1,0:T(8,128)(2,1)S(1)}, u32[]{:S(2)}, u32[]{:S(2)}) %collective-permute-start.14) | collective-permute-done | bytes 32800 | tf_op jit(solution)/shard_map/ppermute | solution.py:396
  36.9 0.0 collective-permute-done.13.b
  36.9 0.6 %final.1 = bf16[4,4,1024]{2,1,0:T(4,128)(2,1)} custom-call(f32[16,1024]{1,0:T(8,128)S(1)} %get-tuple-element.43.residual, bf16[16,1024]{1,0:T(8,128)(2,1)S(1)} %add_convert_fusion.a, bf16[16,1024]{1,0:T(8,128)(2,1)S(1)} %collective-permute-done.13.b, bf16[16,1024]{1,0:T(8,128)(2,1)S(1)} %collective-permute-done.14.c, ...), custom_call_target="tpu_custom_call" | custom-call | tf_op jit(solution)/shard_map/final/pallas_call | solution.py:41
  (2 shorter events, 0.0 us)
Async XLA Ops:
  1.5 7.8 %collective-permute-start.2 = (bf16[32,128]{1,0:T(8,128)(2,1)S(1)}, bf16[32,128]{1,0:T(8,128)(2,1)S(1)}, u32[]{:S(2)}, u32[]{:S(2)}) collective-permute-start(bf16[32,128]{1,0:T(8,128)(2,1)S(1)} %get-tuple-element.27.refs_0_.a), channel_id=1, source_target_pairs={{0,7},{1,6},{2,5},{3,4},{4,3},{5,2},{6,1},{7,0},{8,15},{9,14},{10,... | collective-permute-start | bytes 24584 | tf_op jit(solution)/shard_map/ppermute | solution.py:396
  6.1 3.2 %collective-permute-start.1 = (bf16[32,128]{1,0:T(8,128)(2,1)S(1)}, bf16[32,128]{1,0:T(8,128)(2,1)S(1)}, u32[]{:S(2)}, u32[]{:S(2)}) collective-permute-start(bf16[32,128]{1,0:T(8,128)(2,1)S(1)} %get-tuple-element.27.refs_0_.a), channel_id=1, source_target_pairs={{0,5},{1,4},{2,1},{3,0},{4,7},{5,6},{6,3},{7,2},{8,13},{9,12},{10,... | collective-permute-start | bytes 24584 | tf_op jit(solution)/shard_map/ppermute | solution.py:396
  6.1 4.0 %collective-permute-start = (bf16[32,128]{1,0:T(8,128)(2,1)S(1)}, bf16[32,128]{1,0:T(8,128)(2,1)S(1)}, u32[]{:S(2)}, u32[]{:S(2)}) collective-permute-start(bf16[32,128]{1,0:T(8,128)(2,1)S(1)} %get-tuple-element.27.refs_0_.a), channel_id=1, source_target_pairs={{0,3},{1,2},{2,7},{3,6},{4,1},{5,0},{6,5},{7,4},{8,11},{9,10},{10,... | collective-permute-start | bytes 24584 | tf_op jit(solution)/shard_map/ppermute | solution.py:396
  10.1 10.4 %collective-permute-start.8 = (bf16[128,1024]{1,0:T(8,128)(2,1)S(1)}, bf16[128,1024]{1,0:T(8,128)(2,1)S(1)}, u32[]{:S(2)}, u32[]{:S(2)}) collective-permute-start(bf16[128,1024]{1,0:T(8,128)(2,1)S(1)} %bitcast.6), channel_id=1, source_target_pairs={{0,1},{1,0},{2,3},{3,2},{4,5},{5,4},{6,7},{7,6},{8,9},{9,8},{10,11... | collective-permute-start | bytes 786440 | tf_op jit(solution)/shard_map/ppermute | solution.py:410
  10.7 1.2 %collective-permute-start.3 = (bf16[4,32,128]{2,1,0:T(8,128)(2,1)S(1)}, bf16[4,32,128]{2,1,0:T(8,128)(2,1)S(1)}, u32[]{:S(2)}, u32[]{:S(2)}) collective-permute-start(bf16[4,32,128]{2,1,0:T(8,128)(2,1)S(1)} %get-tuple-element.29.own.refs_0_), channel_id=1, source_target_pairs={{0,1},{1,0},{2,3},{3,2},{4,5},{5,4},{6,7},{7,6},{8,9},{9,8},{10,11... | collective-permute-start | bytes 98312 | tf_op jit(solution)/shard_map/ppermute | solution.py:410
  12.4 6.4 %collective-permute-start.4 = (bf16[64,128]{1,0:T(8,128)(2,1)S(1)}, bf16[64,128]{1,0:T(8,128)(2,1)S(1)}, u32[]{:S(2)}, u32[]{:S(2)}) collective-permute-start(bf16[64,128]{1,0:T(8,128)(2,1)S(1)} %get-tuple-element.33), channel_id=1, source_target_pairs={{0,7},{1,6},{2,5},{3,4},{4,3},{5,2},{6,1},{7,0},{8,15},{9,14},{10,... | collective-permute-start | bytes 49160 | tf_op jit(solution)/shard_map/ppermute | solution.py:396
  14.1 4.7 %collective-permute-start.5 = (bf16[64,128]{1,0:T(8,128)(2,1)S(1)}, bf16[64,128]{1,0:T(8,128)(2,1)S(1)}, u32[]{:S(2)}, u32[]{:S(2)}) collective-permute-start(bf16[64,128]{1,0:T(8,128)(2,1)S(1)} %get-tuple-element.34), channel_id=1, source_target_pairs={{0,5},{1,4},{2,1},{3,0},{4,7},{5,6},{6,3},{7,2},{8,13},{9,12},{10,... | collective-permute-start | bytes 49160 | tf_op jit(solution)/shard_map/ppermute | solution.py:396
  14.8 4.1 %collective-permute-start.6 = (bf16[64,128]{1,0:T(8,128)(2,1)S(1)}, bf16[64,128]{1,0:T(8,128)(2,1)S(1)}, u32[]{:S(2)}, u32[]{:S(2)}) collective-permute-start(bf16[64,128]{1,0:T(8,128)(2,1)S(1)} %get-tuple-element.35), channel_id=1, source_target_pairs={{0,3},{1,2},{2,7},{3,6},{4,1},{5,0},{6,5},{7,4},{8,11},{9,10},{10,... | collective-permute-start | bytes 49160 | tf_op jit(solution)/shard_map/ppermute | solution.py:396
  19.2 1.3 %collective-permute-start.7 = (f32[64,128]{1,0:T(8,128)S(1)}, f32[64,128]{1,0:T(8,128)S(1)}, u32[]{:S(2)}, u32[]{:S(2)}) collective-permute-start(f32[64,128]{1,0:T(8,128)S(1)} %join.1.own), channel_id=1, source_target_pairs={{0,1},{1,0},{2,3},{3,2},{4,5},{5,4},{6,7},{7,6},{8,9},{9,8},{10,11... | collective-permute-start | bytes 98312 | tf_op jit(solution)/shard_map/ppermute | solution.py:410
  20.8 6.5 %collective-permute-start.11 = (bf16[16,1024]{1,0:T(8,128)(2,1)S(1)}, bf16[16,1024]{1,0:T(8,128)(2,1)S(1)}, u32[]{:S(2)}, u32[]{:S(2)}) collective-permute-start(bf16[16,1024]{1,0:T(8,128)(2,1)S(1)} %output.1.refs_0_.a), channel_id=1, source_target_pairs={{0,7},{1,6},{2,5},{3,4},{4,3},{5,2},{6,1},{7,0},{8,15},{9,14},{10,... | collective-permute-start | bytes 98312 | tf_op jit(solution)/shard_map/ppermute | solution.py:396
  22.7 4.6 %collective-permute-start.10 = (bf16[16,1024]{1,0:T(8,128)(2,1)S(1)}, bf16[16,1024]{1,0:T(8,128)(2,1)S(1)}, u32[]{:S(2)}, u32[]{:S(2)}) collective-permute-start(bf16[16,1024]{1,0:T(8,128)(2,1)S(1)} %output.1.refs_0_.a), channel_id=1, source_target_pairs={{0,5},{1,4},{2,1},{3,0},{4,7},{5,6},{6,3},{7,2},{8,13},{9,12},{10,... | collective-permute-start | bytes 98312 | tf_op jit(solution)/shard_map/ppermute | solution.py:396
  22.7 5.1 %collective-permute-start.9 = (bf16[16,1024]{1,0:T(8,128)(2,1)S(1)}, bf16[16,1024]{1,0:T(8,128)(2,1)S(1)}, u32[]{:S(2)}, u32[]{:S(2)}) collective-permute-start(bf16[16,1024]{1,0:T(8,128)(2,1)S(1)} %output.1.refs_0_.a), channel_id=1, source_target_pairs={{0,3},{1,2},{2,7},{3,6},{4,1},{5,0},{6,5},{7,4},{8,11},{9,10},{10,... | collective-permute-start | bytes 98312 | tf_op jit(solution)/shard_map/ppermute | solution.py:396
  29.9 1.2 %collective-permute-start.12 = (bf16[16,1024]{1,0:T(8,128)(2,1)S(1)}, bf16[16,1024]{1,0:T(8,128)(2,1)S(1)}, u32[]{:S(2)}, u32[]{:S(2)}) collective-permute-start(bf16[16,1024]{1,0:T(8,128)(2,1)S(1)} %get-tuple-element.44), channel_id=1, source_target_pairs={{0,1},{1,0},{2,3},{3,2},{4,5},{5,4},{6,7},{7,6},{8,9},{9,8},{10,11... | collective-permute-start | bytes 98312 | tf_op jit(solution)/shard_map/ppermute | solution.py:410
  31.2 4.3 %collective-permute-start.15 = (bf16[16,1024]{1,0:T(8,128)(2,1)S(1)}, bf16[16,1024]{1,0:T(8,128)(2,1)S(1)}, u32[]{:S(2)}, u32[]{:S(2)}) collective-permute-start(bf16[16,1024]{1,0:T(8,128)(2,1)S(1)} %add_convert_fusion.a), channel_id=1, source_target_pairs={{0,3},{1,2},{2,7},{3,6},{4,1},{5,0},{6,5},{7,4},{8,11},{9,10},{10,... | collective-permute-start | bytes 98312 | tf_op jit(solution)/shard_map/ppermute | solution.py:396
  31.7 5.3 %collective-permute-start.14 = (bf16[16,1024]{1,0:T(8,128)(2,1)S(1)}, bf16[16,1024]{1,0:T(8,128)(2,1)S(1)}, u32[]{:S(2)}, u32[]{:S(2)}) collective-permute-start(bf16[16,1024]{1,0:T(8,128)(2,1)S(1)} %add_convert_fusion.a), channel_id=1, source_target_pairs={{0,7},{1,6},{2,5},{3,4},{4,3},{5,2},{6,1},{7,0},{8,15},{9,14},{10,... | collective-permute-start | bytes 98312 | tf_op jit(solution)/shard_map/ppermute | solution.py:396
  33.1 3.9 %collective-permute-start.13 = (bf16[16,1024]{1,0:T(8,128)(2,1)S(1)}, bf16[16,1024]{1,0:T(8,128)(2,1)S(1)}, u32[]{:S(2)}, u32[]{:S(2)}) collective-permute-start(bf16[16,1024]{1,0:T(8,128)(2,1)S(1)} %add_convert_fusion.a), channel_id=1, source_target_pairs={{0,5},{1,4},{2,1},{3,0},{4,7},{5,6},{6,3},{7,2},{8,13},{9,12},{10,... | collective-permute-start | bytes 98312 | tf_op jit(solution)/shard_map/ppermute | solution.py:396

commit v7 on v6

--- a/solution.py
+++ b/solution.py
@@ -199,21 +199,20 @@
     out[n:] = jnp.where(place == 3, 0.0, split).astype(BF16)
 
 
-def read_packed(ref):
-    n = ref.shape[0] // 2
-    split = ref[n:].astype(F32)
-    lanes = split.shape[1]
-    stats = split + pltpu.roll(split, lanes - 8, 1) + pltpu.roll(split, lanes - 16, 1)
-    lane = iota(split.shape, 1) % HEAD_DIMENSION
-    half = HEAD_DIMENSION // 2
-    peak = jnp.where(lane < 8, stats, 0.0)
-    total = jnp.where((lane >= half) & (lane < half + 8), stats, 0.0)
-    for step in (8, 16):
-        peak = peak + pltpu.roll(peak, step, 1)
-        total = total + pltpu.roll(total, step, 1)
-    peak = peak + pltpu.roll(peak, half, 1)
-    total = total + pltpu.roll(total, lanes - half, 1)
-    return peak, total, ref[0:n].astype(F32)
+def read_packed(refs):
+    n = refs[0].shape[0] // 2
+    shape = (128, 256)
+    lane, column = iota(shape, 0), iota(shape, 1)
+    piece = lane % HEAD_DIMENSION - jnp.where(column < 128, 0, HEAD_DIMENSION // 2)
+    hit = (piece == 0) | (piece == 8) | (piece == 16)
+    hit = hit & (lane // HEAD_DIMENSION == column % 128 // HEAD_DIMENSION)
+    place = jnp.where(hit, 1.0, 0.0).astype(BF16)
+    split = merge_rows([ref[n:] for ref in refs])
+    stats = jnp.dot(split, place, preferred_element_type=F32)
+    return [
+        (stats[i * n : (i + 1) * n, :128], stats[i * n : (i + 1) * n, 128:], ref[0:n].astype(F32))
+        for i, ref in enumerate(refs)
+    ]
 
 
 def soft(scores, live):
@@ -309,9 +308,8 @@
 
 def join_kernel(order, a, b, c, d, fetched, out):
     a, b, c, d = sort_chips(order, a, (b, c, d))
-    peak, total, summed = join(
-        join(read_part(a), read_packed(d)), join(read_packed(b), read_packed(c))
-    )
+    b, c, d = read_packed((b, c, d))
+    peak, total, summed = join(join(read_part(a), d), join(b, c))
     n = summed.shape[0]
     out[0:n] = summed
     out[n:] = pack_stats(peak, total)

time: 37.7 us -> 37.6 us (level)
  no operation moved by 1% of the time
where the time goes in v7:
time: 37.6 us; the launch traced here: 37.4 us
  starting transfers between devices  17.8 us (47%)
  Pallas kernels  12.9 us (34%)
  waiting for transfers between devices  6.6 us (18%)
    ppermute x12, starting transfers between devices, other_chip(): lax.ppermute(x, 'tp', [(i, 2 * to[i // 2] + 1 - i % 2) for i in range(dev...  16.6 us
    pallas_call x11, Pallas kernels, call(): pl.pallas_call(kernel, out_shape=[jax.ShapeDtypeStruct(s, d) if hbm_out e...  12.9 us
    ppermute x12, waiting for transfers between devices, other_chip(): lax.ppermute(x, 'tp', [(i, 2 * to[i // 2] + 1 - i % 2) for i in range(dev...  3.88 us
    ppermute x4, waiting for transfers between devices, other_core(): return lax.ppermute(x, 'tp', [(i, i ^ 1) for i in range(devices)])  2.72 us
    ppermute x4, starting transfers between devices, other_core(): return lax.ppermute(x, 'tp', [(i, i ^ 1) for i in range(devices)])  1.17 us
  transfers between devices with their start and end apart: 16, of which 8 were waited for; matrix products, arithmetic and copies ran while one was open for 0% of the time, Pallas kernels for 22%

profile of v7, /device:TPU:0, one launch (start us, length us, event | category | flops | bytes accessed | tf_op | source)
XLA Modules:
  0.0 37.4 jit_solution(6957516140921629182)
XLA Ops:
  0.0 1.5 %project.1 = (bf16[32,128]{1,0:T(8,128)(2,1)S(1)}, s32[4,8,128]{2,1,0:T(8,128)S(1)}, f32[16,1024]{1,0:T(8,128)S(1)}) custom-call(s32[4]{0:T(128)} %lengths_in.1, bf16[4,4,1024]{2,1,0:T(4,128)(2,1)} %hidden_in.1, bf16[256,1024]{1,0:T(8,128)(2,1)} %weight_in.1), custom_call_target="tpu_custom_call" | custom-call | bytes 8000000 | tf_op jit(solution)/shard_map/project/pallas_call | solution.py:41
  1.5 4.6 %collective-permute-start.2 = (bf16[32,128]{1,0:T(8,128)(2,1)S(1)}, bf16[32,128]{1,0:T(8,128)(2,1)S(1)}, u32[]{:S(2)}, u32[]{:S(2)}) collective-permute-start(bf16[32,128]{1,0:T(8,128)(2,1)S(1)} %get-tuple-element.27.refs_0_.a), channel_id=1, source_target_pairs={{0,7},{1,6},{2,5},{3,4},{4,3},{5,2},{6,1},{7,0},{8,15},{9,14},{10,... | collective-permute-start | bytes 24584 | tf_op jit(solution)/shard_map/ppermute | solution.py:394
  6.1 0.0 collective-permute-start.1
  6.1 1.7 %collective-permute-start = (bf16[32,128]{1,0:T(8,128)(2,1)S(1)}, bf16[32,128]{1,0:T(8,128)(2,1)S(1)}, u32[]{:S(2)}, u32[]{:S(2)}) collective-permute-start(bf16[32,128]{1,0:T(8,128)(2,1)S(1)} %get-tuple-element.27.refs_0_.a), channel_id=1, source_target_pairs={{0,3},{1,2},{2,7},{3,6},{4,1},{5,0},{6,5},{7,4},{8,11},{9,10},{10,... | collective-permute-start | bytes 24584 | tf_op jit(solution)/shard_map/ppermute | solution.py:394
  7.8 1.5 %fetch_cache.1 = (bf16[4,128,512]{2,1,0:T(8,128)(2,1)S(1)}, bf16[4,128,512]{2,1,0:T(8,128)(2,1)S(1)}, bf16[1,128,1024]{2,1,0:T(8,128)(2,1)S(1)}, s32[1,4,4,8]{3,2,1,0:T(4,128)S(1)}, s32[1,4,4,8]{3,2,1,0:T(4,128)S(1)}) custom-call(bf16[32,128]{1,0:T(8,128)(2,1)S(1)} %get-tuple-element.27.refs_0_.a, bf16[4,128,512]{2,1,0:T(8,128)(2,1)} %refs_1_.2, ...), custom_call_target="tpu_custom_call" | custom-call | bytes 1311232 | tf_op jit(solution)/shard_map/fetch_cache/pallas_call | solution.py:41
  9.3 0.0 collective-permute-done.2.d
  9.3 0.0 collective-permute-done.1.c
  9.3 0.8 %collective-permute-done.b = bf16[32,128]{1,0:T(8,128)(2,1)S(1)} collective-permute-done((bf16[32,128]{1,0:T(8,128)(2,1)S(1)}, bf16[32,128]{1,0:T(8,128)(2,1)S(1)}, u32[]{:S(2)}, u32[]{:S(2)}) %collective-permute-start) | collective-permute-done | bytes 8224 | tf_op jit(solution)/shard_map/ppermute | solution.py:394
  10.1 0.6 %collective-permute-start.8 = (bf16[128,1024]{1,0:T(8,128)(2,1)S(1)}, bf16[128,1024]{1,0:T(8,128)(2,1)S(1)}, u32[]{:S(2)}, u32[]{:S(2)}) collective-permute-start(bf16[128,1024]{1,0:T(8,128)(2,1)S(1)} %bitcast.6), channel_id=1, source_target_pairs={{0,1},{1,0},{2,3},{3,2},{4,5},{5,4},{6,7},{7,6},{8,9},{9,8},{10,11... | collective-permute-start | bytes 786440 | tf_op jit(solution)/shard_map/ppermute | solution.py:408
  10.7 0.1 collective-permute-start.3
  10.8 0.4 %attend_own.1.blocks_own = f32[2,64,128]{2,1,0:T(8,128)S(1)} custom-call(s32[4,8,128]{2,1,0:T(8,128)S(1)} %get-tuple-element.26.limits, bf16[4,32,128]{2,1,0:T(8,128)(2,1)S(1)} %get-tuple-element.29.own.refs_0_, bf16[4,128,512]{2,1,0:T(8,128)(2,1)S(1)} %get-tuple-element.30.keys, bf16[4,128,512]{2,1,0:T(8,128)(2,1)S(1)} %get-tuple-element.31.values), custom_call_target="tpu_custom_call" | custom-call | bytes 6000000 | tf_op jit(solution)/shard_map/attend_own/pallas_call | solution.py:41
  11.2 0.7 %collective-permute-done.3.sibling.refs_1_ = bf16[4,32,128]{2,1,0:T(8,128)(2,1)S(1)} collective-permute-done((bf16[4,32,128]{2,1,0:T(8,128)(2,1)S(1)}, bf16[4,32,128]{2,1,0:T(8,128)(2,1)S(1)}, u32[]{:S(2)}, u32[]{:S(2)}) %collective-permute-start.3) | collective-permute-done | bytes 32800 | tf_op jit(solution)/shard_map/ppermute | solution.py:408
  11.9 0.5 %attend.1 = (f32[64,128]{1,0:T(8,128)S(1)}, bf16[64,128]{1,0:T(8,128)(2,1)S(1)}, bf16[64,128]{1,0:T(8,128)(2,1)S(1)}, bf16[64,128]{1,0:T(8,128)(2,1)S(1)}) custom-call(s32[4,8,128]{2,1,0:T(8,128)S(1)} %get-tuple-element.26.limits, bf16[4,32,128]{2,1,0:T(8,128)(2,1)S(1)} %collective-permute-done.3.sibling.refs_1_, ...), custom_call_target="tpu_custom_call" | custom-call | bytes 6000000 | tf_op jit(solution)/shard_map/attend/pallas_call | solution.py:41
  12.4 1.7 %collective-permute-start.4 = (bf16[64,128]{1,0:T(8,128)(2,1)S(1)}, bf16[64,128]{1,0:T(8,128)(2,1)S(1)}, u32[]{:S(2)}, u32[]{:S(2)}) collective-permute-start(bf16[64,128]{1,0:T(8,128)(2,1)S(1)} %get-tuple-element.33), channel_id=1, source_target_pairs={{0,7},{1,6},{2,5},{3,4},{4,3},{5,2},{6,1},{7,0},{8,15},{9,14},{10,... | collective-permute-start | bytes 49160 | tf_op jit(solution)/shard_map/ppermute | solution.py:394
  14.1 0.7 %collective-permute-start.5 = (bf16[64,128]{1,0:T(8,128)(2,1)S(1)}, bf16[64,128]{1,0:T(8,128)(2,1)S(1)}, u32[]{:S(2)}, u32[]{:S(2)}) collective-permute-start(bf16[64,128]{1,0:T(8,128)(2,1)S(1)} %get-tuple-element.34), channel_id=1, source_target_pairs={{0,5},{1,4},{2,1},{3,0},{4,7},{5,6},{6,3},{7,2},{8,13},{9,12},{10,... | collective-permute-start | bytes 49160 | tf_op jit(solution)/shard_map/ppermute | solution.py:394
  14.8 1.0 %collective-permute-start.6 = (bf16[64,128]{1,0:T(8,128)(2,1)S(1)}, bf16[64,128]{1,0:T(8,128)(2,1)S(1)}, u32[]{:S(2)}, u32[]{:S(2)}) collective-permute-start(bf16[64,128]{1,0:T(8,128)(2,1)S(1)} %get-tuple-element.35), channel_id=1, source_target_pairs={{0,3},{1,2},{2,7},{3,6},{4,1},{5,0},{6,5},{7,4},{8,11},{9,10},{10,... | collective-permute-start | bytes 49160 | tf_op jit(solution)/shard_map/ppermute | solution.py:394
  15.9 2.9 %fetch_b.1 = (bf16[3,1024,1024]{2,1,0:T(8,128)(2,1)S(1)}, f32[64,128]{1,0:T(8,128)S(1)}) custom-call(bf16[4,32,128]{2,1,0:T(8,128)(2,1)S(1)} %get-tuple-element.29.own.refs_0_, bf16[4,32,128]{2,1,0:T(8,128)(2,1)S(1)} %collective-permute-done.3.sibling.refs_1_, f32[64,128]{1,0:T(8,128)S(1)} %get-tuple-element.32.refs_2_.a, bf16[4,1024,1024]{2,1,0:T(8,128)(2,1)} %refs_1_.3), custom_call_target="tpu_custom_call" | custom-call | bytes 6291456 | tf_op jit(solution)/shard_map/fetch_b/pallas_call | solution.py:41
  18.8 0.0 collective-permute-done.4.b
  18.8 0.0 collective-permute-done.5.c
  18.8 0.1 collective-permute-done.6.d
  18.9 0.2 join.1.own
  19.1 0.3 collective-permute-start.7
  19.4 0.9 %collective-permute-done.7.sibling = f32[64,128]{1,0:T(8,128)S(1)} collective-permute-done((f32[64,128]{1,0:T(8,128)S(1)}, f32[64,128]{1,0:T(8,128)S(1)}, u32[]{:S(2)}, u32[]{:S(2)}) %collective-permute-start.7) | collective-permute-done | bytes 32800 | tf_op jit(solution)/shard_map/ppermute | solution.py:408
  20.3 0.0 collective-permute-done.8.sibling_weight
  20.3 0.3 output.1.refs_0_.a
  20.7 1.9 %collective-permute-start.11 = (bf16[16,1024]{1,0:T(8,128)(2,1)S(1)}, bf16[16,1024]{1,0:T(8,128)(2,1)S(1)}, u32[]{:S(2)}, u32[]{:S(2)}) collective-permute-start(bf16[16,1024]{1,0:T(8,128)(2,1)S(1)} %output.1.refs_0_.a), channel_id=1, source_target_pairs={{0,7},{1,6},{2,5},{3,4},{4,3},{5,2},{6,1},{7,0},{8,15},{9,14},{10,... | collective-permute-start | bytes 98312 | tf_op jit(solution)/shard_map/ppermute | solution.py:394
  22.5 0.0 collective-permute-start.10
  22.5 1.7 %collective-permute-start.9 = (bf16[16,1024]{1,0:T(8,128)(2,1)S(1)}, bf16[16,1024]{1,0:T(8,128)(2,1)S(1)}, u32[]{:S(2)}, u32[]{:S(2)}) collective-permute-start(bf16[16,1024]{1,0:T(8,128)(2,1)S(1)} %output.1.refs_0_.a), channel_id=1, source_target_pairs={{0,3},{1,2},{2,7},{3,6},{4,1},{5,0},{6,5},{7,4},{8,11},{9,10},{10,... | collective-permute-start | bytes 98312 | tf_op jit(solution)/shard_map/ppermute | solution.py:394
  24.3 2.8 %fetch_c.1 = (bf16[1,1024,1024]{2,1,0:T(8,128)(2,1)S(1)}, bf16[4,512,1024]{2,1,0:T(8,128)(2,1)S(1)}) custom-call(bf16[16,1024]{1,0:T(8,128)(2,1)S(1)} %output.1.refs_0_.a, bf16[4,1024,1024]{2,1,0:T(8,128)(2,1)} %refs_1_.3, bf16[4,512,1024]{2,1,0:T(8,128)(2,1)} %refs_2_.3), custom_call_target="tpu_custom_call" | custom-call | bytes 6291456 | tf_op jit(solution)/shard_map/fetch_c/pallas_call | solution.py:41
  27.1 0.0 collective-permute-done.11.d
  27.1 0.0 collective-permute-done.10.c
  27.1 0.5 %collective-permute-done.9.b = bf16[16,1024]{1,0:T(8,128)(2,1)S(1)} collective-permute-done((bf16[16,1024]{1,0:T(8,128)(2,1)S(1)}, bf16[16,1024]{1,0:T(8,128)(2,1)S(1)}, u32[]{:S(2)}, u32[]{:S(2)}) %collective-permute-start.9) | collective-permute-done | bytes 32800 | tf_op jit(solution)/shard_map/ppermute | solution.py:394
  27.6 2.2 %experts.1 = (bf16[16,1024]{1,0:T(8,128)(2,1)S(1)}, f32[16,1024]{1,0:T(8,128)S(1)}) custom-call(f32[16,1024]{1,0:T(8,128)S(1)} %get-tuple-element.25.inputs, bf16[16,1024]{1,0:T(8,128)(2,1)S(1)} %output.1.refs_0_.a, bf16[16,1024]{1,0:T(8,128)(2,1)S(1)} %collective-permute-done.9.b, bf16[16,1024]{1,0:T(8,128)(2,1)S(1)} %collective-permute-done.10.c, ...), custom_call_target="tpu_custom_call" | custom-call | bytes 12000000 | tf_op jit(solution)/shard_map/experts/pallas_call | solution.py:41
  29.8 0.1 collective-permute-start.12
  29.9 1.1 %collective-permute-done.12 = bf16[16,1024]{1,0:T(8,128)(2,1)S(1)} collective-permute-done((bf16[16,1024]{1,0:T(8,128)(2,1)S(1)}, bf16[16,1024]{1,0:T(8,128)(2,1)S(1)}, u32[]{:S(2)}, u32[]{:S(2)}) %collective-permute-start.12) | collective-permute-done | bytes 32800 | tf_op jit(solution)/shard_map/ppermute | solution.py:408
  31.0 0.5 %collective-permute-start.15 = (bf16[16,1024]{1,0:T(8,128)(2,1)S(1)}, bf16[16,1024]{1,0:T(8,128)(2,1)S(1)}, u32[]{:S(2)}, u32[]{:S(2)}) collective-permute-start(bf16[16,1024]{1,0:T(8,128)(2,1)S(1)} %add_convert_fusion.a), channel_id=1, source_target_pairs={{0,3},{1,2},{2,7},{3,6},{4,1},{5,0},{6,5},{7,4},{8,11},{9,10},{10,... | collective-permute-start | bytes 98312 | tf_op jit(solution)/shard_map/ppermute | solution.py:394
  31.5 1.4 %collective-permute-start.14 = (bf16[16,1024]{1,0:T(8,128)(2,1)S(1)}, bf16[16,1024]{1,0:T(8,128)(2,1)S(1)}, u32[]{:S(2)}, u32[]{:S(2)}) collective-permute-start(bf16[16,1024]{1,0:T(8,128)(2,1)S(1)} %add_convert_fusion.a), channel_id=1, source_target_pairs={{0,7},{1,6},{2,5},{3,4},{4,3},{5,2},{6,1},{7,0},{8,15},{9,14},{10,... | collective-permute-start | bytes 98312 | tf_op jit(solution)/shard_map/ppermute | solution.py:394
  32.9 1.4 %collective-permute-start.13 = (bf16[16,1024]{1,0:T(8,128)(2,1)S(1)}, bf16[16,1024]{1,0:T(8,128)(2,1)S(1)}, u32[]{:S(2)}, u32[]{:S(2)}) collective-permute-start(bf16[16,1024]{1,0:T(8,128)(2,1)S(1)} %add_convert_fusion.a), channel_id=1, source_target_pairs={{0,5},{1,4},{2,1},{3,0},{4,7},{5,6},{6,3},{7,2},{8,13},{9,12},{10,... | collective-permute-start | bytes 98312 | tf_op jit(solution)/shard_map/ppermute | solution.py:394
  34.3 1.0 %collective-permute-done.15.d = bf16[16,1024]{1,0:T(8,128)(2,1)S(1)} collective-permute-done((bf16[16,1024]{1,0:T(8,128)(2,1)S(1)}, bf16[16,1024]{1,0:T(8,128)(2,1)S(1)}, u32[]{:S(2)}, u32[]{:S(2)}) %collective-permute-start.15) | collective-permute-done | bytes 32800 | tf_op jit(solution)/shard_map/ppermute | solution.py:394
  35.3 1.5 %collective-permute-done.14.c = bf16[16,1024]{1,0:T(8,128)(2,1)S(1)} collective-permute-done((bf16[16,1024]{1,0:T(8,128)(2,1)S(1)}, bf16[16,1024]{1,0:T(8,128)(2,1)S(1)}, u32[]{:S(2)}, u32[]{:S(2)}) %collective-permute-start.14) | collective-permute-done | bytes 32800 | tf_op jit(solution)/shard_map/ppermute | solution.py:394
  36.8 0.0 collective-permute-done.13.b
  36.8 0.6 %final.1 = bf16[4,4,1024]{2,1,0:T(4,128)(2,1)} custom-call(f32[16,1024]{1,0:T(8,128)S(1)} %get-tuple-element.43.residual, bf16[16,1024]{1,0:T(8,128)(2,1)S(1)} %add_convert_fusion.a, bf16[16,1024]{1,0:T(8,128)(2,1)S(1)} %collective-permute-done.13.b, bf16[16,1024]{1,0:T(8,128)(2,1)S(1)} %collective-permute-done.14.c, ...), custom_call_target="tpu_custom_call" | custom-call | tf_op jit(solution)/shard_map/final/pallas_call | solution.py:41
  (2 shorter events, 0.0 us)
Async XLA Ops:
  1.5 7.8 %collective-permute-start.2 = (bf16[32,128]{1,0:T(8,128)(2,1)S(1)}, bf16[32,128]{1,0:T(8,128)(2,1)S(1)}, u32[]{:S(2)}, u32[]{:S(2)}) collective-permute-start(bf16[32,128]{1,0:T(8,128)(2,1)S(1)} %get-tuple-element.27.refs_0_.a), channel_id=1, source_target_pairs={{0,7},{1,6},{2,5},{3,4},{4,3},{5,2},{6,1},{7,0},{8,15},{9,14},{10,... | collective-permute-start | bytes 24584 | tf_op jit(solution)/shard_map/ppermute | solution.py:394
  6.1 3.2 %collective-permute-start.1 = (bf16[32,128]{1,0:T(8,128)(2,1)S(1)}, bf16[32,128]{1,0:T(8,128)(2,1)S(1)}, u32[]{:S(2)}, u32[]{:S(2)}) collective-permute-start(bf16[32,128]{1,0:T(8,128)(2,1)S(1)} %get-tuple-element.27.refs_0_.a), channel_id=1, source_target_pairs={{0,5},{1,4},{2,1},{3,0},{4,7},{5,6},{6,3},{7,2},{8,13},{9,12},{10,... | collective-permute-start | bytes 24584 | tf_op jit(solution)/shard_map/ppermute | solution.py:394
  6.1 4.0 %collective-permute-start = (bf16[32,128]{1,0:T(8,128)(2,1)S(1)}, bf16[32,128]{1,0:T(8,128)(2,1)S(1)}, u32[]{:S(2)}, u32[]{:S(2)}) collective-permute-start(bf16[32,128]{1,0:T(8,128)(2,1)S(1)} %get-tuple-element.27.refs_0_.a), channel_id=1, source_target_pairs={{0,3},{1,2},{2,7},{3,6},{4,1},{5,0},{6,5},{7,4},{8,11},{9,10},{10,... | collective-permute-start | bytes 24584 | tf_op jit(solution)/shard_map/ppermute | solution.py:394
  10.1 10.3 %collective-permute-start.8 = (bf16[128,1024]{1,0:T(8,128)(2,1)S(1)}, bf16[128,1024]{1,0:T(8,128)(2,1)S(1)}, u32[]{:S(2)}, u32[]{:S(2)}) collective-permute-start(bf16[128,1024]{1,0:T(8,128)(2,1)S(1)} %bitcast.6), channel_id=1, source_target_pairs={{0,1},{1,0},{2,3},{3,2},{4,5},{5,4},{6,7},{7,6},{8,9},{9,8},{10,11... | collective-permute-start | bytes 786440 | tf_op jit(solution)/shard_map/ppermute | solution.py:408
  10.7 1.2 %collective-permute-start.3 = (bf16[4,32,128]{2,1,0:T(8,128)(2,1)S(1)}, bf16[4,32,128]{2,1,0:T(8,128)(2,1)S(1)}, u32[]{:S(2)}, u32[]{:S(2)}) collective-permute-start(bf16[4,32,128]{2,1,0:T(8,128)(2,1)S(1)} %get-tuple-element.29.own.refs_0_), channel_id=1, source_target_pairs={{0,1},{1,0},{2,3},{3,2},{4,5},{5,4},{6,7},{7,6},{8,9},{9,8},{10,11... | collective-permute-start | bytes 98312 | tf_op jit(solution)/shard_map/ppermute | solution.py:408
  12.4 6.4 %collective-permute-start.4 = (bf16[64,128]{1,0:T(8,128)(2,1)S(1)}, bf16[64,128]{1,0:T(8,128)(2,1)S(1)}, u32[]{:S(2)}, u32[]{:S(2)}) collective-permute-start(bf16[64,128]{1,0:T(8,128)(2,1)S(1)} %get-tuple-element.33), channel_id=1, source_target_pairs={{0,7},{1,6},{2,5},{3,4},{4,3},{5,2},{6,1},{7,0},{8,15},{9,14},{10,... | collective-permute-start | bytes 49160 | tf_op jit(solution)/shard_map/ppermute | solution.py:394
  14.1 4.7 %collective-permute-start.5 = (bf16[64,128]{1,0:T(8,128)(2,1)S(1)}, bf16[64,128]{1,0:T(8,128)(2,1)S(1)}, u32[]{:S(2)}, u32[]{:S(2)}) collective-permute-start(bf16[64,128]{1,0:T(8,128)(2,1)S(1)} %get-tuple-element.34), channel_id=1, source_target_pairs={{0,5},{1,4},{2,1},{3,0},{4,7},{5,6},{6,3},{7,2},{8,13},{9,12},{10,... | collective-permute-start | bytes 49160 | tf_op jit(solution)/shard_map/ppermute | solution.py:394
  14.8 4.1 %collective-permute-start.6 = (bf16[64,128]{1,0:T(8,128)(2,1)S(1)}, bf16[64,128]{1,0:T(8,128)(2,1)S(1)}, u32[]{:S(2)}, u32[]{:S(2)}) collective-permute-start(bf16[64,128]{1,0:T(8,128)(2,1)S(1)} %get-tuple-element.35), channel_id=1, source_target_pairs={{0,3},{1,2},{2,7},{3,6},{4,1},{5,0},{6,5},{7,4},{8,11},{9,10},{10,... | collective-permute-start | bytes 49160 | tf_op jit(solution)/shard_map/ppermute | solution.py:394
  19.1 1.3 %collective-permute-start.7 = (f32[64,128]{1,0:T(8,128)S(1)}, f32[64,128]{1,0:T(8,128)S(1)}, u32[]{:S(2)}, u32[]{:S(2)}) collective-permute-start(f32[64,128]{1,0:T(8,128)S(1)} %join.1.own), channel_id=1, source_target_pairs={{0,1},{1,0},{2,3},{3,2},{4,5},{5,4},{6,7},{7,6},{8,9},{9,8},{10,11... | collective-permute-start | bytes 98312 | tf_op jit(solution)/shard_map/ppermute | solution.py:408
  20.7 6.5 %collective-permute-start.11 = (bf16[16,1024]{1,0:T(8,128)(2,1)S(1)}, bf16[16,1024]{1,0:T(8,128)(2,1)S(1)}, u32[]{:S(2)}, u32[]{:S(2)}) collective-permute-start(bf16[16,1024]{1,0:T(8,128)(2,1)S(1)} %output.1.refs_0_.a), channel_id=1, source_target_pairs={{0,7},{1,6},{2,5},{3,4},{4,3},{5,2},{6,1},{7,0},{8,15},{9,14},{10,... | collective-permute-start | bytes 98312 | tf_op jit(solution)/shard_map/ppermute | solution.py:394
  22.5 4.6 %collective-permute-start.10 = (bf16[16,1024]{1,0:T(8,128)(2,1)S(1)}, bf16[16,1024]{1,0:T(8,128)(2,1)S(1)}, u32[]{:S(2)}, u32[]{:S(2)}) collective-permute-start(bf16[16,1024]{1,0:T(8,128)(2,1)S(1)} %output.1.refs_0_.a), channel_id=1, source_target_pairs={{0,5},{1,4},{2,1},{3,0},{4,7},{5,6},{6,3},{7,2},{8,13},{9,12},{10,... | collective-permute-start | bytes 98312 | tf_op jit(solution)/shard_map/ppermute | solution.py:394
  22.5 5.1 %collective-permute-start.9 = (bf16[16,1024]{1,0:T(8,128)(2,1)S(1)}, bf16[16,1024]{1,0:T(8,128)(2,1)S(1)}, u32[]{:S(2)}, u32[]{:S(2)}) collective-permute-start(bf16[16,1024]{1,0:T(8,128)(2,1)S(1)} %output.1.refs_0_.a), channel_id=1, source_target_pairs={{0,3},{1,2},{2,7},{3,6},{4,1},{5,0},{6,5},{7,4},{8,11},{9,10},{10,... | collective-permute-start | bytes 98312 | tf_op jit(solution)/shard_map/ppermute | solution.py:394
  29.8 1.2 %collective-permute-start.12 = (bf16[16,1024]{1,0:T(8,128)(2,1)S(1)}, bf16[16,1024]{1,0:T(8,128)(2,1)S(1)}, u32[]{:S(2)}, u32[]{:S(2)}) collective-permute-start(bf16[16,1024]{1,0:T(8,128)(2,1)S(1)} %get-tuple-element.44), channel_id=1, source_target_pairs={{0,1},{1,0},{2,3},{3,2},{4,5},{5,4},{6,7},{7,6},{8,9},{9,8},{10,11... | collective-permute-start | bytes 98312 | tf_op jit(solution)/shard_map/ppermute | solution.py:408
  31.0 4.3 %collective-permute-start.15 = (bf16[16,1024]{1,0:T(8,128)(2,1)S(1)}, bf16[16,1024]{1,0:T(8,128)(2,1)S(1)}, u32[]{:S(2)}, u32[]{:S(2)}) collective-permute-start(bf16[16,1024]{1,0:T(8,128)(2,1)S(1)} %add_convert_fusion.a), channel_id=1, source_target_pairs={{0,3},{1,2},{2,7},{3,6},{4,1},{5,0},{6,5},{7,4},{8,11},{9,10},{10,... | collective-permute-start | bytes 98312 | tf_op jit(solution)/shard_map/ppermute | solution.py:394
  31.5 5.3 %collective-permute-start.14 = (bf16[16,1024]{1,0:T(8,128)(2,1)S(1)}, bf16[16,1024]{1,0:T(8,128)(2,1)S(1)}, u32[]{:S(2)}, u32[]{:S(2)}) collective-permute-start(bf16[16,1024]{1,0:T(8,128)(2,1)S(1)} %add_convert_fusion.a), channel_id=1, source_target_pairs={{0,7},{1,6},{2,5},{3,4},{4,3},{5,2},{6,1},{7,0},{8,15},{9,14},{10,... | collective-permute-start | bytes 98312 | tf_op jit(solution)/shard_map/ppermute | solution.py:394
  32.9 3.9 %collective-permute-start.13 = (bf16[16,1024]{1,0:T(8,128)(2,1)S(1)}, bf16[16,1024]{1,0:T(8,128)(2,1)S(1)}, u32[]{:S(2)}, u32[]{:S(2)}) collective-permute-start(bf16[16,1024]{1,0:T(8,128)(2,1)S(1)} %add_convert_fusion.a), channel_id=1, source_target_pairs={{0,5},{1,4},{2,1},{3,0},{4,7},{5,6},{6,3},{7,2},{8,13},{9,12},{10,... | collective-permute-start | bytes 98312 | tf_op jit(solution)/shard_map/ppermute | solution.py:394

commit v8 on v7

--- a/solution.py
+++ b/solution.py
@@ -338,7 +338,7 @@
     return [first] + [part for _, part in sorted(zip(order, parts), key=lambda pair: pair[0])]
 
 
-def gather_kernel(order, a, b, c, d, weight, out, same_weight):
+def gather_kernel(order, a, b, c, d, weight, out):
     chip = lax.axis_index("tp") // 2
     own, *others = sort_chips(order, a, (b, c, d))
     out[chip] = own[...]
@@ -425,6 +425,7 @@
     devices = lax.axis_size("tp")
     chips = devices // 2
     rows = tokens * GROUP
+    sibling_weight = other_core(out_weight, devices)
     heads, limits, inputs = call(
         project_kernel,
         [((rows, 128), BF16), ((requests, 8, 128), jnp.int32), ((tokens, model_width), F32)],
@@ -445,14 +446,12 @@
     cuts = [(0, SPLIT[0]), (SPLIT[0], SPLIT[1] - SPLIT[0]), (SPLIT[1], experts - SPLIT[1])]
     gate_up = [[(gate_up_weight, *cut)] if cut[1] else [] for cut in cuts]
     keys, values, own_weight, ids, shares, *gate_up_a = fetch(caches + small + gate_up[0], [heads], "fetch_cache")
-    gathered, own_weight = call(
+    (gathered,) = call(
         functools.partial(gather_kernel, ORDER[0]),
-        [((chips, rows, 128), BF16), (own_weight.shape, BF16)],
+        [((chips, rows, 128), BF16)],
         [*to_chips([heads] * chips, devices, ORDER[0]), own_weight],
         "gather",
-        same={chips: 1},
-    )
-    sibling_weight = other_core(own_weight[0], devices)
+    )
     sibling = other_core(gathered, devices)
     (blocks_own,) = call(
         functools.partial(attend_own_kernel, steps),

time: 37.6 us -> 37.5 us (level)
  transfers between devices with their start and end apart: 16 -> 16, of which waited for: 8 -> 7; matrix products, arithmetic and copies ran while one was open for 0% -> 0% of each run, Pallas kernels for 22% -> 26%
where the time goes in v8:
time: 37.5 us; the launch traced here: 37.3 us
  starting transfers between devices  17.8 us (47%)
  Pallas kernels  12.9 us (34%)
  waiting for transfers between devices  6.46 us (17%)
    ppermute x12, starting transfers between devices, other_chip(): lax.ppermute(x, 'tp', [(i, 2 * to[i // 2] + 1 - i % 2) for i in range(dev...  16.9 us
    pallas_call x11, Pallas kernels, call(): pl.pallas_call(kernel, out_shape=[jax.ShapeDtypeStruct(s, d) if hbm_out e...  12.9 us
    ppermute x12, waiting for transfers between devices, other_chip(): lax.ppermute(x, 'tp', [(i, 2 * to[i // 2] + 1 - i % 2) for i in range(dev...  3.67 us
    ppermute x4, waiting for transfers between devices, other_core(): return lax.ppermute(x, 'tp', [(i, i ^ 1) for i in range(devices)])  2.79 us
    ppermute x4, starting transfers between devices, other_core(): return lax.ppermute(x, 'tp', [(i, i ^ 1) for i in range(devices)])  0.92 us
  transfers between devices with their start and end apart: 16, of which 7 were waited for; matrix products, arithmetic and copies ran while one was open for 0% of the time, Pallas kernels for 26%

profile of v8, /device:TPU:0, one launch (start us, length us, event | category | flops | bytes accessed | tf_op | source)
XLA Modules:
  0.0 37.3 jit_solution(8278994906794782594)
XLA Ops:
  0.0 0.5 %collective-permute-start.8 = (bf16[128,1024]{1,0:T(8,128)(2,1)}, bf16[128,1024]{1,0:T(8,128)(2,1)S(1)}, u32[]{:S(2)}, u32[]{:S(2)}) collective-permute-start(bf16[128,1024]{1,0:T(8,128)(2,1)} %param.15), channel_id=1, source_target_pairs={{0,1},{1,0},{2,3},{3,2},{4,5},{5,4},{6,7},{7,6},{8,9},{9,8},{10,11... | collective-permute-start | bytes 786440 | tf_op jit(solution)/shard_map/ppermute | solution.py:408
  0.5 1.5 %project.1 = (bf16[32,128]{1,0:T(8,128)(2,1)S(1)}, s32[4,8,128]{2,1,0:T(8,128)S(1)}, f32[16,1024]{1,0:T(8,128)S(1)}) custom-call(s32[4]{0:T(128)} %lengths_in.1, bf16[4,4,1024]{2,1,0:T(4,128)(2,1)} %hidden_in.1, bf16[256,1024]{1,0:T(8,128)(2,1)} %weight_in.1), custom_call_target="tpu_custom_call" | custom-call | bytes 8000000 | tf_op jit(solution)/shard_map/project/pallas_call | solution.py:41
  2.0 4.8 %collective-permute-start.2 = (bf16[32,128]{1,0:T(8,128)(2,1)S(1)}, bf16[32,128]{1,0:T(8,128)(2,1)S(1)}, u32[]{:S(2)}, u32[]{:S(2)}) collective-permute-start(bf16[32,128]{1,0:T(8,128)(2,1)S(1)} %get-tuple-element.25.refs_0_.a), channel_id=1, source_target_pairs={{0,7},{1,6},{2,5},{3,4},{4,3},{5,2},{6,1},{7,0},{8,15},{9,14},{10,... | collective-permute-start | bytes 24584 | tf_op jit(solution)/shard_map/ppermute | solution.py:394
  6.7 0.0 collective-permute-start.1
  6.7 1.7 %collective-permute-start = (bf16[32,128]{1,0:T(8,128)(2,1)S(1)}, bf16[32,128]{1,0:T(8,128)(2,1)S(1)}, u32[]{:S(2)}, u32[]{:S(2)}) collective-permute-start(bf16[32,128]{1,0:T(8,128)(2,1)S(1)} %get-tuple-element.25.refs_0_.a), channel_id=1, source_target_pairs={{0,3},{1,2},{2,7},{3,6},{4,1},{5,0},{6,5},{7,4},{8,11},{9,10},{10,... | collective-permute-start | bytes 24584 | tf_op jit(solution)/shard_map/ppermute | solution.py:394
  8.5 1.5 %fetch_cache.1 = (bf16[4,128,512]{2,1,0:T(8,128)(2,1)S(1)}, bf16[4,128,512]{2,1,0:T(8,128)(2,1)S(1)}, bf16[1,128,1024]{2,1,0:T(8,128)(2,1)S(1)}, s32[1,4,4,8]{3,2,1,0:T(4,128)S(1)}, s32[1,4,4,8]{3,2,1,0:T(4,128)S(1)}) custom-call(bf16[32,128]{1,0:T(8,128)(2,1)S(1)} %get-tuple-element.25.refs_0_.a, bf16[4,128,512]{2,1,0:T(8,128)(2,1)} %refs_1_.2, ...), custom_call_target="tpu_custom_call" | custom-call | bytes 1311232 | tf_op jit(solution)/shard_map/fetch_cache/pallas_call | solution.py:41
  9.9 0.0 collective-permute-done.2.d
  10.0 0.0 collective-permute-done.1.c
  10.0 0.7 %collective-permute-done.b = bf16[32,128]{1,0:T(8,128)(2,1)S(1)} collective-permute-done((bf16[32,128]{1,0:T(8,128)(2,1)S(1)}, bf16[32,128]{1,0:T(8,128)(2,1)S(1)}, u32[]{:S(2)}, u32[]{:S(2)}) %collective-permute-start) | collective-permute-done | bytes 8224 | tf_op jit(solution)/shard_map/ppermute | solution.py:394
  10.7 0.1 collective-permute-start.3
  10.8 0.4 %attend_own.1.blocks_own = f32[2,64,128]{2,1,0:T(8,128)S(1)} custom-call(s32[4,8,128]{2,1,0:T(8,128)S(1)} %get-tuple-element.24.limits, bf16[4,32,128]{2,1,0:T(8,128)(2,1)S(1)} %gather.1.own.refs_0_, bf16[4,128,512]{2,1,0:T(8,128)(2,1)S(1)} %get-tuple-element.27.keys, bf16[4,128,512]{2,1,0:T(8,128)(2,1)S(1)} %get-tuple-element.28.values), custom_call_target="tpu_custom_call" | custom-call | bytes 6000000 | tf_op jit(solution)/shard_map/attend_own/pallas_call | solution.py:41
  11.3 0.6 %collective-permute-done.3.sibling.refs_1_ = bf16[4,32,128]{2,1,0:T(8,128)(2,1)S(1)} collective-permute-done((bf16[4,32,128]{2,1,0:T(8,128)(2,1)S(1)}, bf16[4,32,128]{2,1,0:T(8,128)(2,1)S(1)}, u32[]{:S(2)}, u32[]{:S(2)}) %collective-permute-start.3) | collective-permute-done | bytes 32800 | tf_op jit(solution)/shard_map/ppermute | solution.py:408
  11.9 0.5 %attend.1 = (f32[64,128]{1,0:T(8,128)S(1)}, bf16[64,128]{1,0:T(8,128)(2,1)S(1)}, bf16[64,128]{1,0:T(8,128)(2,1)S(1)}, bf16[64,128]{1,0:T(8,128)(2,1)S(1)}) custom-call(s32[4,8,128]{2,1,0:T(8,128)S(1)} %get-tuple-element.24.limits, bf16[4,32,128]{2,1,0:T(8,128)(2,1)S(1)} %collective-permute-done.3.sibling.refs_1_, ...), custom_call_target="tpu_custom_call" | custom-call | bytes 6000000 | tf_op jit(solution)/shard_map/attend/pallas_call | solution.py:41
  12.4 1.7 %collective-permute-start.4 = (bf16[64,128]{1,0:T(8,128)(2,1)S(1)}, bf16[64,128]{1,0:T(8,128)(2,1)S(1)}, u32[]{:S(2)}, u32[]{:S(2)}) collective-permute-start(bf16[64,128]{1,0:T(8,128)(2,1)S(1)} %get-tuple-element.30), channel_id=1, source_target_pairs={{0,7},{1,6},{2,5},{3,4},{4,3},{5,2},{6,1},{7,0},{8,15},{9,14},{10,... | collective-permute-start | bytes 49160 | tf_op jit(solution)/shard_map/ppermute | solution.py:394
  14.1 0.4 %collective-permute-start.5 = (bf16[64,128]{1,0:T(8,128)(2,1)S(1)}, bf16[64,128]{1,0:T(8,128)(2,1)S(1)}, u32[]{:S(2)}, u32[]{:S(2)}) collective-permute-start(bf16[64,128]{1,0:T(8,128)(2,1)S(1)} %get-tuple-element.31), channel_id=1, source_target_pairs={{0,5},{1,4},{2,1},{3,0},{4,7},{5,6},{6,3},{7,2},{8,13},{9,12},{10,... | collective-permute-start | bytes 49160 | tf_op jit(solution)/shard_map/ppermute | solution.py:394
  14.5 1.3 %collective-permute-start.6 = (bf16[64,128]{1,0:T(8,128)(2,1)S(1)}, bf16[64,128]{1,0:T(8,128)(2,1)S(1)}, u32[]{:S(2)}, u32[]{:S(2)}) collective-permute-start(bf16[64,128]{1,0:T(8,128)(2,1)S(1)} %get-tuple-element.32), channel_id=1, source_target_pairs={{0,3},{1,2},{2,7},{3,6},{4,1},{5,0},{6,5},{7,4},{8,11},{9,10},{10,... | collective-permute-start | bytes 49160 | tf_op jit(solution)/shard_map/ppermute | solution.py:394
  15.8 2.9 %fetch_b.1 = (bf16[3,1024,1024]{2,1,0:T(8,128)(2,1)S(1)}, f32[64,128]{1,0:T(8,128)S(1)}) custom-call(bf16[4,32,128]{2,1,0:T(8,128)(2,1)S(1)} %gather.1.own.refs_0_, bf16[4,32,128]{2,1,0:T(8,128)(2,1)S(1)} %collective-permute-done.3.sibling.refs_1_, f32[64,128]{1,0:T(8,128)S(1)} %get-tuple-element.29.refs_2_.a, bf16[4,1024,1024]{2,1,0:T(8,128)(2,1)} %refs_1_.3), custom_call_target="tpu_custom_call" | custom-call | bytes 6291456 | tf_op jit(solution)/shard_map/fetch_b/pallas_call | solution.py:41
  18.8 0.0 collective-permute-done.4.b
  18.8 0.0 collective-permute-done.5.c
  18.8 0.0 collective-permute-done.6.d
  18.8 0.2 join.1.own
  19.0 0.2 collective-permute-start.7
  19.2 1.0 %collective-permute-done.7.sibling = f32[64,128]{1,0:T(8,128)S(1)} collective-permute-done((f32[64,128]{1,0:T(8,128)S(1)}, f32[64,128]{1,0:T(8,128)S(1)}, u32[]{:S(2)}, u32[]{:S(2)}) %collective-permute-start.7) | collective-permute-done | bytes 32800 | tf_op jit(solution)/shard_map/ppermute | solution.py:408
  20.2 0.0 collective-permute-done.8.sibling_weight
  20.2 0.3 output.1.refs_0_.a
  20.6 1.9 %collective-permute-start.11 = (bf16[16,1024]{1,0:T(8,128)(2,1)S(1)}, bf16[16,1024]{1,0:T(8,128)(2,1)S(1)}, u32[]{:S(2)}, u32[]{:S(2)}) collective-permute-start(bf16[16,1024]{1,0:T(8,128)(2,1)S(1)} %output.1.refs_0_.a), channel_id=1, source_target_pairs={{0,7},{1,6},{2,5},{3,4},{4,3},{5,2},{6,1},{7,0},{8,15},{9,14},{10,... | collective-permute-start | bytes 98312 | tf_op jit(solution)/shard_map/ppermute | solution.py:394
  22.5 0.0 collective-permute-start.10
  22.5 1.7 %collective-permute-start.9 = (bf16[16,1024]{1,0:T(8,128)(2,1)S(1)}, bf16[16,1024]{1,0:T(8,128)(2,1)S(1)}, u32[]{:S(2)}, u32[]{:S(2)}) collective-permute-start(bf16[16,1024]{1,0:T(8,128)(2,1)S(1)} %output.1.refs_0_.a), channel_id=1, source_target_pairs={{0,3},{1,2},{2,7},{3,6},{4,1},{5,0},{6,5},{7,4},{8,11},{9,10},{10,... | collective-permute-start | bytes 98312 | tf_op jit(solution)/shard_map/ppermute | solution.py:394
  24.2 2.8 %fetch_c.1 = (bf16[1,1024,1024]{2,1,0:T(8,128)(2,1)S(1)}, bf16[4,512,1024]{2,1,0:T(8,128)(2,1)S(1)}) custom-call(bf16[16,1024]{1,0:T(8,128)(2,1)S(1)} %output.1.refs_0_.a, bf16[4,1024,1024]{2,1,0:T(8,128)(2,1)} %refs_1_.3, bf16[4,512,1024]{2,1,0:T(8,128)(2,1)} %refs_2_.3), custom_call_target="tpu_custom_call" | custom-call | bytes 6291456 | tf_op jit(solution)/shard_map/fetch_c/pallas_call | solution.py:41
  27.1 0.0 collective-permute-done.11.d
  27.1 0.0 collective-permute-done.10.c
  27.1 0.3 collective-permute-done.9.b
  27.5 2.2 %experts.1 = (bf16[16,1024]{1,0:T(8,128)(2,1)S(1)}, f32[16,1024]{1,0:T(8,128)S(1)}) custom-call(f32[16,1024]{1,0:T(8,128)S(1)} %get-tuple-element.23.inputs, bf16[16,1024]{1,0:T(8,128)(2,1)S(1)} %output.1.refs_0_.a, bf16[16,1024]{1,0:T(8,128)(2,1)S(1)} %collective-permute-done.9.b, bf16[16,1024]{1,0:T(8,128)(2,1)S(1)} %collective-permute-done.10.c, ...), custom_call_target="tpu_custom_call" | custom-call | bytes 12000000 | tf_op jit(solution)/shard_map/experts/pallas_call | solution.py:41
  29.6 0.1 collective-permute-start.12
  29.7 1.1 %collective-permute-done.12 = bf16[16,1024]{1,0:T(8,128)(2,1)S(1)} collective-permute-done((bf16[16,1024]{1,0:T(8,128)(2,1)S(1)}, bf16[16,1024]{1,0:T(8,128)(2,1)S(1)}, u32[]{:S(2)}, u32[]{:S(2)}) %collective-permute-start.12) | collective-permute-done | bytes 32800 | tf_op jit(solution)/shard_map/ppermute | solution.py:408
  30.8 0.6 %collective-permute-start.15 = (bf16[16,1024]{1,0:T(8,128)(2,1)S(1)}, bf16[16,1024]{1,0:T(8,128)(2,1)S(1)}, u32[]{:S(2)}, u32[]{:S(2)}) collective-permute-start(bf16[16,1024]{1,0:T(8,128)(2,1)S(1)} %add_convert_fusion.a), channel_id=1, source_target_pairs={{0,3},{1,2},{2,7},{3,6},{4,1},{5,0},{6,5},{7,4},{8,11},{9,10},{10,... | collective-permute-start | bytes 98312 | tf_op jit(solution)/shard_map/ppermute | solution.py:394
  31.4 1.3 %collective-permute-start.14 = (bf16[16,1024]{1,0:T(8,128)(2,1)S(1)}, bf16[16,1024]{1,0:T(8,128)(2,1)S(1)}, u32[]{:S(2)}, u32[]{:S(2)}) collective-permute-start(bf16[16,1024]{1,0:T(8,128)(2,1)S(1)} %add_convert_fusion.a), channel_id=1, source_target_pairs={{0,7},{1,6},{2,5},{3,4},{4,3},{5,2},{6,1},{7,0},{8,15},{9,14},{10,... | collective-permute-start | bytes 98312 | tf_op jit(solution)/shard_map/ppermute | solution.py:394
  32.7 1.4 %collective-permute-start.13 = (bf16[16,1024]{1,0:T(8,128)(2,1)S(1)}, bf16[16,1024]{1,0:T(8,128)(2,1)S(1)}, u32[]{:S(2)}, u32[]{:S(2)}) collective-permute-start(bf16[16,1024]{1,0:T(8,128)(2,1)S(1)} %add_convert_fusion.a), channel_id=1, source_target_pairs={{0,5},{1,4},{2,1},{3,0},{4,7},{5,6},{6,3},{7,2},{8,13},{9,12},{10,... | collective-permute-start | bytes 98312 | tf_op jit(solution)/shard_map/ppermute | solution.py:394
  34.1 1.0 %collective-permute-done.15.d = bf16[16,1024]{1,0:T(8,128)(2,1)S(1)} collective-permute-done((bf16[16,1024]{1,0:T(8,128)(2,1)S(1)}, bf16[16,1024]{1,0:T(8,128)(2,1)S(1)}, u32[]{:S(2)}, u32[]{:S(2)}) %collective-permute-start.15) | collective-permute-done | bytes 32800 | tf_op jit(solution)/shard_map/ppermute | solution.py:394
  35.1 1.5 %collective-permute-done.14.c = bf16[16,1024]{1,0:T(8,128)(2,1)S(1)} collective-permute-done((bf16[16,1024]{1,0:T(8,128)(2,1)S(1)}, bf16[16,1024]{1,0:T(8,128)(2,1)S(1)}, u32[]{:S(2)}, u32[]{:S(2)}) %collective-permute-start.14) | collective-permute-done | bytes 32800 | tf_op jit(solution)/shard_map/ppermute | solution.py:394
  36.7 0.0 collective-permute-done.13.b
  36.7 0.6 %final.1 = bf16[4,4,1024]{2,1,0:T(4,128)(2,1)} custom-call(f32[16,1024]{1,0:T(8,128)S(1)} %get-tuple-element.39.residual, bf16[16,1024]{1,0:T(8,128)(2,1)S(1)} %add_convert_fusion.a, bf16[16,1024]{1,0:T(8,128)(2,1)S(1)} %collective-permute-done.13.b, bf16[16,1024]{1,0:T(8,128)(2,1)S(1)} %collective-permute-done.14.c, ...), custom_call_target="tpu_custom_call" | custom-call | tf_op jit(solution)/shard_map/final/pallas_call | solution.py:41
  (2 shorter events, 0.0 us)
Async XLA Ops:
  0.0 20.2 %collective-permute-start.8 = (bf16[128,1024]{1,0:T(8,128)(2,1)}, bf16[128,1024]{1,0:T(8,128)(2,1)S(1)}, u32[]{:S(2)}, u32[]{:S(2)}) collective-permute-start(bf16[128,1024]{1,0:T(8,128)(2,1)} %param.15), channel_id=1, source_target_pairs={{0,1},{1,0},{2,3},{3,2},{4,5},{5,4},{6,7},{7,6},{8,9},{9,8},{10,11... | collective-permute-start | bytes 786440 | tf_op jit(solution)/shard_map/ppermute | solution.py:408
  2.0 8.0 %collective-permute-start.2 = (bf16[32,128]{1,0:T(8,128)(2,1)S(1)}, bf16[32,128]{1,0:T(8,128)(2,1)S(1)}, u32[]{:S(2)}, u32[]{:S(2)}) collective-permute-start(bf16[32,128]{1,0:T(8,128)(2,1)S(1)} %get-tuple-element.25.refs_0_.a), channel_id=1, source_target_pairs={{0,7},{1,6},{2,5},{3,4},{4,3},{5,2},{6,1},{7,0},{8,15},{9,14},{10,... | collective-permute-start | bytes 24584 | tf_op jit(solution)/shard_map/ppermute | solution.py:394
  6.7 3.2 %collective-permute-start.1 = (bf16[32,128]{1,0:T(8,128)(2,1)S(1)}, bf16[32,128]{1,0:T(8,128)(2,1)S(1)}, u32[]{:S(2)}, u32[]{:S(2)}) collective-permute-start(bf16[32,128]{1,0:T(8,128)(2,1)S(1)} %get-tuple-element.25.refs_0_.a), channel_id=1, source_target_pairs={{0,5},{1,4},{2,1},{3,0},{4,7},{5,6},{6,3},{7,2},{8,13},{9,12},{10,... | collective-permute-start | bytes 24584 | tf_op jit(solution)/shard_map/ppermute | solution.py:394
  6.7 4.0 %collective-permute-start = (bf16[32,128]{1,0:T(8,128)(2,1)S(1)}, bf16[32,128]{1,0:T(8,128)(2,1)S(1)}, u32[]{:S(2)}, u32[]{:S(2)}) collective-permute-start(bf16[32,128]{1,0:T(8,128)(2,1)S(1)} %get-tuple-element.25.refs_0_.a), channel_id=1, source_target_pairs={{0,3},{1,2},{2,7},{3,6},{4,1},{5,0},{6,5},{7,4},{8,11},{9,10},{10,... | collective-permute-start | bytes 24584 | tf_op jit(solution)/shard_map/ppermute | solution.py:394
  10.7 1.2 %collective-permute-start.3 = (bf16[4,32,128]{2,1,0:T(8,128)(2,1)S(1)}, bf16[4,32,128]{2,1,0:T(8,128)(2,1)S(1)}, u32[]{:S(2)}, u32[]{:S(2)}) collective-permute-start(bf16[4,32,128]{2,1,0:T(8,128)(2,1)S(1)} %gather.1.own.refs_0_), channel_id=1, source_target_pairs={{0,1},{1,0},{2,3},{3,2},{4,5},{5,4},{6,7},{7,6},{8,9},{9,8},{10,11... | collective-permute-start | bytes 98312 | tf_op jit(solution)/shard_map/ppermute | solution.py:408
  12.4 6.4 %collective-permute-start.4 = (bf16[64,128]{1,0:T(8,128)(2,1)S(1)}, bf16[64,128]{1,0:T(8,128)(2,1)S(1)}, u32[]{:S(2)}, u32[]{:S(2)}) collective-permute-start(bf16[64,128]{1,0:T(8,128)(2,1)S(1)} %get-tuple-element.30), channel_id=1, source_target_pairs={{0,7},{1,6},{2,5},{3,4},{4,3},{5,2},{6,1},{7,0},{8,15},{9,14},{10,... | collective-permute-start | bytes 49160 | tf_op jit(solution)/shard_map/ppermute | solution.py:394
  14.1 4.7 %collective-permute-start.5 = (bf16[64,128]{1,0:T(8,128)(2,1)S(1)}, bf16[64,128]{1,0:T(8,128)(2,1)S(1)}, u32[]{:S(2)}, u32[]{:S(2)}) collective-permute-start(bf16[64,128]{1,0:T(8,128)(2,1)S(1)} %get-tuple-element.31), channel_id=1, source_target_pairs={{0,5},{1,4},{2,1},{3,0},{4,7},{5,6},{6,3},{7,2},{8,13},{9,12},{10,... | collective-permute-start | bytes 49160 | tf_op jit(solution)/shard_map/ppermute | solution.py:394
  14.5 4.2 %collective-permute-start.6 = (bf16[64,128]{1,0:T(8,128)(2,1)S(1)}, bf16[64,128]{1,0:T(8,128)(2,1)S(1)}, u32[]{:S(2)}, u32[]{:S(2)}) collective-permute-start(bf16[64,128]{1,0:T(8,128)(2,1)S(1)} %get-tuple-element.32), channel_id=1, source_target_pairs={{0,3},{1,2},{2,7},{3,6},{4,1},{5,0},{6,5},{7,4},{8,11},{9,10},{10,... | collective-permute-start | bytes 49160 | tf_op jit(solution)/shard_map/ppermute | solution.py:394
  19.0 1.3 %collective-permute-start.7 = (f32[64,128]{1,0:T(8,128)S(1)}, f32[64,128]{1,0:T(8,128)S(1)}, u32[]{:S(2)}, u32[]{:S(2)}) collective-permute-start(f32[64,128]{1,0:T(8,128)S(1)} %join.1.own), channel_id=1, source_target_pairs={{0,1},{1,0},{2,3},{3,2},{4,5},{5,4},{6,7},{7,6},{8,9},{9,8},{10,11... | collective-permute-start | bytes 98312 | tf_op jit(solution)/shard_map/ppermute | solution.py:408
  20.6 6.5 %collective-permute-start.11 = (bf16[16,1024]{1,0:T(8,128)(2,1)S(1)}, bf16[16,1024]{1,0:T(8,128)(2,1)S(1)}, u32[]{:S(2)}, u32[]{:S(2)}) collective-permute-start(bf16[16,1024]{1,0:T(8,128)(2,1)S(1)} %output.1.refs_0_.a), channel_id=1, source_target_pairs={{0,7},{1,6},{2,5},{3,4},{4,3},{5,2},{6,1},{7,0},{8,15},{9,14},{10,... | collective-permute-start | bytes 98312 | tf_op jit(solution)/shard_map/ppermute | solution.py:394
  22.5 4.6 %collective-permute-start.10 = (bf16[16,1024]{1,0:T(8,128)(2,1)S(1)}, bf16[16,1024]{1,0:T(8,128)(2,1)S(1)}, u32[]{:S(2)}, u32[]{:S(2)}) collective-permute-start(bf16[16,1024]{1,0:T(8,128)(2,1)S(1)} %output.1.refs_0_.a), channel_id=1, source_target_pairs={{0,5},{1,4},{2,1},{3,0},{4,7},{5,6},{6,3},{7,2},{8,13},{9,12},{10,... | collective-permute-start | bytes 98312 | tf_op jit(solution)/shard_map/ppermute | solution.py:394
  22.5 4.9 %collective-permute-start.9 = (bf16[16,1024]{1,0:T(8,128)(2,1)S(1)}, bf16[16,1024]{1,0:T(8,128)(2,1)S(1)}, u32[]{:S(2)}, u32[]{:S(2)}) collective-permute-start(bf16[16,1024]{1,0:T(8,128)(2,1)S(1)} %output.1.refs_0_.a), channel_id=1, source_target_pairs={{0,3},{1,2},{2,7},{3,6},{4,1},{5,0},{6,5},{7,4},{8,11},{9,10},{10,... | collective-permute-start | bytes 98312 | tf_op jit(solution)/shard_map/ppermute | solution.py:394
  29.6 1.2 %collective-permute-start.12 = (bf16[16,1024]{1,0:T(8,128)(2,1)S(1)}, bf16[16,1024]{1,0:T(8,128)(2,1)S(1)}, u32[]{:S(2)}, u32[]{:S(2)}) collective-permute-start(bf16[16,1024]{1,0:T(8,128)(2,1)S(1)} %get-tuple-element.40), channel_id=1, source_target_pairs={{0,1},{1,0},{2,3},{3,2},{4,5},{5,4},{6,7},{7,6},{8,9},{9,8},{10,11... | collective-permute-start | bytes 98312 | tf_op jit(solution)/shard_map/ppermute | solution.py:408
  30.8 4.3 %collective-permute-start.15 = (bf16[16,1024]{1,0:T(8,128)(2,1)S(1)}, bf16[16,1024]{1,0:T(8,128)(2,1)S(1)}, u32[]{:S(2)}, u32[]{:S(2)}) collective-permute-start(bf16[16,1024]{1,0:T(8,128)(2,1)S(1)} %add_convert_fusion.a), channel_id=1, source_target_pairs={{0,3},{1,2},{2,7},{3,6},{4,1},{5,0},{6,5},{7,4},{8,11},{9,10},{10,... | collective-permute-start | bytes 98312 | tf_op jit(solution)/shard_map/ppermute | solution.py:394
  31.4 5.3 %collective-permute-start.14 = (bf16[16,1024]{1,0:T(8,128)(2,1)S(1)}, bf16[16,1024]{1,0:T(8,128)(2,1)S(1)}, u32[]{:S(2)}, u32[]{:S(2)}) collective-permute-start(bf16[16,1024]{1,0:T(8,128)(2,1)S(1)} %add_convert_fusion.a), channel_id=1, source_target_pairs={{0,7},{1,6},{2,5},{3,4},{4,3},{5,2},{6,1},{7,0},{8,15},{9,14},{10,... | collective-permute-start | bytes 98312 | tf_op jit(solution)/shard_map/ppermute | solution.py:394
  32.7 4.0 %collective-permute-start.13 = (bf16[16,1024]{1,0:T(8,128)(2,1)S(1)}, bf16[16,1024]{1,0:T(8,128)(2,1)S(1)}, u32[]{:S(2)}, u32[]{:S(2)}) collective-permute-start(bf16[16,1024]{1,0:T(8,128)(2,1)S(1)} %add_convert_fusion.a), channel_id=1, source_target_pairs={{0,5},{1,4},{2,1},{3,0},{4,7},{5,6},{6,3},{7,2},{8,13},{9,12},{10,... | collective-permute-start | bytes 98312 | tf_op jit(solution)/shard_map/ppermute | solution.py:394
